TPU v7x, 32 devices: a whole 2x2x4 slice. The times are simulated.
32 devices in a mesh: clip: 4 (over x, core), win: 8 (over z, y).
Axes of the slice: x: 2, y: 2, z: 4, core: 2. Of those that a mesh axis runs over, the one named last changes fastest.
Arguments:
- tokens: bfloat16 [4, 8, 1, 5, 128, 1024], P('clip', 'win'), may hold values from -6 to 6
- grad_output: bfloat16 [4, 8, 1, 5, 128, 1024], P('clip', 'win'), may hold values from -16 to 16
- clip_height: int32 [4], P('clip'), may hold values from 9 to 16
- clip_width: int32 [4], P('clip'), may hold values from 33 to 64
- modulation: float32 [4, 12, 1024], P('clip'), may hold values from -3 to 3
- sp_qkv: float32 [1024, 3072], P('clip', 'win'), may hold values from -0.1875 to 0.1875
- sp_out: float32 [1024, 1024], P('clip', 'win'), may hold values from -0.75 to 0.75
- sp_up: float32 [1024, 4096], P('clip', 'win'), may hold values from -0.1875 to 0.1875
- sp_down: float32 [4096, 1024], P('clip', 'win'), may hold values from -0.09375 to 0.09375
- sp_table: float32 [16, 31, 31], replicated, may hold values from -3 to 3
- st_qkv: float32 [1024, 3072], P('clip', 'win'), may hold values from -0.1875 to 0.1875
- st_out: float32 [1024, 1024], P('clip', 'win'), may hold values from -0.75 to 0.75
- st_up: float32 [1024, 4096], P('clip', 'win'), may hold values from -0.1875 to 0.1875
- st_down: float32 [4096, 1024], P('clip', 'win'), may hold values from -0.09375 to 0.09375
- st_table: float32 [16, 9, 15, 15], replicated, may hold values from -3 to 3
Outputs:
- out_tokens: float32 [4, 8, 1, 5, 128, 1024], P('clip', 'win')
- grad_tokens: float32 [4, 8, 1, 5, 128, 1024], P('clip', 'win')
- grad_modulation: float32 [4, 12, 1024], P('clip')
- grad_sp_qkv: float32 [1024, 3072], P('clip', 'win')
- grad_sp_out: float32 [1024, 1024], P('clip', 'win')
- grad_sp_up: float32 [1024, 4096], P('clip', 'win')
- grad_sp_down: float32 [4096, 1024], P('clip', 'win')
- grad_sp_table: float32 [16, 31, 31], replicated
- grad_st_qkv: float32 [1024, 2048], P('clip', 'win')
- grad_st_value: float32 [1024, 1024], P('clip', 'win')
- grad_st_out: float32 [1024, 1024], P('clip', 'win')
- grad_st_up: float32 [1024, 4096], P('clip', 'win')
- grad_st_down: float32 [4096, 1024], P('clip', 'win')
- grad_st_table: float32 [16, 9, 15, 15], replicated
All inputs are finite; a program needn't handle non-finite values.
Results may differ from a plain program's by a relative error of at most 0.03.
Values may be sent and summed in bfloat16 or wider, within the bound.
No kernel may reach another device: no remote copies, remote signals or barrier semaphores. Data moves between devices by JAX's collectives and lax.ppermute only.
A program may use at most 448 MiB of HBM per device.

v0:
```python
from functools import partial

import jax
import jax.numpy as jnp
from jax import lax
from jax.sharding import PartitionSpec as P

HEADS = 16
WS = 16
FR = 5
LOC_W = 4
PAIR_LOCS = 1
HS = 8
SLOTS = 3


epsilon = 1e-06
masked_score = -1000000000.0
highest = lax.Precision.HIGHEST


def from_partner(value, axis, bit):
    mask = 2**bit
    pairs = [(source, source ^ mask) for source in range(lax.axis_size(axis))]
    return lax.ppermute(value, axis, pairs)


def modulated_norm(values, shift_vec, scale_vec):
    center = values - jnp.mean(values, axis=-1, keepdims=True)
    spread = jnp.mean(center * center, axis=-1, keepdims=True)
    return center * lax.rsqrt(spread + epsilon) * (1.0 + scale_vec) + shift_vec


def pair_table(extent):
    table_dims = (extent, extent, 2 * extent - 1)
    query_pos = lax.broadcasted_iota(jnp.int32, table_dims, 0)
    key_pos = lax.broadcasted_iota(jnp.int32, table_dims, 1)
    offset = lax.broadcasted_iota(jnp.int32, table_dims, 2)
    return (query_pos - key_pos + extent - 1 == offset).astype(jnp.float32)


def spatial_bias(bias_table):
    pair_onehot = pair_table(WS)
    full_bias = jnp.einsum(
        "hab,ija,klb->hjlik", bias_table, pair_onehot, pair_onehot, precision=highest
    )
    return full_bias.reshape(HEADS, WS * WS, WS * WS)


def spatial_bias_grad(grad_bias):
    pair_onehot = pair_table(WS)
    shaped = grad_bias.reshape(HEADS, WS, WS, WS, WS)
    return jnp.einsum("hjlik,ija,klb->hab", shaped, pair_onehot, pair_onehot, precision=highest)


def joint_bias(bias_table):
    frame_onehot = pair_table(FR)
    side_onehot = pair_table(HS)
    full_bias = jnp.einsum(
        "habc,ija,klb,mnc->hjlnikm",
        bias_table,
        frame_onehot,
        side_onehot,
        side_onehot,
        precision=highest,
    )
    return full_bias.reshape(HEADS, FR * HS * HS, FR * HS * HS)


def joint_bias_grad(grad_bias):
    frame_onehot = pair_table(FR)
    side_onehot = pair_table(HS)
    shaped = grad_bias.reshape(HEADS, FR, HS, HS, FR, HS, HS)
    return jnp.einsum(
        "hjlnikm,ija,klb,mnc->habc",
        shaped,
        frame_onehot,
        side_onehot,
        side_onehot,
        precision=highest,
    )


def window_allowed(valid_rows):
    win_len = valid_rows.shape[-1]
    return valid_rows[:, :, None] | jnp.eye(win_len, dtype=bool)[None]


def window_group(flat_rows):
    return flat_rows.reshape(SLOTS, WS * WS, flat_rows.shape[-1])


def window_ungroup(grouped):
    return grouped.reshape(SLOTS * WS * WS, grouped.shape[-1])


def joint_group(flat_rows):
    features = flat_rows.shape[-1]
    split_cols = flat_rows.reshape(PAIR_LOCS, FR, HS, 2, HS, features)
    return split_cols.transpose(0, 3, 1, 2, 4, 5).reshape(2 * PAIR_LOCS, FR * HS * HS, features)


def joint_ungroup(grouped):
    features = grouped.shape[-1]
    split_cols = grouped.reshape(PAIR_LOCS, 2, FR, HS, HS, features)
    return split_cols.transpose(0, 2, 3, 1, 4, 5).reshape(PAIR_LOCS * FR * HS * 2 * HS, features)


def split_halves(half_rows, own_half):
    pair_windows = half_rows.shape[0]
    filler = jnp.zeros((2 * SLOTS - pair_windows,) + half_rows.shape[1:], half_rows.dtype)
    padded = jnp.concatenate([half_rows, filler], axis=0)
    keep_part = lax.dynamic_slice_in_dim(padded, own_half * SLOTS, SLOTS, 0)
    send_part = lax.dynamic_slice_in_dim(padded, (1 - own_half) * SLOTS, SLOTS, 0)
    return (keep_part, send_part)


def join_windows(keep_part, came_part, own_half):
    upper_half = jnp.where(own_half == 0, keep_part, came_part)
    lower_half = jnp.where(own_half == 0, came_part, keep_part)
    return jnp.concatenate([upper_half, lower_half], axis=1)


def split_windows(grouped, own_half):
    half_len = grouped.shape[1] // 2
    upper_half = grouped[:, :half_len]
    lower_half = grouped[:, half_len:]
    keep_part = jnp.where(own_half == 0, upper_half, lower_half)
    send_part = jnp.where(own_half == 0, lower_half, upper_half)
    return (keep_part, send_part)


def join_halves(keep_part, came_part, own_half, pair_windows):
    leading = jnp.where(own_half == 0, keep_part, came_part)
    trailing = jnp.where(own_half == 0, came_part, keep_part)
    return jnp.concatenate([leading, trailing], axis=0)[:pair_windows]


def leave_windows(win_rows, own_half, pair_windows):
    keep_part, send_part = split_windows(window_group(win_rows), own_half)
    came_part = from_partner(send_part.astype(jnp.bfloat16), "win", 0).astype(send_part.dtype)
    return join_halves(keep_part, came_part, own_half, pair_windows).reshape(-1, win_rows.shape[-1])


def enter_windows(flat_grad, own_half, pair_windows):
    half_rows = flat_grad.reshape(pair_windows, -1, flat_grad.shape[-1])
    keep_part, send_part = split_halves(half_rows, own_half)
    came_part = from_partner(send_part.astype(jnp.bfloat16), "win", 0).astype(send_part.dtype)
    return window_ungroup(join_windows(keep_part, came_part, own_half))


def leave_grads(win_rows, own_half, pair_windows):
    keep_part, send_part = split_windows(window_group(win_rows), own_half)
    came_part = from_partner(send_part.astype(jnp.bfloat16), "win", 0).astype(send_part.dtype)
    return join_halves(keep_part, came_part, own_half, pair_windows)


def window_scores(qkv_rows, score_bias, allowed):
    win_count, win_len, triple = qkv_rows.shape
    head_dim = triple // (3 * HEADS)
    split_heads = qkv_rows.reshape(win_count, win_len, 3, HEADS, head_dim)
    queries = split_heads[:, :, 0]
    key_rows = split_heads[:, :, 1]
    value_rows = split_heads[:, :, 2]
    scores = (
        jnp.einsum("wkhe,wqhe->whkq", key_rows, queries, preferred_element_type=jnp.float32)
        * head_dim ** (-0.5)
        + score_bias[None]
    )
    scores = jnp.where(allowed[:, None], scores, masked_score)
    return (scores, queries, key_rows, value_rows)


def attend(qkv_rows, score_bias, allowed):
    win_count, win_len, triple = qkv_rows.shape
    scores, queries, key_rows, value_rows = window_scores(qkv_rows, score_bias, allowed)
    col_max = jnp.max(scores, axis=-2, keepdims=True)
    exp_scores = jnp.exp(scores - col_max)
    col_sum = jnp.sum(exp_scores, axis=-2, keepdims=True)
    attn_probs = (exp_scores / col_sum).astype(jnp.bfloat16)
    attn_mixed = jnp.einsum(
        "whkq,wkhe->wqhe", attn_probs, value_rows, preferred_element_type=jnp.float32
    )
    return (
        attn_mixed.reshape(win_count, win_len, triple // 3).astype(jnp.bfloat16),
        col_max + jnp.log(col_sum),
    )


def attend_back(qkv_rows, score_bias, allowed, log_sum, grad_mixed):
    scores, queries, key_rows, value_rows = window_scores(qkv_rows, score_bias, allowed)
    attn_probs = jnp.exp(scores - log_sum)
    win_count, win_len, model_width = grad_mixed.shape
    head_dim = model_width // HEADS
    grad_heads = grad_mixed.reshape(win_count, win_len, HEADS, head_dim)
    grad_values = jnp.einsum(
        "whkq,wqhe->wkhe",
        attn_probs.astype(jnp.bfloat16),
        grad_heads,
        preferred_element_type=jnp.float32,
    )
    grad_probs = jnp.einsum(
        "wkhe,wqhe->whkq", value_rows, grad_heads, preferred_element_type=jnp.float32
    )
    col_inner = jnp.sum(grad_probs * attn_probs, axis=-2, keepdims=True)
    grad_scores = (attn_probs * (grad_probs - col_inner)).astype(jnp.bfloat16)
    scale_factor = head_dim ** (-0.5)
    grad_queries = (
        jnp.einsum("whkq,wkhe->wqhe", grad_scores, key_rows, preferred_element_type=jnp.float32)
        * scale_factor
    )
    grad_keys = (
        jnp.einsum("whkq,wqhe->wkhe", grad_scores, queries, preferred_element_type=jnp.float32)
        * scale_factor
    )
    grad_qkv = (
        jnp.stack([grad_queries, grad_keys, grad_values], axis=2)
        .reshape(win_count, win_len, 3 * model_width)
        .astype(jnp.bfloat16)
    )
    grad_bias = jnp.sum(grad_scores, axis=0, dtype=jnp.float32)
    return (grad_qkv, grad_bias)


def attention_forward(
    residual, params, qkv_weight, out_weight, score_bias, allowed, group, ungroup
):
    attn_in = modulated_norm(residual, params[0], params[1]).astype(jnp.bfloat16)
    qkv_rows = jnp.dot(attn_in, qkv_weight, preferred_element_type=jnp.float32).astype(jnp.bfloat16)
    grouped = group(qkv_rows)
    attn_out, log_sum = attend(grouped, score_bias, allowed)
    flat_out = ungroup(attn_out)
    mixed_rows = jnp.dot(flat_out, out_weight, preferred_element_type=jnp.float32)
    return (residual + params[2] * mixed_rows, (attn_in, grouped, flat_out, log_sum, mixed_rows))


def attention_backward(
    grad_rows,
    residual,
    params,
    qkv_weight,
    out_weight,
    score_bias,
    allowed,
    group,
    ungroup,
    saved_rows,
):
    attn_in, grouped, flat_out, log_sum, mixed_rows = saved_rows
    grad_gate = jnp.sum(grad_rows * mixed_rows, axis=0)
    grad_mixed = (params[2] * grad_rows).astype(jnp.bfloat16)
    grad_out_weight = jnp.einsum(
        "rd,re->de", flat_out, grad_mixed, preferred_element_type=jnp.float32
    )
    grad_flat = jnp.einsum(
        "re,de->rd", grad_mixed, out_weight, preferred_element_type=jnp.float32
    ).astype(jnp.bfloat16)
    grad_grouped, grad_bias = attend_back(grouped, score_bias, allowed, log_sum, group(grad_flat))
    grad_qkv = ungroup(grad_grouped)
    grad_qkv_weight = jnp.einsum("rd,re->de", attn_in, grad_qkv, preferred_element_type=jnp.float32)
    grad_in = jnp.einsum("re,de->rd", grad_qkv, qkv_weight, preferred_element_type=jnp.float32)
    unused, norm_pull = jax.vjp(modulated_norm, residual, params[0], params[1])
    grad_resid, grad_shift, grad_scale = norm_pull(grad_in)
    return (
        grad_rows + grad_resid,
        (grad_shift, grad_scale, grad_gate),
        grad_qkv_weight,
        grad_out_weight,
        grad_bias,
    )


def mlp_forward(residual, params, up_weight, down_weight):
    mlp_in = modulated_norm(residual, params[0], params[1]).astype(jnp.bfloat16)
    upward = jnp.dot(mlp_in, up_weight, preferred_element_type=jnp.float32)
    hidden = jax.nn.gelu(upward, approximate=False).astype(jnp.bfloat16)
    downward = jnp.dot(hidden, down_weight, preferred_element_type=jnp.float32)
    return (residual + params[2] * downward, (mlp_in, upward, hidden, downward))


def mlp_backward(grad_rows, residual, params, up_weight, down_weight, saved_rows):
    mlp_in, upward, hidden, downward = saved_rows
    grad_gate = jnp.sum(grad_rows * downward, axis=0)
    grad_down = (params[2] * grad_rows).astype(jnp.bfloat16)
    grad_down_weight = jnp.einsum(
        "rf,rd->fd", hidden, grad_down, preferred_element_type=jnp.float32
    )
    grad_hidden = jnp.einsum(
        "rd,fd->rf", grad_down, down_weight, preferred_element_type=jnp.float32
    )
    unused, gelu_pull = jax.vjp(partial(jax.nn.gelu, approximate=False), upward)
    grad_up = gelu_pull(grad_hidden)[0].astype(jnp.bfloat16)
    grad_up_weight = jnp.einsum("rd,rf->df", mlp_in, grad_up, preferred_element_type=jnp.float32)
    grad_in = jnp.einsum("rf,df->rd", grad_up, up_weight, preferred_element_type=jnp.float32)
    unused_norm, norm_pull = jax.vjp(modulated_norm, residual, params[0], params[1])
    grad_resid, grad_shift, grad_scale = norm_pull(grad_in)
    return (
        grad_rows + grad_resid,
        (grad_shift, grad_scale, grad_gate),
        grad_up_weight,
        grad_down_weight,
    )


def body(
    tokens,
    grad_output,
    clip_height,
    clip_width,
    modulation,
    sp_qkv,
    sp_out,
    sp_up,
    sp_down,
    sp_table,
    st_qkv,
    st_out,
    st_up,
    st_down,
    st_table,
):
    model_width = tokens.shape[-1]
    half_len = tokens.shape[-2]
    pair_windows = PAIR_LOCS * FR
    shard_index = lax.axis_index("win")
    pair_index = shard_index // 2
    own_half = shard_index % 2
    low_masters = (
        sp_qkv.astype(jnp.bfloat16),
        sp_out.astype(jnp.bfloat16),
        sp_up.astype(jnp.bfloat16),
        sp_down.astype(jnp.bfloat16),
        st_qkv.astype(jnp.bfloat16),
        st_out.astype(jnp.bfloat16),
        st_up.astype(jnp.bfloat16),
        st_down.astype(jnp.bfloat16),
    )
    clip_gathered = (
        lax.all_gather(low_masters[0], "clip", axis=0, tiled=True),
        lax.all_gather(low_masters[1], "clip", axis=0, tiled=True),
        lax.all_gather(low_masters[2], "clip", axis=0, tiled=True),
        lax.all_gather(low_masters[3], "clip", axis=0, tiled=True),
        lax.all_gather(low_masters[4], "clip", axis=0, tiled=True),
        lax.all_gather(low_masters[5], "clip", axis=0, tiled=True),
        lax.all_gather(low_masters[6], "clip", axis=0, tiled=True),
        lax.all_gather(low_masters[7], "clip", axis=0, tiled=True),
    )
    full_weights = (
        lax.all_gather(clip_gathered[0], "win", axis=1, tiled=True),
        lax.all_gather(clip_gathered[1], "win", axis=1, tiled=True),
        lax.all_gather(clip_gathered[2], "win", axis=1, tiled=True),
        lax.all_gather(clip_gathered[3], "win", axis=1, tiled=True),
        lax.all_gather(clip_gathered[4], "win", axis=1, tiled=True),
        lax.all_gather(clip_gathered[5], "win", axis=1, tiled=True),
        lax.all_gather(clip_gathered[6], "win", axis=1, tiled=True),
        lax.all_gather(clip_gathered[7], "win", axis=1, tiled=True),
    )
    mod_rows = modulation[0]
    sp_bias = spatial_bias(sp_table)
    st_bias = joint_bias(st_table)
    slot_ids = own_half * SLOTS + jnp.arange(SLOTS, dtype=jnp.int32)
    window_ids = jnp.minimum(slot_ids, pair_windows - 1)
    location = pair_index * PAIR_LOCS + window_ids // FR
    token_ids = jnp.arange(WS * WS, dtype=jnp.int32)
    row_pos = (location // LOC_W * WS)[:, None] + (token_ids // WS)[None, :]
    col_pos = (location % LOC_W * WS)[:, None] + (token_ids % WS)[None, :]
    sp_allowed = window_allowed((row_pos < clip_height[0]) & (col_pos < clip_width[0]))
    joint_loc = pair_index * PAIR_LOCS + jnp.arange(PAIR_LOCS, dtype=jnp.int32)
    joint_ids = jnp.arange(FR * HS * HS, dtype=jnp.int32)
    half_cols = jnp.arange(2, dtype=jnp.int32)
    joint_row = (joint_loc // LOC_W * WS + own_half * HS)[:, None, None] + (joint_ids // HS % HS)[
        None, None, :
    ]
    joint_col = (
        (joint_loc % LOC_W * WS)[:, None, None]
        + (half_cols * HS)[None, :, None]
        + (joint_ids % HS)[None, None, :]
    )
    joint_valid = (joint_row < clip_height[0]) & (joint_col < clip_width[0])
    st_allowed = window_allowed(joint_valid.reshape(2 * PAIR_LOCS, FR * HS * HS))
    half_tokens = tokens.reshape(pair_windows, half_len, model_width)
    keep_part, send_part = split_halves(half_tokens, own_half)
    came_part = from_partner(send_part, "win", 0)
    win_input = window_ungroup(join_windows(keep_part, came_part, own_half)).astype(jnp.float32)
    win_middle, attn_saved_a = attention_forward(
        win_input,
        mod_rows[0:3],
        full_weights[0],
        full_weights[1],
        sp_bias,
        sp_allowed,
        window_group,
        window_ungroup,
    )
    flat_middle = leave_windows(win_middle, own_half, pair_windows)
    first_out, mlp_saved_a = mlp_forward(
        flat_middle, mod_rows[3:6], full_weights[2], full_weights[3]
    )
    second_mid, attn_saved_b = attention_forward(
        first_out,
        mod_rows[6:9],
        full_weights[4],
        full_weights[5],
        st_bias,
        st_allowed,
        joint_group,
        joint_ungroup,
    )
    final_rows, mlp_saved_b = mlp_forward(
        second_mid, mod_rows[9:12], full_weights[6], full_weights[7]
    )
    out_tokens = final_rows.reshape(tokens.shape)
    grad_final = grad_output.reshape(-1, model_width).astype(jnp.float32)
    grad_second_mid, mlp_grads_b, grad_up_b, grad_down_b = mlp_backward(
        grad_final, second_mid, mod_rows[9:12], full_weights[6], full_weights[7], mlp_saved_b
    )
    grad_first_out, attn_grads_b, grad_qkv_b, grad_out_b, grad_bias_b = attention_backward(
        grad_second_mid,
        first_out,
        mod_rows[6:9],
        full_weights[4],
        full_weights[5],
        st_bias,
        st_allowed,
        joint_group,
        joint_ungroup,
        attn_saved_b,
    )
    grad_flat_middle, mlp_grads_a, grad_up_a, grad_down_a = mlp_backward(
        grad_first_out, flat_middle, mod_rows[3:6], full_weights[2], full_weights[3], mlp_saved_a
    )
    grad_win_middle = enter_windows(grad_flat_middle, own_half, pair_windows)
    grad_win_input, attn_grads_a, grad_qkv_a, grad_out_a, grad_bias_a = attention_backward(
        grad_win_middle,
        win_input,
        mod_rows[0:3],
        full_weights[0],
        full_weights[1],
        sp_bias,
        sp_allowed,
        window_group,
        window_ungroup,
        attn_saved_a,
    )
    grad_tokens = leave_grads(grad_win_input, own_half, pair_windows).reshape(tokens.shape)
    grad_qk_b = grad_qkv_b[:, : 2 * model_width]
    grad_value_b = grad_qkv_b[:, 2 * model_width :]
    local_grads = (
        grad_qkv_a,
        grad_out_a,
        grad_up_a,
        grad_down_a,
        grad_qk_b,
        grad_value_b,
        grad_out_b,
        grad_up_b,
        grad_down_b,
    )
    spread = (
        lax.psum_scatter(
            local_grads[0].astype(jnp.bfloat16), "win", scatter_dimension=1, tiled=True
        ).astype(jnp.float32),
        lax.psum_scatter(
            local_grads[1].astype(jnp.bfloat16), "win", scatter_dimension=1, tiled=True
        ).astype(jnp.float32),
        lax.psum_scatter(
            local_grads[2].astype(jnp.bfloat16), "win", scatter_dimension=1, tiled=True
        ).astype(jnp.float32),
        lax.psum_scatter(
            local_grads[3].astype(jnp.bfloat16), "win", scatter_dimension=1, tiled=True
        ).astype(jnp.float32),
        lax.psum_scatter(
            local_grads[4].astype(jnp.bfloat16), "win", scatter_dimension=1, tiled=True
        ).astype(jnp.float32),
        lax.psum_scatter(
            local_grads[5].astype(jnp.bfloat16), "win", scatter_dimension=1, tiled=True
        ).astype(jnp.float32),
        lax.psum_scatter(
            local_grads[6].astype(jnp.bfloat16), "win", scatter_dimension=1, tiled=True
        ).astype(jnp.float32),
        lax.psum_scatter(
            local_grads[7].astype(jnp.bfloat16), "win", scatter_dimension=1, tiled=True
        ).astype(jnp.float32),
        lax.psum_scatter(
            local_grads[8].astype(jnp.bfloat16), "win", scatter_dimension=1, tiled=True
        ).astype(jnp.float32),
    )
    weight_grads = (
        lax.psum_scatter(
            spread[0].astype(jnp.bfloat16), "clip", scatter_dimension=0, tiled=True
        ).astype(jnp.float32),
        lax.psum_scatter(
            spread[1].astype(jnp.bfloat16), "clip", scatter_dimension=0, tiled=True
        ).astype(jnp.float32),
        lax.psum_scatter(
            spread[2].astype(jnp.bfloat16), "clip", scatter_dimension=0, tiled=True
        ).astype(jnp.float32),
        lax.psum_scatter(
            spread[3].astype(jnp.bfloat16), "clip", scatter_dimension=0, tiled=True
        ).astype(jnp.float32),
        lax.psum_scatter(
            spread[4].astype(jnp.bfloat16), "clip", scatter_dimension=0, tiled=True
        ).astype(jnp.float32),
        lax.psum_scatter(
            spread[5].astype(jnp.bfloat16), "clip", scatter_dimension=0, tiled=True
        ).astype(jnp.float32),
        lax.psum_scatter(
            spread[6].astype(jnp.bfloat16), "clip", scatter_dimension=0, tiled=True
        ).astype(jnp.float32),
        lax.psum_scatter(
            spread[7].astype(jnp.bfloat16), "clip", scatter_dimension=0, tiled=True
        ).astype(jnp.float32),
        lax.psum_scatter(
            spread[8].astype(jnp.bfloat16), "clip", scatter_dimension=0, tiled=True
        ).astype(jnp.float32),
    )
    mod_grads = jnp.stack(
        [
            attn_grads_a[0],
            attn_grads_a[1],
            attn_grads_a[2],
            mlp_grads_a[0],
            mlp_grads_a[1],
            mlp_grads_a[2],
            attn_grads_b[0],
            attn_grads_b[1],
            attn_grads_b[2],
            mlp_grads_b[0],
            mlp_grads_b[1],
            mlp_grads_b[2],
        ],
        axis=0,
    )
    grad_modulation = lax.psum(mod_grads.astype(jnp.bfloat16), "win").astype(jnp.float32)[None]
    table_grads = lax.psum(
        (spatial_bias_grad(grad_bias_a), joint_bias_grad(grad_bias_b)), ("clip", "win")
    )
    return (
        out_tokens,
        grad_tokens,
        grad_modulation,
        weight_grads[0],
        weight_grads[1],
        weight_grads[2],
        weight_grads[3],
        table_grads[0],
        weight_grads[4],
        weight_grads[5],
        weight_grads[6],
        weight_grads[7],
        weight_grads[8],
        table_grads[1],
    )


def solution(mesh):
    in_specs = (
        P("clip", "win", None, None, None, None),
        P("clip", "win", None, None, None, None),
        P("clip"),
        P("clip"),
        P("clip", None, None),
        P("clip", "win"),
        P("clip", "win"),
        P("clip", "win"),
        P("clip", "win"),
        P(),
        P("clip", "win"),
        P("clip", "win"),
        P("clip", "win"),
        P("clip", "win"),
        P(),
    )
    out_specs = (
        P("clip", "win", None, None, None, None),
        P("clip", "win", None, None, None, None),
        P("clip", None, None),
        P("clip", "win"),
        P("clip", "win"),
        P("clip", "win"),
        P("clip", "win"),
        P(),
        P("clip", "win"),
        P("clip", "win"),
        P("clip", "win"),
        P("clip", "win"),
        P("clip", "win"),
        P(),
    )
    return jax.shard_map(body, mesh=mesh, in_specs=in_specs, out_specs=out_specs, check_vma=False)
```

profile of v0, /device:TPU:0, one launch (start us, length us, event | category | flops | bytes accessed | tf_op | source)
XLA Modules:
  0.0 2475.5 jit_solution(12781133707191049629)
XLA Ops:
  88.3 35.3 %copy.100 = f32[16,16,16,16,16]{4,3,2,1,0:T(8,128)} copy(f32[16,16,16,16,16]{2,0,4,1,3:T(8,128)} %convolution_bitcast_fusion) | data formatting | bytes 8388608 | tf_op jit(solution)/shard_map/hab,ija,klb->hjlik/transpose | solution.py:44
  168.1 49.1 %fusion.4 = f32[16,5,8,8,5,8,8]{0,1,4,3,6,2,5:T(8,128)} fusion(f32[8,8,16,9,8,8,1]{2,4,5,3,1,0,6:T(8,128)} %convolution_bitcast_fusion.1), kind=kOutput, calls=%fused_computation.4 | convolution fusion | flops 176947872 | bytes 8912896 | tf_op jit(solution)/shard_map/habc,ija,klb,mnc->hjlnikm/dot_general | solution.py:59
  289.0 46.5 %copy.111 = f32[16,5,8,8,5,8,8]{0,6,5,4,3,2,1:T(8,128)} copy(f32[16,5,8,8,5,8,8]{0,1,4,3,6,2,5:T(8,128)} %fusion.4) | data formatting | bytes 13107200 | tf_op jit(solution)/shard_map/habc,ija,klb,mnc->hjlnikm/transpose | solution.py:59
  335.5 30.5 %copy.112 = f32[16,320,320]{2,1,0:T(8,128)} copy(f32[16,320,320]{0,2,1:T(8,128)} %bitcast.355) | data formatting | bytes 13107200 | tf_op jit(solution)/shard_map/add | solution.py:166
  379.6 31.8 %multiply_convert_fusion.3 = (bf16[640,4096]{1,0:T(8,128)(2,1)}, f32[640,4096]{1,0:T(8,128)}, f32[640,4096]{1,0:T(8,128)}) fusion(bf16[640,1024]{1,0:T(8,128)(2,1)} %add_convert_fusion.4, bf16[1024,4096]{1,0:T(8,128)(2,1)} %all-gather.19.cloned.1.call-done), kind=kOutput, calls=%fused_computation.45 | convolution fusion | flops 5539102720 | bytes 35913728 | tf_op jit(solution)/shard_map/dot_general | solution.py:275
  411.4 92.9 %all-gather.23.cloned.1.call-done = bf16[4096,1024]{1,0:T(8,128)(2,1)} async-done(((bf16[4096,128]{1,0:T(8,128)(2,1)}), bf16[4096,1024]{1,0:T(8,128)(2,1)}) %all-gather.23.cloned.1.call-update) | async-done | bytes 8388624 | tf_op jit(solution)/shard_map/all_gather | solution.py:352
  517.1 87.4 %all-gather.25.cloned.1.call-done = bf16[1024,3072]{1,0:T(8,128)(2,1)} async-done(((bf16[1024,384]{1,0:T(8,128)(2,1)}), bf16[1024,3072]{1,0:T(8,128)(2,1)}) %all-gather.25.cloned.1.call-update) | async-done | bytes 6291472 | tf_op jit(solution)/shard_map/all_gather | solution.py:353
  689.7 91.7 %all-gather.31.cloned.1.call-done = bf16[1024,4096]{1,0:T(8,128)(2,1)} async-done(((bf16[1024,512]{1,0:T(8,128)(2,1)}), bf16[1024,4096]{1,0:T(8,128)(2,1)}) %all-gather.31.cloned.1.call-update) | async-done | bytes 8388624 | tf_op jit(solution)/shard_map/all_gather | solution.py:355
  792.8 114.1 %all-gather.35.cloned.1.call-done = bf16[4096,1024]{1,0:T(8,128)(2,1)} async-done(((bf16[4096,128]{1,0:T(8,128)(2,1)}), bf16[4096,1024]{1,0:T(8,128)(2,1)}) %all-gather.35.cloned.1.call-update) | async-done | bytes 8388624 | tf_op jit(solution)/shard_map/all_gather | solution.py:356
  906.9 33.1 %add_convert_fusion.1 = (bf16[640,4096]{1,0:T(8,128)(2,1)S(1)}, f32[640,4096]{1,0:T(8,128)}) fusion(f32[640,4096]{1,0:T(8,128)} %fusion.156, bf16[640,1024]{1,0:T(8,128)(2,1)} %fusion.54, bf16[4096,1024]{1,0:T(8,128)(2,1)} %all-gather.35.cloned.1.call-done), kind=kOutput, calls=%fused_computation.31 | convolution fusion | flops 5557452800 | bytes 35913728 | tf_op jit(solution)/shard_map/rd,fd->rf/dot_general | solution.py:288
  1274.0 26.2 %copy.125 = f32[16,320,320]{0,2,1:T(8,128)} copy(f32[16,320,320]{2,1,0:T(8,128)} %get-tuple-element.82) | data formatting | bytes 13107200 | tf_op jit(solution)/shard_map/reduce_sum | solution.py:221
  1300.2 99.7 %fusion.10 = f32[9,16,8,8,8,8]{1,0,5,4,3,2:T(8,128)} fusion(f32[16,5,8,8,5,8,8]{0,6,5,4,3,2,1:T(8,128)} %bitcast.354, pred[5,5,9,1,1,1,1]{2,1,0,6,5,4,3:T(8,128)(4,1)S(1)} %fusion.222), kind=kOutput, calls=%fused_computation.18 | convolution fusion | flops 176947200 | bytes 8913121 | tf_op jit(solution)/shard_map/hjlnikm,ija,klb,mnc->habc/dot_general | solution.py:74
  1399.9 29.0 %fusion.57 = f32[9,16,8,8,15]{1,4,3,2,0:T(8,128)} fusion(f32[9,16,8,8,8,8]{1,0,5,4,3,2:T(8,128)} %fusion.10), kind=kOutput, calls=%fused_computation.146 | convolution fusion | flops 106171200 | bytes 2912256 | tf_op jit(solution)/shard_map/hjlnikm,ija,klb,mnc->habc/dot_general | solution.py:74
  1495.7 150.1 %reduce-scatter.35.cloned.1.call-done = bf16[1024,512]{1,0:T(8,128)(2,1)} async-done(((bf16[1024,4096]{1,0:T(8,128)(2,1)}), bf16[1024,512]{1,0:T(8,128)(2,1)}) %reduce-scatter.35.cloned.1.call-update) | async-done | bytes 1048592 | tf_op jit(solution)/shard_map/reduce_scatter | solution.py:466
  1645.9 151.6 %reduce-scatter.59.cloned.1.call-done = bf16[128,4096]{1,0:T(8,128)(2,1)} async-done(((bf16[1024,4096]{1,0:T(8,128)(2,1)}), bf16[128,4096]{1,0:T(8,128)(2,1)}) %reduce-scatter.59.cloned.1.call-update) | async-done | bytes 1048592
  1800.6 133.7 %all-reduce.4.cloned.1.call-done = f32[16,9,15,15]{3,2,0,1:T(8,128)} async-done(((f32[16,9,15,15]{3,2,0,1:T(8,128)}), f32[16,9,15,15]{3,2,0,1:T(8,128)}) %all-reduce.4.cloned.1.call-update) | async-done | bytes 129616 | tf_op jit(solution)/shard_map/psum | solution.py:535
  1936.8 149.5 %reduce-scatter.49.cloned.1.call-done = bf16[1024,512]{1,0:T(8,128)(2,1)} async-done(((bf16[1024,4096]{1,0:T(8,128)(2,1)}), bf16[1024,512]{1,0:T(8,128)(2,1)}) %reduce-scatter.49.cloned.1.call-update) | async-done | bytes 1048592 | tf_op jit(solution)/shard_map/reduce_scatter | solution.py:481
  2123.9 41.7 %copy.124 = f32[16,16,16,16,16]{1,2,3,4,0:T(8,128)} copy(f32[16,16,16,16,16]{4,3,2,1,0:T(8,128)} %reshape.759) | data formatting | bytes 8388608 | tf_op jit(solution)/shard_map/reshape | solution.py:52
  2165.6 72.8 %reduce-scatter.65.cloned.1.call-done = bf16[128,4096]{1,0:T(8,128)(2,1)} async-done(((bf16[1024,4096]{1,0:T(8,128)(2,1)}), bf16[128,4096]{1,0:T(8,128)(2,1)}) %reduce-scatter.65.cloned.1.call-update) | async-done | bytes 1048592
  2266.0 35.8 %psum.21 = bf16[1,12,1024]{2,0,1:T(2,128)(2,1)S(1)} all-reduce(bf16[1,12,1024]{2,0,1:T(2,128)(2,1)S(1)} %broadcast_in_dim.65), channel_id=1, replica_groups=mesh['clip'=4,'win'=8] {'win'}, use_global_device_ids=true, to_apply=%region_34.35 | all-reduce | flops 12288 | bytes 49152 | tf_op jit(solution)/shard_map/psum | solution.py:534
  2305.9 40.6 %psum.22 = f32[16,31,31]{2,1,0:T(8,128)} all-reduce(f32[16,31,31]{2,1,0:T(8,128)S(1)} %fusion.101), channel_id=1, replica_groups=mesh['clip'=4,'win'=8] {'clip','win'}, use_global_device_ids=true, to_apply=%region_44.45 | all-reduce | flops 15376 | bytes 123008 | tf_op jit(solution)/shard_map/psum | solution.py:535
  2386.1 25.7 %reduce-scatter.39.cloned.1.call-done = bf16[1024,128]{1,0:T(8,128)(2,1)} async-done(((bf16[4096,128]{1,0:T(8,128)(2,1)}), bf16[1024,128]{1,0:T(8,128)(2,1)}) %reduce-scatter.39.cloned.1.call-update) | async-done | bytes 262160 | tf_op jit(solution)/shard_map/reduce_scatter | solution.py:498
  2413.5 25.7 %reduce-scatter.51.cloned.1.call-done = bf16[256,512]{1,0:T(8,128)(2,1)} async-done(((bf16[1024,512]{1,0:T(8,128)(2,1)}), bf16[256,512]{1,0:T(8,128)(2,1)}) %reduce-scatter.51.cloned.1.call-update) | async-done | bytes 262160 | tf_op jit(solution)/shard_map/reduce_scatter | solution.py:510
  2441.0 25.7 %reduce-scatter.53.cloned.1.call-done = bf16[1024,128]{1,0:T(8,128)(2,1)} async-done(((bf16[4096,128]{1,0:T(8,128)(2,1)}), bf16[1024,128]{1,0:T(8,128)(2,1)}) %reduce-scatter.53.cloned.1.call-update) | async-done | bytes 262160 | tf_op jit(solution)/shard_map/reduce_scatter | solution.py:513
  (537 shorter events, 837.6 us)
Async XLA Ops:
  30.9 338.3 %all-gather.33.cloned.1.call-start = ((), (), s32[]{:S(2)}) async-start(), calls=%async_computation.28 | async-start | bytes 1310720 | tf_op jit(solution)/shard_map/all_gather | solution.py:346
  31.7 347.9 %all-gather.19.cloned.1.call-start = ((), (), s32[]{:S(2)}) async-start(), calls=%async_computation.21 | async-start | bytes 9437184 | tf_op jit(solution)/shard_map/all_gather | solution.py:351
  32.4 471.9 %all-gather.23.cloned.1.call-start = ((), (), s32[]{:S(2)}) async-start(), calls=%async_computation.23 | async-start | bytes 9437184 | tf_op jit(solution)/shard_map/all_gather | solution.py:352
  49.1 555.4 %all-gather.25.cloned.1.call-start = ((), (), s32[]{:S(2)}) async-start(), calls=%async_computation.24 | async-start | bytes 7077888 | tf_op jit(solution)/shard_map/all_gather | solution.py:353
  58.3 624.4 %all-gather.27.cloned.1.call-start = ((), (), s32[]{:S(2)}) async-start(), calls=%async_computation.25 | async-start | bytes 2359296 | tf_op jit(solution)/shard_map/all_gather | solution.py:354
  66.3 715.1 %all-gather.31.cloned.1.call-start = ((), (), s32[]{:S(2)}) async-start(), calls=%async_computation.27 | async-start | bytes 9437184 | tf_op jit(solution)/shard_map/all_gather | solution.py:355
  70.8 836.1 %all-gather.35.cloned.1.call-start = ((), (), s32[]{:S(2)}) async-start(), calls=%async_computation.29 | async-start | bytes 9437184 | tf_op jit(solution)/shard_map/all_gather | solution.py:356
  369.2 1111.8 %reduce-scatter.61.cloned.1.call-start = ((), (), s32[]{:S(2)}) async-start(), calls=%async_computation.46 | async-start | bytes 2359296
  1074.3 408.7 %reduce-scatter.63.cloned.1.call-start = ((), (), s32[]{:S(2)}) async-start(), calls=%async_computation.47 | async-start | bytes 2359296
  1094.8 390.0 %reduce-scatter.57.cloned.1.call-start = ((), (), s32[]{:S(2)}) async-start(), calls=%async_computation.44 | async-start | bytes 2359296
  1236.2 409.6 %reduce-scatter.35.cloned.1.call-start = ((), (), s32[]{:S(2)}) async-start(), calls=%async_computation.32 | async-start | bytes 9437184 | tf_op jit(solution)/shard_map/reduce_scatter | solution.py:466
  1249.0 548.5 %reduce-scatter.59.cloned.1.call-start = ((), (), s32[]{:S(2)}) async-start(), calls=%async_computation.45 | async-start | bytes 9437184
  1273.9 660.3 %all-reduce.4.cloned.1.call-start = ((), (), s32[]{:S(2)}) async-start(), calls=%async_computation.42 | async-start | bytes 2359296 | tf_op jit(solution)/shard_map/psum | solution.py:535
  1444.1 642.2 %reduce-scatter.49.cloned.1.call-start = ((), (), s32[]{:S(2)}) async-start(), calls=%async_computation.39 | async-start | bytes 9437184 | tf_op jit(solution)/shard_map/reduce_scatter | solution.py:481
  1456.1 782.3 %reduce-scatter.65.cloned.1.call-start = ((), (), s32[]{:S(2)}) async-start(), calls=%async_computation.48 | async-start | bytes 9437184
  1481.0 870.7 %reduce-scatter.45.cloned.1.call-start = ((), (), s32[]{:S(2)}) async-start(), calls=%async_computation.37 | async-start | bytes 327680 | tf_op jit(solution)/shard_map/reduce_scatter | solution.py:504
  1482.9 870.3 %reduce-scatter.47.cloned.1.call-start = ((), (), s32[]{:S(2)}) async-start(), calls=%async_computation.38 | async-start | bytes 327680 | tf_op jit(solution)/shard_map/reduce_scatter | solution.py:507
  1484.8 869.9 %reduce-scatter.33.cloned.1.call-start = ((), (), s32[]{:S(2)}) async-start(), calls=%async_computation.31 | async-start | bytes 327680 | tf_op jit(solution)/shard_map/reduce_scatter | solution.py:492
  1486.7 869.5 %reduce-scatter.43.cloned.1.call-start = ((), (), s32[]{:S(2)}) async-start(), calls=%async_computation.36 | async-start | bytes 655360 | tf_op jit(solution)/shard_map/reduce_scatter | solution.py:501
  1487.2 870.5 %reduce-scatter.31.cloned.1.call-start = ((), (), s32[]{:S(2)}) async-start(), calls=%async_computation.30 | async-start | bytes 983040 | tf_op jit(solution)/shard_map/reduce_scatter | solution.py:489
  1495.7 888.6 %reduce-scatter.37.cloned.1.call-start = ((), (), s32[]{:S(2)}) async-start(), calls=%async_computation.33 | async-start | bytes 1310720 | tf_op jit(solution)/shard_map/reduce_scatter | solution.py:495
  1645.8 766.0 %reduce-scatter.39.cloned.1.call-start = ((), (), s32[]{:S(2)}) async-start(), calls=%async_computation.34 | async-start | bytes 1310720 | tf_op jit(solution)/shard_map/reduce_scatter | solution.py:498
  1799.9 639.3 %reduce-scatter.51.cloned.1.call-start = ((), (), s32[]{:S(2)}) async-start(), calls=%async_computation.40 | async-start | bytes 1310720 | tf_op jit(solution)/shard_map/reduce_scatter | solution.py:510
  2086.4 380.3 %reduce-scatter.53.cloned.1.call-start = ((), (), s32[]{:S(2)}) async-start(), calls=%async_computation.41 | async-start | bytes 1310720 | tf_op jit(solution)/shard_map/reduce_scatter | solution.py:513
  (138 other events, 8833.7 us)
Sparse Core Ops, SparseCore 0:
  71.3 105.3 all-gather.12
  178.6 49.2 all-gather.14
  246.8 132.6 all-gather.18
  381.6 122.6 all-gather.22
  506.4 98.1 all-gather.24
  606.4 49.2 all-gather.26
  657.8 123.5 all-gather.30
  783.3 123.5 all-gather.34
  1074.4 66.0 reduce-scatter.60
  1143.9 66.7 reduce-scatter.62
  1214.0 66.7 reduce-scatter.56
  1284.3 87.3 reduce-scatter.40
  1375.5 117.7 reduce-scatter.54
  1497.2 148.5 reduce-scatter.34
  1649.4 148.0 reduce-scatter.58
  1804.2 130.0 all-reduce.3
  1937.9 148.3 reduce-scatter.48
  2090.4 147.9 reduce-scatter.64
  2309.2 21.6 reduce-scatter.42
  2333.3 23.3 reduce-scatter.30
  2359.3 24.9 reduce-scatter.36
  2386.8 24.8 reduce-scatter.38
  2414.3 24.8 reduce-scatter.50
  2441.8 24.8 reduce-scatter.52
  (7 shorter events, 128.4 us)
where the time goes:
time: 2490 us; the launch traced here: 2480 us
  waiting for transfers between devices  1190 us (48%)
  matrix products  578 us (23%)
  local copies, waits for them, and re-layouts  449 us (18%)
  other arithmetic  117 us (5%)
  blocking collectives  111 us (4%)
    unnamed x37, waiting for transfers between devices  232 us
    reduce_scatter x1, waiting for transfers between devices, body(): lax.psum_scatter(local_grads[2].astype(jnp.bfloat16), 'win', scatter_dime...  150 us
    reduce_scatter x1, waiting for transfers between devices, body(): lax.psum_scatter(local_grads[7].astype(jnp.bfloat16), 'win', scatter_dime...  149 us
    dot_general x3, matrix products, joint_bias_grad(): jnp.einsum('hjlnikm,ija,klb,mnc->habc', shaped, frame_onehot, side_onehot...  136 us
    psum x1, waiting for transfers between devices, body(): lax.psum((spatial_bias_grad(grad_bias_a), joint_bias_grad(grad_bias_b)),...  134 us
    unnamed x277, local copies, waits for them, and re-layouts  114 us
    all_gather x1, waiting for transfers between devices, body(): lax.all_gather(clip_gathered[7], 'win', axis=1, tiled=True)  114 us
    all_gather x1, waiting for transfers between devices, body(): lax.all_gather(clip_gathered[3], 'win', axis=1, tiled=True)  92.9 us
  transfers between devices with their start and end apart: 35, of which 17 were waited for; matrix products, arithmetic and copies ran while one was open for 39% of the time, Pallas kernels for 0%

commit v1 on v0

v1 whole, which is shorter than its diff:
```python
from functools import partial

import jax
import jax.numpy as jnp
from jax import lax
from jax.experimental import pallas as pl
from jax.experimental.pallas import tpu as pltpu
from jax.sharding import PartitionSpec as P

HEADS = 16
WS = 16
FR = 5
LOC_W = 4
PAIR_LOCS = 1
HS = 8
SLOTS = 3
VMEM_BYTES = 56 * 1024 * 1024

epsilon = 1e-06
masked_score = -1000000000.0
highest = lax.Precision.HIGHEST
NT = (((1,), (1,)), ((), ()))
TN = (((0,), (0,)), ((), ()))


BITS = {"core": ("clip", 1), "x": ("clip", 2), "y": ("win", 1), "z0": ("win", 2), "z1": ("win", 4)}


def hop(value, link):
    axis, mask = BITS[link]
    return lax.ppermute(value, axis, [(i, i ^ mask) for i in range(lax.axis_size(axis))])


def z_groups():
    size = lax.axis_size("win")
    return [list(range(start, size, 2)) for start in range(2)]


class Gather:
    def __init__(self, shard):
        rows, cols = shard.shape
        self.rows = rows
        halves = shard.reshape(2, rows // 2, cols)
        grown = lax.all_gather(halves, "win", axis=1, tiled=False, axis_index_groups=z_groups())
        self.values = (grown[0], grown[1])
        self.stage = 0

    def advance(self, values):
        if self.stage == 0:
            a0, b0 = values
            new = (jnp.stack([a0, hop(a0, "y")]), jnp.stack([b0, hop(b0, "x")]))
        elif self.stage == 1:
            a1, b1 = values
            new = (a1, hop(a1, "x"), hop(a1, "core"), b1, hop(b1, "y"), hop(b1, "core"))
        else:
            a1, a2, a3, b1, b2, b3 = values
            new = (a1, a2, a3, hop(a2, "core"), b1, b2, b3, hop(b2, "core"))
        self.values = new
        self.stage += 1


def assemble_kernel(row_of, y_of, *refs, rows, widths):
    count = len(widths)
    pieces = refs[:8]
    outs = refs[8 : 8 + count]
    whole = refs[8 + count : 8 + 2 * count]
    in_sems, out_sems = refs[8 + 2 * count :]
    half = rows // 2
    bands = []
    for part in range(2):
        for c_rel in range(2):
            for x_rel in range(2):
                block = row_of[c_rel * 2 + x_rel]
                row = pl.multiple_of(block * rows + part * half, half)
                copies = []
                for y_rel in range(2):
                    far, near = (x_rel, y_rel) if part == 0 else (y_rel, x_rel)
                    source = pieces[part * 4 + c_rel * 2 + far]
                    for z in range(4):
                        place = z * 2 + y_of[y_rel]
                        start = 0
                        for held, width in zip(whole, widths):
                            col = pl.multiple_of(place * width, 128)
                            copies.append(
                                pltpu.make_async_copy(
                                    source.at[near, z, :, pl.ds(start, width)],
                                    held.at[pl.ds(row, half), pl.ds(col, width)],
                                    in_sems.at[len(bands) * 8 * count + len(copies)],
                                )
                            )
                            start += width
                bands.append((row, copies))
    for row, copies in bands:
        for copy in copies:
            copy.start()
    sent = []
    for band, (row, copies) in enumerate(bands):
        for copy in copies:
            copy.wait()
        for which, (held, out) in enumerate(zip(whole, outs)):
            there = pl.ds(row, half)
            sent.append(
                pltpu.make_async_copy(held.at[there], out.at[there], out_sems.at[band * count + which])
            )
            sent[-1].start()
    for copy in sent:
        copy.wait()


def assemble(values, place, rows, widths):
    shapes = [(4 * rows, 8 * width) for width in widths]
    return pl.pallas_call(
        partial(assemble_kernel, rows=rows, widths=widths),
        out_shape=[jax.ShapeDtypeStruct(shape, jnp.bfloat16) for shape in shapes],
        in_specs=[pl.BlockSpec(memory_space=pltpu.SMEM)] * 2 + [pl.BlockSpec(memory_space=pl.ANY)] * 8,
        out_specs=[pl.BlockSpec(memory_space=pl.ANY)] * len(widths),
        scratch_shapes=[pltpu.VMEM(shape, jnp.bfloat16) for shape in shapes]
        + [pltpu.SemaphoreType.DMA((64 * len(widths),)), pltpu.SemaphoreType.DMA((8 * len(widths),))],
        compiler_params=pltpu.CompilerParams(vmem_limit_bytes=VMEM_BYTES),
        cost_estimate=pl.CostEstimate(
            flops=0, bytes_accessed=4 * sum(a * b for a, b in shapes), transcendentals=0
        ),
        name="assemble",
    )(place["rows"], place["cols"], *values)


def grad_kernel(row_of, y_of, x_ref, *refs, part, rows, widths):
    dy_refs = refs[: len(widths)]
    out_ref, turned = refs[len(widths) :]
    half = rows // 2
    total = sum(widths)

    @pl.when(pl.program_id(0) == 0)
    def turn():
        for x_rel in range(2):
            start = pl.multiple_of(row_of[part * 2 + x_rel] * rows, rows)
            turned[x_rel * rows : (x_rel + 1) * rows, :] = x_ref[:, pl.ds(start, rows)].T

    offset = 0
    for dy_ref, width in zip(dy_refs, widths):
        product = jnp.dot(turned[...], dy_ref[...], preferred_element_type=jnp.float32)
        for y in range(2):
            for x_rel in range(2):
                for ab in range(2):
                    first = x_rel * rows + ab * half
                    out_ref[ab, x_rel, y_of[y], 0, :, offset : offset + width] = product[
                        first : first + half, y * width : (y + 1) * width
                    ].astype(jnp.bfloat16)
        offset += width


def weight_grad(x, dys, place, part, rows, widths, starts):
    count = x.shape[0]
    total = sum(widths)
    return pl.pallas_call(
        partial(grad_kernel, part=part, rows=rows, widths=widths),
        grid=(4,),
        out_shape=jax.ShapeDtypeStruct((2, 2, 2, 4, rows // 2, total), jnp.bfloat16),
        in_specs=[pl.BlockSpec(memory_space=pltpu.SMEM)] * 2
        + [pl.BlockSpec((count, 4 * rows), lambda z: (0, 0))]
        + [
            pl.BlockSpec((count, 2 * width), lambda z, s=start: (0, s + z))
            for width, start in zip(widths, starts)
        ],
        out_specs=pl.BlockSpec((2, 2, 2, 1, rows // 2, total), lambda z: (0, 0, 0, z, 0, 0)),
        scratch_shapes=[pltpu.VMEM((2 * rows, count), jnp.bfloat16)],
        compiler_params=pltpu.CompilerParams(vmem_limit_bytes=VMEM_BYTES),
        cost_estimate=pl.CostEstimate(
            flops=2 * count * 2 * rows * 8 * total,
            bytes_accessed=2 * count * (4 * rows + 8 * total) + 32 * rows * total,
            transcendentals=0,
        ),
        name="weight_grad",
    )(place["rows"], place["cols"], x, *dys)


class Scatter:
    def __init__(self, values):
        self.values = values
        self.stage = 0

    def advance(self, values):
        if self.stage == 0:
            send, keep = values
            new = (keep, hop(send, "core"))
        elif self.stage == 1:
            keep, came = values
            a_send = keep[0, 1] + came[0, 1]
            b_send = keep[1, :, 1] + came[1, :, 1]
            a_keep = keep[0, 0] + came[0, 0]
            b_keep = keep[1, :, 0] + came[1, :, 0]
            new = (a_keep, hop(a_send, "x"), b_keep, hop(b_send, "y"))
        elif self.stage == 2:
            a_keep, a_came, b_keep, b_came = values
            a_send = a_keep[1] + a_came[1]
            b_send = b_keep[1] + b_came[1]
            new = (a_keep[0] + a_came[0], hop(a_send, "y"), b_keep[0] + b_came[0], hop(b_send, "x"))
        else:
            a_keep, a_came, b_keep, b_came = values
            both = jnp.stack([a_keep + a_came, b_keep + b_came], axis=1)
            mine = lax.psum_scatter(
                both.reshape(-1, both.shape[-1]),
                "win",
                scatter_dimension=0,
                tiled=True,
                axis_index_groups=z_groups(),
            )
            new = mine.astype(jnp.float32)
        self.values = new
        self.stage += 1


class Total:
    def __init__(self, value, links):
        self.shape = value.shape
        self.size = value.size
        self.values = jnp.pad(value.reshape(-1), (0, -value.size % 1024)).reshape(-1, 128)
        self.links = list(links)

    def advance(self, values):
        self.values = values + hop(values, self.links.pop(0))

    def result(self):
        return self.values.reshape(-1)[: self.size].reshape(self.shape)


def together(jobs, state):
    held, state = lax.optimization_barrier(([job.values for job in jobs], state))
    for job, values in zip(jobs, held):
        job.advance(values)
    return state


def pair_table(extent):
    table_dims = (extent, extent, 2 * extent - 1)
    query_pos = lax.broadcasted_iota(jnp.int32, table_dims, 0)
    key_pos = lax.broadcasted_iota(jnp.int32, table_dims, 1)
    offset = lax.broadcasted_iota(jnp.int32, table_dims, 2)
    return (query_pos - key_pos + extent - 1 == offset).astype(jnp.float32)


def spatial_strip(table):
    side = 2 * WS - 1
    onehot = pair_table(WS).transpose(2, 1, 0).reshape(side, WS * WS)
    strip = jnp.dot(table.reshape(HEADS * side, side), onehot, precision=highest)
    strip = strip.reshape(HEADS, side, WS, WS).transpose(0, 2, 1, 3).reshape(HEADS, WS, side * WS)
    return jnp.pad(strip, ((0, 0), (0, 0), (0, WS)))


def spatial_strip_back(strip):
    side = 2 * WS - 1
    onehot = pair_table(WS).transpose(2, 1, 0).reshape(side, WS * WS)
    shaped = strip[:, :, : side * WS].reshape(HEADS, WS, side, WS).transpose(0, 2, 1, 3)
    flat = shaped.reshape(HEADS * side, WS * WS)
    return lax.dot_general(flat, onehot, NT, precision=highest).reshape(HEADS, side, side)


def joint_onehot():
    span = 2 * HS - 1
    table_dims = (span * span, HS**4)
    offset = lax.broadcasted_iota(jnp.int32, table_dims, 0)
    pair = lax.broadcasted_iota(jnp.int32, table_dims, 1)
    key_row, key_col = pair // HS**3, pair // HS**2 % HS
    query_row, query_col = pair // HS % HS, pair % HS
    wanted = (query_row - key_row + HS - 1) * span + query_col - key_col + HS - 1
    return (offset == wanted).astype(jnp.float32)


def joint_strip(table):
    frames = 2 * FR - 1
    places = HS * HS
    strip = jnp.dot(table.reshape(HEADS * frames, -1), joint_onehot(), precision=highest)
    strip = strip.reshape(HEADS, frames, places, places).transpose(0, 2, 1, 3)
    return jnp.pad(strip.reshape(HEADS, places, frames * places), ((0, 0), (0, 0), (0, places)))


def joint_strip_back(strip):
    frames = 2 * FR - 1
    places = HS * HS
    shaped = strip[:, :, : frames * places].reshape(HEADS, places, frames, places).transpose(0, 2, 1, 3)
    flat = shaped.reshape(HEADS * frames, places * places)
    grad = lax.dot_general(flat, joint_onehot(), NT, precision=highest)
    return grad.reshape(HEADS, frames, 2 * HS - 1, 2 * HS - 1)


def head_lanes(which):
    lane = lax.broadcasted_iota(jnp.int32, (1, 128), 1)
    return (lane // 64 == which).astype(jnp.float32)


def attend_kernel(q_ref, k_ref, v_ref, strip_ref, mask_ref, out_ref, probs_ref, bias, *, wins, length):
    rows, lanes = strip_ref.shape[1:]
    blocks = length // rows
    masks = mask_ref.shape[0]
    for head in range(2):
        strip = strip_ref[head]
        for block in range(blocks):
            offset = (blocks - 1 - block) * rows
            turned = strip if offset == 0 else pltpu.roll(strip, lanes - offset, 1)
            bias[block * rows : (block + 1) * rows, :] = turned[:, :length]
        chosen = head_lanes(head)
        low = chosen.astype(jnp.bfloat16)
        for win in range(wins):
            here = slice(win * length, (win + 1) * length)
            queries = q_ref[here, :] * jnp.bfloat16(0.125)
            scores = lax.dot_general(k_ref[here, :] * low, queries, NT, preferred_element_type=jnp.float32)
            scores = jnp.where(mask_ref[win % masks] > 0.0, scores + bias[...], masked_score)
            raised = jnp.exp(scores - jnp.max(scores, axis=0, keepdims=True))
            probs = raised * (1.0 / jnp.sum(raised, axis=0, keepdims=True))
            probs = probs.astype(jnp.bfloat16)
            probs_ref[head, win] = probs
            mixed = lax.dot_general(probs, v_ref[here, :] * low, TN, preferred_element_type=jnp.float32)
            if head == 0:
                out_ref[here, :] = mixed.astype(jnp.bfloat16)
            else:
                out_ref[here, :] = out_ref[here, :] + mixed.astype(jnp.bfloat16)


def attend(qkv, strip, allowed, wins, length):
    count, triple = qkv.shape
    width = triple // 3
    rows, lanes = strip.shape[1:]
    return pl.pallas_call(
        partial(attend_kernel, wins=wins, length=length),
        grid=(HEADS // 2,),
        out_shape=[
            jax.ShapeDtypeStruct((count, width), jnp.bfloat16),
            jax.ShapeDtypeStruct((HEADS, wins, length, length), jnp.bfloat16),
        ],
        in_specs=[
            pl.BlockSpec((count, 128), lambda h: (0, h)),
            pl.BlockSpec((count, 128), lambda h: (0, HEADS // 2 + h)),
            pl.BlockSpec((count, 128), lambda h: (0, HEADS + h)),
            pl.BlockSpec((2, rows, lanes), lambda h: (h, 0, 0)),
            pl.BlockSpec(allowed.shape, lambda h: (0, 0, 0)),
        ],
        out_specs=[
            pl.BlockSpec((count, 128), lambda h: (0, h)),
            pl.BlockSpec((2, wins, length, length), lambda h: (h, 0, 0, 0)),
        ],
        scratch_shapes=[pltpu.VMEM((length, length), jnp.float32)],
        compiler_params=pltpu.CompilerParams(vmem_limit_bytes=VMEM_BYTES),
        cost_estimate=pl.CostEstimate(
            flops=8 * HEADS * wins * length * length * 64,
            bytes_accessed=8 * count * width + 2 * HEADS * wins * length * length,
            transcendentals=HEADS * wins * length * length,
        ),
        name="attend",
    )(qkv, qkv, qkv, strip, allowed)


def attend_back_kernel(q_ref, k_ref, v_ref, g_ref, probs_ref, out_ref, strip_ref, total, *, wins, length):
    rows, lanes = strip_ref.shape[1:]
    blocks = length // rows
    width = out_ref.shape[1] // 3
    step = pl.program_id(0)
    grads = [[None] * 3 for _ in range(wins)]
    total[...] = jnp.zeros_like(total)
    for head in range(2):
        chosen = head_lanes(head)
        low = chosen.astype(jnp.bfloat16)
        for win in range(wins):
            here = slice(win * length, (win + 1) * length)
            queries = q_ref[here, :] * jnp.bfloat16(0.125)
            key_rows = k_ref[here, :]
            outer = g_ref[here, :]
            probs = probs_ref[head, win]
            grad_probs = lax.dot_general(v_ref[here, :] * low, outer, NT, preferred_element_type=jnp.float32)
            wide = probs.astype(jnp.float32)
            inner = jnp.sum(wide * grad_probs, axis=0, keepdims=True)
            grad_scores = (wide * (grad_probs - inner)).astype(jnp.bfloat16)
            if win == 0:
                total[:, :length] = grad_scores.astype(jnp.float32)
            else:
                total[:, :length] = total[:, :length] + grad_scores.astype(jnp.float32)
            new = (
                lax.dot_general(grad_scores, key_rows, TN, preferred_element_type=jnp.float32) * 0.125,
                jnp.dot(grad_scores, queries, preferred_element_type=jnp.float32),
                jnp.dot(probs, outer, preferred_element_type=jnp.float32),
            )
            for kind in range(3):
                column = pl.multiple_of(step * 128 + kind * width, 128)
                if head == 0:
                    out_ref[here, pl.ds(column, 128)] = (new[kind] * chosen).astype(jnp.bfloat16)
                else:
                    out_ref[here, pl.ds(column, 128)] = out_ref[here, pl.ds(column, 128)] + (
                        new[kind] * chosen
                    ).astype(jnp.bfloat16)
        strip = total[:rows, :] if blocks == 1 else pltpu.roll(total[:rows, :], (blocks - 1) * rows, 1)
        for block in range(1, blocks):
            offset = (blocks - 1 - block) * rows
            piece = total[block * rows : (block + 1) * rows, :]
            strip = strip + (piece if offset == 0 else pltpu.roll(piece, offset, 1))
        strip_ref[head] = strip


def attend_back(qkv, probs, grad_out, wins, length, rows, lanes):
    count, triple = qkv.shape
    width = triple // 3
    return pl.pallas_call(
        partial(attend_back_kernel, wins=wins, length=length),
        grid=(HEADS // 2,),
        out_shape=[
            jax.ShapeDtypeStruct((count, triple), jnp.bfloat16),
            jax.ShapeDtypeStruct((HEADS, rows, lanes), jnp.float32),
        ],
        in_specs=[
            pl.BlockSpec((count, 128), lambda h: (0, h)),
            pl.BlockSpec((count, 128), lambda h: (0, HEADS // 2 + h)),
            pl.BlockSpec((count, 128), lambda h: (0, HEADS + h)),
            pl.BlockSpec((count, 128), lambda h: (0, h)),
            pl.BlockSpec((2, wins, length, length), lambda h: (h, 0, 0, 0)),
        ],
        out_specs=[
            pl.BlockSpec((count, triple), lambda h: (0, 0)),
            pl.BlockSpec((2, rows, lanes), lambda h: (h, 0, 0)),
        ],
        scratch_shapes=[pltpu.VMEM((length, lanes), jnp.float32)],
        compiler_params=pltpu.CompilerParams(vmem_limit_bytes=VMEM_BYTES),
        cost_estimate=pl.CostEstimate(
            flops=20 * HEADS * wins * length * length * 64,
            bytes_accessed=14 * count * width + 2 * HEADS * wins * length * length,
            transcendentals=0,
        ),
        name="attend_back",
    )(qkv, qkv, qkv, grad_out, probs)


def plain_norm(values):
    center = values - jnp.mean(values, axis=-1, keepdims=True)
    spread = jnp.mean(center * center, axis=-1, keepdims=True)
    scale = lax.rsqrt(spread + epsilon)
    return center * scale, scale


def modulated_norm(values, shift_vec, scale_vec):
    return (plain_norm(values)[0] * (1.0 + scale_vec) + shift_vec).astype(jnp.bfloat16)


def norm_back(grad_in, values, scale_vec):
    unit, scale = plain_norm(values)
    inner = grad_in * (1.0 + scale_vec)
    mean_one = jnp.mean(inner, axis=-1, keepdims=True)
    mean_two = jnp.mean(inner * unit, axis=-1, keepdims=True)
    grad = scale * (inner - mean_one - unit * mean_two)
    return grad, jnp.sum(grad_in, axis=0), jnp.sum(grad_in * unit, axis=0)


def product(left, right):
    return jnp.dot(left, right, preferred_element_type=jnp.float32)


def product_turned(left, right):
    return lax.dot_general(left, right, NT, preferred_element_type=jnp.float32)


def gelu_both(upward):
    half = 0.5 * (1.0 + lax.erf(upward * 0.7071067811865476))
    density = 0.3989422804014327 * jnp.exp(-0.5 * upward * upward)
    return (upward * half).astype(jnp.bfloat16), (half + upward * density).astype(jnp.bfloat16)


def joint_group(rows):
    split = rows.reshape(FR * HS, 2, HS, rows.shape[-1])
    return split.transpose(1, 0, 2, 3).reshape(rows.shape)


def joint_ungroup(rows):
    split = rows.reshape(2, FR * HS, HS, rows.shape[-1])
    return split.transpose(1, 0, 2, 3).reshape(rows.shape)


def window_group(flat_rows):
    return flat_rows.reshape(SLOTS, WS * WS, flat_rows.shape[-1])


def split_halves(half_rows, own_half):
    pair_windows = half_rows.shape[0]
    filler = jnp.zeros((2 * SLOTS - pair_windows,) + half_rows.shape[1:], half_rows.dtype)
    padded = jnp.concatenate([half_rows, filler], axis=0)
    keep_part = lax.dynamic_slice_in_dim(padded, own_half * SLOTS, SLOTS, 0)
    send_part = lax.dynamic_slice_in_dim(padded, (1 - own_half) * SLOTS, SLOTS, 0)
    return (keep_part, send_part)


def join_windows(keep_part, came_part, own_half):
    upper_half = jnp.where(own_half == 0, keep_part, came_part)
    lower_half = jnp.where(own_half == 0, came_part, keep_part)
    joined = jnp.concatenate([upper_half, lower_half], axis=1)
    return joined.reshape(-1, joined.shape[-1])


def split_windows(win_rows, own_half):
    grouped = window_group(win_rows)
    half_len = grouped.shape[1] // 2
    upper_half = grouped[:, :half_len]
    lower_half = grouped[:, half_len:]
    keep_part = jnp.where(own_half == 0, upper_half, lower_half)
    send_part = jnp.where(own_half == 0, lower_half, upper_half)
    return (keep_part, send_part)


def join_halves(keep_part, came_part, own_half, pair_windows):
    leading = jnp.where(own_half == 0, keep_part, came_part)
    trailing = jnp.where(own_half == 0, came_part, keep_part)
    joined = jnp.concatenate([leading, trailing], axis=0)[:pair_windows]
    return joined.reshape(-1, joined.shape[-1])


def from_pair(value):
    pairs = [(i, i ^ 1) for i in range(lax.axis_size("win"))]
    return lax.ppermute(value, "win", pairs)


def leave_windows(win_rows, own_half, pair_windows):
    keep_part, send_part = split_windows(win_rows, own_half)
    came_part = from_pair(send_part.astype(jnp.bfloat16)).astype(send_part.dtype)
    return join_halves(keep_part, came_part, own_half, pair_windows)


def enter_windows(flat_rows, own_half, pair_windows):
    half_rows = flat_rows.reshape(pair_windows, -1, flat_rows.shape[-1])
    keep_part, send_part = split_halves(half_rows, own_half)
    came_part = from_pair(send_part.astype(jnp.bfloat16)).astype(send_part.dtype)
    return join_windows(keep_part, came_part, own_half)


class Weights:
    def __init__(self, masters, place, quick):
        self.quick = quick
        low = [master.astype(jnp.bfloat16) for master in masters]
        self.place = place
        if quick:
            shards = []
            for block in range(2):
                qkv, out, up, down = low[4 * block : 4 * block + 4]
                shards += [jnp.concatenate([qkv, out], axis=1), up, down]
            self.widths = [(384, 128), (512,), (128,)] * 2
            self.jobs = [Gather(shard) for shard in shards]
        else:
            self.full = [
                lax.all_gather(lax.all_gather(shard, "win", axis=1, tiled=True), "clip", axis=0, tiled=True)
                for shard in low
            ]
            self.full = [tuple(self.full[0:2]), (self.full[2],), (self.full[3],)] + [
                tuple(self.full[4:6]),
                (self.full[6],),
                (self.full[7],),
            ]

    def round(self, active, state):
        if not self.quick:
            return state
        return together([self.jobs[unit] for unit in active], state)

    def take(self, unit):
        if not self.quick:
            return self.full[unit]
        job = self.jobs[unit]
        return assemble(job.values, self.place, job.rows, self.widths[unit])


def body(
    tokens,
    grad_output,
    clip_height,
    clip_width,
    modulation,
    sp_qkv,
    sp_out,
    sp_up,
    sp_down,
    sp_table,
    st_qkv,
    st_out,
    st_up,
    st_down,
    st_table,
    quick,
):
    model_width = tokens.shape[-1]
    half_len = tokens.shape[-2]
    pair_windows = PAIR_LOCS * FR
    shard_index = lax.axis_index("win")
    clip_index = lax.axis_index("clip")
    pair_index = shard_index // 2
    own_half = shard_index % 2
    own_core = clip_index % 2
    own_x = clip_index // 2
    row_places = [
        (own_x ^ x_rel) * 2 + (own_core ^ c_rel) for c_rel in range(2) for x_rel in range(2)
    ]
    place = {
        "rows": jnp.stack(row_places).astype(jnp.int32),
        "cols": jnp.stack([own_half, own_half ^ 1]).astype(jnp.int32),
    }
    weights = Weights(
        (sp_qkv, sp_out, sp_up, sp_down, st_qkv, st_out, st_up, st_down), place, quick
    )
    mod = modulation[0]

    location = pair_index
    token_ids = jnp.arange(WS * WS, dtype=jnp.int32)
    row_pos = location // LOC_W * WS + token_ids // WS
    col_pos = location % LOC_W * WS + token_ids % WS
    sp_valid = (row_pos < clip_height[0]) & (col_pos < clip_width[0])
    sp_allowed = (sp_valid[None, :, None] | jnp.eye(WS * WS, dtype=bool)[None]).astype(jnp.float32)
    joint_len = FR * HS * HS
    joint_ids = jnp.arange(joint_len, dtype=jnp.int32)
    joint_row = location // LOC_W * WS + own_half * HS + joint_ids // HS % HS
    joint_col = location % LOC_W * WS + jnp.arange(2, dtype=jnp.int32)[:, None] * HS + joint_ids[None] % HS
    st_valid = (joint_row[None] < clip_height[0]) & (joint_col < clip_width[0])
    st_allowed = (st_valid[:, :, None] | jnp.eye(joint_len, dtype=bool)[None]).astype(jnp.float32)

    half_tokens = tokens.reshape(pair_windows, half_len, model_width)
    win_input = enter_windows(half_tokens, own_half, pair_windows).astype(jnp.float32)
    sp_strip = spatial_strip(sp_table)
    st_strip = joint_strip(st_table)
    attn_in_a = modulated_norm(win_input, mod[0], mod[1])

    state = (win_input, attn_in_a)
    state = weights.round([0], state)
    state = weights.round([0], state)
    state = weights.round([0, 1], state)
    win_input, attn_in_a = weights.round([1], state)
    w_qkv_a, w_out_a = weights.take(0)
    qkv_a = product(attn_in_a, w_qkv_a).astype(jnp.bfloat16)
    win_input, qkv_a, w_out_a = weights.round([2], (win_input, qkv_a, w_out_a))
    attn_out_a, probs_a = attend(qkv_a, sp_strip, sp_allowed, SLOTS, WS * WS)
    win_input, attn_out_a, w_out_a = weights.round([1], (win_input, attn_out_a, w_out_a))
    mixed_a = product(attn_out_a, w_out_a)
    win_middle = win_input + mod[2] * mixed_a
    middle_a = joint_group(leave_windows(win_middle, own_half, pair_windows))
    mlp_in_a = modulated_norm(middle_a, mod[3], mod[4])

    middle_a, mlp_in_a = weights.round([2, 3], (middle_a, mlp_in_a))
    (w_up_a,) = weights.take(1)
    hidden_a, slope_a = gelu_both(product(mlp_in_a, w_up_a))
    middle_a, hidden_a, slope_a = weights.round([2], (middle_a, hidden_a, slope_a))

    middle_a, hidden_a = weights.round([3, 4], (middle_a, hidden_a))
    (w_down_a,) = weights.take(2)
    downward_a = product(hidden_a, w_down_a)
    first_out = middle_a + mod[5] * downward_a
    attn_in_b = modulated_norm(first_out, mod[6], mod[7])
    first_out, attn_in_b = weights.round([3], (first_out, attn_in_b))

    first_out, attn_in_b = weights.round([4, 5], (first_out, attn_in_b))
    w_qkv_b, w_out_b = weights.take(3)
    qkv_b = product(attn_in_b, w_qkv_b).astype(jnp.bfloat16)
    first_out, qkv_b, w_out_b = weights.round([4], (first_out, qkv_b, w_out_b))
    attn_out_b, probs_b = attend(qkv_b, st_strip, st_allowed, 2, joint_len)
    mixed_b = product(attn_out_b, w_out_b)
    middle_b = first_out + mod[8] * mixed_b
    mlp_in_b = modulated_norm(middle_b, mod[9], mod[10])

    middle_b, mlp_in_b = weights.round([5], (middle_b, mlp_in_b))
    (w_up_b,) = weights.take(4)
    hidden_b, slope_b = gelu_both(product(mlp_in_b, w_up_b))
    middle_b, hidden_b, slope_b = weights.round([5], (middle_b, hidden_b, slope_b))
    (w_down_b,) = weights.take(5)
    downward_b = product(hidden_b, w_down_b)
    out_rows = middle_b + mod[11] * downward_b
    out_tokens = joint_ungroup(out_rows).reshape(tokens.shape)

    def start_grad(x, dys, rows, widths, starts):
        if quick:
            return Scatter(
                tuple(weight_grad(x, dys, place, part, rows, widths, starts) for part in (1, 0))
            )
        return Plain(x, dys, widths, starts)

    def rounds(jobs, state):
        if quick:
            return together(jobs, state)
        return state

    grad_out_b = joint_group(grad_output.reshape(-1, model_width)).astype(jnp.float32)
    grad_down_b = (mod[11] * grad_out_b).astype(jnp.bfloat16)
    grad_gate_mb = jnp.sum(grad_out_b * downward_b, axis=0)
    d_st_down = start_grad(hidden_b, [grad_down_b], 1024, (128,), (0,))
    grad_down_b = rounds([d_st_down], grad_down_b)
    grad_up_b = (product_turned(grad_down_b, w_down_b) * slope_b).astype(jnp.bfloat16)
    grad_up_b = rounds([d_st_down], grad_up_b)
    d_st_up = start_grad(mlp_in_b, [grad_up_b], 256, (512,), (0,))
    grad_up_b = rounds([d_st_up, d_st_down], grad_up_b)
    grad_mlp_b = product_turned(grad_up_b, w_up_b)
    norm_grad, grad_shift_mb, grad_scale_mb = norm_back(grad_mlp_b, middle_b, mod[10])
    grad_middle_b = grad_out_b + norm_grad
    grad_mixed_b = (mod[8] * grad_middle_b).astype(jnp.bfloat16)
    grad_gate_ab = jnp.sum(grad_middle_b * mixed_b, axis=0)
    grad_middle_b, grad_mixed_b = rounds([d_st_up, d_st_down], (grad_middle_b, grad_mixed_b))
    d_st_out = start_grad(attn_out_b, [grad_mixed_b], 256, (128,), (0,))
    grad_attn_b = product_turned(grad_mixed_b, w_out_b).astype(jnp.bfloat16)
    grad_qkv_b, strip_grad_b = attend_back(
        qkv_b, probs_b, grad_attn_b, 2, joint_len, st_strip.shape[1], st_strip.shape[2]
    )
    grad_middle_b, grad_qkv_b = rounds([d_st_out, d_st_up], (grad_middle_b, grad_qkv_b))
    st_total = Total(joint_strip_back(strip_grad_b), ("x", "core", "y", "z0", "z1"))
    d_st_qkv = start_grad(attn_in_b, [grad_qkv_b, grad_qkv_b], 256, (256, 128), (0, 8))
    grad_middle_b, grad_qkv_b = rounds(
        [d_st_qkv, d_st_out, d_st_up], (grad_middle_b, grad_qkv_b)
    )
    grad_in_b = product_turned(grad_qkv_b, w_qkv_b)
    norm_grad, grad_shift_ab, grad_scale_ab = norm_back(grad_in_b, first_out, mod[7])
    grad_first = grad_middle_b + norm_grad
    grad_down_a = (mod[5] * grad_first).astype(jnp.bfloat16)
    grad_gate_ma = jnp.sum(grad_first * downward_a, axis=0)
    grad_first, grad_down_a = rounds([d_st_qkv, d_st_out, st_total], (grad_first, grad_down_a))

    d_sp_down = start_grad(hidden_a, [grad_down_a], 1024, (128,), (0,))
    grad_first, grad_down_a = rounds(
        [d_sp_down, d_st_qkv, d_st_out, st_total], (grad_first, grad_down_a)
    )
    grad_up_a = (product_turned(grad_down_a, w_down_a) * slope_a).astype(jnp.bfloat16)
    d_sp_up = start_grad(mlp_in_a, [grad_up_a], 256, (512,), (0,))
    grad_first, grad_up_a = rounds([d_sp_down, d_sp_up, d_st_qkv, st_total], (grad_first, grad_up_a))
    grad_mlp_a = product_turned(grad_up_a, w_up_a)
    norm_grad, grad_shift_ma, grad_scale_ma = norm_back(grad_mlp_a, middle_a, mod[4])
    grad_middle_a = joint_ungroup(grad_first + norm_grad)
    grad_win = enter_windows(grad_middle_a, own_half, pair_windows)
    grad_mixed_a = (mod[2] * grad_win).astype(jnp.bfloat16)
    grad_gate_aa = jnp.sum(grad_win * mixed_a, axis=0)
    grad_win, grad_mixed_a = rounds([d_sp_up, d_sp_down, st_total], (grad_win, grad_mixed_a))
    d_sp_out = start_grad(attn_out_a, [grad_mixed_a], 256, (128,), (0,))
    grad_attn_a = product_turned(grad_mixed_a, w_out_a).astype(jnp.bfloat16)
    grad_qkv_a, strip_grad_a = attend_back(
        qkv_a, probs_a, grad_attn_a, SLOTS, WS * WS, sp_strip.shape[1], sp_strip.shape[2]
    )
    grad_win, grad_qkv_a = rounds([d_sp_out, d_sp_up, d_sp_down, st_total], (grad_win, grad_qkv_a))
    sp_total = Total(spatial_strip_back(strip_grad_a), ("x", "core", "y", "z0", "z1"))
    d_sp_qkv = start_grad(attn_in_a, [grad_qkv_a], 256, (384,), (0,))
    grad_win, grad_qkv_a = rounds([d_sp_qkv, d_sp_out, d_sp_up, sp_total], (grad_win, grad_qkv_a))
    grad_in_a = product_turned(grad_qkv_a, w_qkv_a)
    norm_grad, grad_shift_aa, grad_scale_aa = norm_back(grad_in_a, win_input, mod[1])
    mod_rows = [
        grad_shift_aa,
        grad_scale_aa,
        grad_gate_aa,
        grad_shift_ma,
        grad_scale_ma,
        grad_gate_ma,
        grad_shift_ab,
        grad_scale_ab,
        grad_gate_ab,
        grad_shift_mb,
        grad_scale_mb,
        grad_gate_mb,
    ]
    mod_total = Total(jnp.stack(mod_rows, axis=0), ("y", "z0", "z1"))
    win_sum = grad_win + norm_grad
    win_sum = rounds([d_sp_qkv, d_sp_out, sp_total, mod_total], win_sum)
    grad_tokens = leave_windows(win_sum, own_half, pair_windows).reshape(tokens.shape)
    grad_tokens = rounds([d_sp_qkv, d_sp_out, sp_total, mod_total], grad_tokens)
    rounds([d_sp_qkv, sp_total, mod_total], ())
    rounds([sp_total], ())
    if quick:
        grad_modulation = mod_total.result()[None]
        grad_sp_table = sp_total.result()
        grad_st_table = st_total.result()
    else:
        grad_modulation = lax.psum(jnp.stack(mod_rows, axis=0), "win")[None]
        grad_sp_table = lax.psum(sp_total.result(), ("clip", "win"))
        grad_st_table = lax.psum(st_total.result(), ("clip", "win"))
    value_width = d_st_out.values.shape[1]
    return (
        out_tokens,
        grad_tokens,
        grad_modulation,
        d_sp_qkv.values,
        d_sp_out.values,
        d_sp_up.values,
        d_sp_down.values,
        grad_sp_table,
        d_st_qkv.values[:, :-value_width],
        d_st_qkv.values[:, -value_width:],
        d_st_out.values,
        d_st_up.values,
        d_st_down.values,
        grad_st_table,
    )


class Plain:
    def __init__(self, x, dys, widths, starts):
        win = lax.axis_size("win")
        grads = []
        for dy, width, start in zip(dys, widths, starts):
            part = dy[:, start * 2 * width : start * 2 * width + 8 * width]
            full = lax.dot_general(x, part, TN, preferred_element_type=jnp.float32)
            full = lax.psum_scatter(
                full.astype(jnp.bfloat16), "clip", scatter_dimension=0, tiled=True
            )
            grads.append(lax.psum_scatter(full, "win", scatter_dimension=1, tiled=True))
        self.values = jnp.concatenate(grads, axis=1).astype(jnp.float32)


def solution(mesh):
    grid = P("clip", "win")
    whole = P("clip", "win", None, None, None, None)
    in_specs = (whole, whole, P("clip"), P("clip"), P("clip", None, None)) + ((grid,) * 4 + (P(),)) * 2
    out_specs = (whole, whole, P("clip", None, None)) + (grid,) * 4 + (P(),) + (grid,) * 5 + (P(),)
    quick = mesh.shape["clip"] == 4 and mesh.shape["win"] == 8
    return jax.shard_map(
        partial(body, quick=quick), mesh=mesh, in_specs=in_specs, out_specs=out_specs, check_vma=False
    )
```

time: 2490 us -> 950 us (0.38)
  waiting for transfers between devices: 1190 us -> 162 us
  matrix products: 578 us -> 161 us
  local copies, waits for them, and re-layouts: 449 us -> 110 us
  Pallas kernels: 0 us -> 238 us
  blocking collectives: 111 us -> 0 us
  starting transfers between devices: 7.89 us -> 87.9 us
  other arithmetic: 117 us -> 164 us
    dot_general x46 -> x20, matrix products: 578 us -> 161 us  [the longest x8 80.6 us: product(): return jnp.dot(left, right, preferred_element_type=jnp.float32)]
    all_gather x12 -> x6, waiting for transfers between devices: 409 us -> 3.37 us  [__init__(): lax.all_gather(halves, 'win', axis=1, tiled=False, axis_index_groups=z_gr...]
    reduce_scatter x12 -> x8, waiting for transfers between devices: 401 us -> 4.3 us  [advance(): lax.psum_scatter(both.reshape(-1, both.shape[-1]), 'win', scatter_dimensi...]
    pallas_call x0 -> x26, Pallas kernels: none -> 238 us  [the longest x16 115 us: weight_grad(): pl.pallas_call(partial(grad_kernel, part=part, rows=rows, widths=widths),...]
    unnamed x37 -> x14, waiting for transfers between devices: 232 us -> 0.23 us
    ppermute x4 -> x105, waiting for transfers between devices: 18.2 us -> 154 us  [the longest x101 140 us: hop(): lax.ppermute(value, axis, [(i, i ^ mask) for i in range(lax.axis_size(axi...]
    psum x1 -> x0, waiting for transfers between devices: 134 us -> none  [body(): lax.psum((spatial_bias_grad(grad_bias_a), joint_bias_grad(grad_bias_b)),...]
    unnamed x277 -> x288, local copies, waits for them, and re-layouts: 114 us -> 17.4 us
  transfers between devices with their start and end apart: 35 -> 119, of which waited for: 17 -> 31; matrix products, arithmetic and copies ran while one was open for 39% -> 43% of each run, Pallas kernels for 0% -> 22%
where the time goes in v1:
time: 950 us; the launch traced here: 941 us
  Pallas kernels  238 us (25%)
  other arithmetic  164 us (17%)
  waiting for transfers between devices  162 us (17%)
  matrix products  161 us (17%)
  local copies, waits for them, and re-layouts  110 us (12%)
  starting transfers between devices  87.9 us (9%)
  between operations  18 us (2%)
    ppermute x101, waiting for transfers between devices, hop(): lax.ppermute(value, axis, [(i, i ^ mask) for i in range(lax.axis_size(axi...  140 us
    pallas_call x16, Pallas kernels, weight_grad(): pl.pallas_call(partial(grad_kernel, part=part, rows=rows, widths=widths),...  115 us
    dot_general x8, matrix products, product(): return jnp.dot(left, right, preferred_element_type=jnp.float32)  80.6 us
    ppermute x101, starting transfers between devices, hop(): lax.ppermute(value, axis, [(i, i ^ mask) for i in range(lax.axis_size(axi...  79.2 us
    dot_general x8, matrix products, product_turned(): return lax.dot_general(left, right, NT, preferred_element_type=jnp.float32)  69 us
    pallas_call x6, Pallas kernels, assemble(): pl.pallas_call(partial(assemble_kernel, rows=rows, widths=widths), out_sh...  48.1 us
    pallas_call x2, Pallas kernels, attend_back(): pl.pallas_call(partial(attend_back_kernel, wins=wins, length=length), gri...  43.6 us
    pallas_call x2, Pallas kernels, attend(): pl.pallas_call(partial(attend_kernel, wins=wins, length=length), grid=(HE...  31.7 us
  transfers between devices with their start and end apart: 119, of which 31 were waited for; matrix products, arithmetic and copies ran while one was open for 43% of the time, Pallas kernels for 22%

profile of v1, /device:TPU:0, one launch (start us, length us, event | category | flops | bytes accessed | tf_op | source)
XLA Modules:
  0.0 941.0 jit_solution(11183910201073378028)
XLA Ops:
  21.7 14.7 %collective-permute-done = bf16[3,128,1024]{2,1,0:T(8,128)(2,1)S(1)} collective-permute-done((bf16[3,128,1024]{2,1,0:T(8,128)(2,1)S(1)}, bf16[3,128,1024]{2,1,0:T(8,128)(2,1)S(1)}, u32[]{:S(2)}, u32[]{:S(2)}) %collective-permute-start) | collective-permute-done | bytes 786464 | tf_op jit(solution)/shard_map/ppermute | solution.py:512
  72.7 13.0 %collective-permute-done.3.refs_1_ = bf16[2,4,128,512]{3,2,1,0:T(8,128)(2,1)} collective-permute-done((bf16[2,4,128,512]{3,2,1,0:T(8,128)(2,1)}, bf16[2,4,128,512]{3,2,1,0:T(8,128)(2,1)}, u32[]{:S(2)}, u32[]{:S(2)}) %collective-permute-start.3) | collective-permute-done | bytes 1048608 | tf_op jit(solution)/shard_map/ppermute | solution.py:31
  126.4 9.4 %convolution_convert_fusion.q_ref.k_ref.v_ref = bf16[768,3072]{1,0:T(8,128)(2,1)} fusion(bf16[768,1024]{1,0:T(8,128)(2,1)S(1)} %copy-done.19, bf16[1024,3072]{1,0:T(8,128)(2,1)} %get-tuple-element.270), kind=kOutput, calls=%fused_computation.28 | convolution fusion | flops 4834197504 | bytes 12582912 | tf_op jit(solution)/shard_map/dot_general | solution.py:450
  136.4 13.6 %attend.2 = (bf16[768,1024]{1,0:T(8,128)(2,1)}, bf16[16,3,256,256]{3,2,1,0:T(8,128)(2,1)}) custom-call(bf16[768,3072]{1,0:T(8,128)(2,1)} %convolution_convert_fusion.q_ref.k_ref.v_ref, bf16[768,3072]{1,0:T(8,128)(2,1)} %convolution_convert_fusion.q_ref.k_ref.v_ref, bf16[768,3072]{1,0:T(8,128)(2,1)} %convolution_convert_fusion.q_ref.k_ref.v_ref, ...), custom_call_target="tpu_custom_call" | custom-call | flops 1610612736 | bytes 12582912 | tf_op jit(solution)/shard_map/attend/pallas_call | solution.py:323
  167.6 23.8 %collective-permute-done.11 = bf16[4,512,128]{2,1,0:T(8,128)(2,1)} collective-permute-done((bf16[4,512,128]{2,1,0:T(8,128)(2,1)}, bf16[4,512,128]{2,1,0:T(8,128)(2,1)}, u32[]{:S(2)}, u32[]{:S(2)}) %collective-permute-start.11) | collective-permute-done | bytes 524320 | tf_op jit(solution)/shard_map/ppermute | solution.py:31
  212.9 13.7 %fusion.4 = (bf16[640,4096]{1,0:T(8,128)(2,1)}, bf16[640,4096]{1,0:T(8,128)(2,1)}) fusion(bf16[640,1024]{1,0:T(8,128)(2,1)S(1)} %add_convert_fusion.3.x_ref, bf16[1024,4096]{1,0:T(8,128)(2,1)} %assemble.7), kind=kOutput, calls=%fused_computation.6 | convolution fusion | flops 5397544960 | bytes 20185088 | tf_op jit(solution)/shard_map/dot_general | solution.py:450
  253.8 11.6 %fusion.56 = (f32[640]{0:T(1024)S(1)}, f32[640,1024]{1,0:T(8,128)S(1)}, f32[640]{0:T(1024)}, f32[640,1024]{1,0:T(8,128)}) fusion(f32[640,1024]{1,0:T(8,128)S(1)} %bitcast.379, f32[1024]{0:T(1024)S(1)} %bitcast.444, f32[640]{0:T(1024)S(1)} %broadcast_multiply_fusion.6, bf16[640,4096]{1,0:T(8,128)(2,1)} %get-tuple-element.302.x_ref, ...), kind=kOutput, calls=%fused_computation.321 | convolution fusion | flops 5372640256 | bytes 21507584 | tf_op jit(solution)/shard_map/dot_general | solution.py:450
  333.6 18.1 %attend.3 = (bf16[640,1024]{1,0:T(8,128)(2,1)}, bf16[16,2,320,320]{3,2,1,0:T(8,128)(2,1)}) custom-call(bf16[640,3072]{1,0:T(8,128)(2,1)} %convolution_convert_fusion.1.q_ref.k_ref.v_ref, bf16[640,3072]{1,0:T(8,128)(2,1)} %convolution_convert_fusion.1.q_ref.k_ref.v_ref, bf16[640,3072]{1,0:T(8,128)(2,1)} %convolution_convert_fusion.1.q_ref.k_ref.v_ref, ...), custom_call_target="tpu_custom_call" | custom-call | flops 1677721600 | bytes 11796480 | tf_op jit(solution)/shard_map/attend/pallas_call | solution.py:323
  368.3 13.6 %fusion.9 = (bf16[640,4096]{1,0:T(8,128)(2,1)}, bf16[640,4096]{1,0:T(8,128)(2,1)}) fusion(bf16[640,1024]{1,0:T(8,128)(2,1)S(1)} %add_convert_fusion.1.x_ref, bf16[1024,4096]{1,0:T(8,128)(2,1)} %assemble.10), kind=kOutput, calls=%fused_computation.11 | convolution fusion | flops 5397544960 | bytes 20185088 | tf_op jit(solution)/shard_map/dot_general | solution.py:450
  384.5 8.8 weight_grad.17
  393.3 8.8 weight_grad.16
  420.3 11.8 %multiply_convert_fusion.1.refs_0_ = bf16[640,4096]{1,0:T(8,128)(2,1)} fusion(bf16[640,4096]{1,0:T(8,128)(2,1)} %get-tuple-element.350, bf16[640,1024]{1,0:T(8,128)(2,1)S(1)} %copy-done.25, bf16[4096,1024]{1,0:T(8,128)(2,1)} %assemble.11), kind=kOutput, calls=%fused_computation.13 | convolution fusion | flops 5376573440 | bytes 20185088 | tf_op jit(solution)/shard_map/dot_general | solution.py:454
  470.0 12.1 %multiply_reduce_fusion.6 = (f32[1024]{0:T(1024)}, f32[640]{0:T(1024)S(1)}, f32[640]{0:T(1024)S(1)}, f32[1024]{0:T(1024)}, f32[640,1024]{1,0:T(8,128)}) fusion(f32[640,1024]{1,0:T(8,128)S(1)} %copy-done.8, f32[640]{0:T(1024)S(1)} %add_rsqrt_fusion.4, f32[640]{0:T(1024)S(1)} %broadcast_multiply_fusion.12, f32[1024]{0:T(1024)S(1)} %bitcast.454, ...), kind=kOutput, calls=%fused_computation.66 | convolution fusion | flops 5374604288 | bytes 18896896 | tf_op jit(solution)/shard_map/dot_general | solution.py:454
  482.2 12.9 %multiply_reduce_fusion.7 = (f32[1024]{0:T(1024)}, f32[640,1024]{1,0:T(8,128)S(1)}, f32[1024]{0:T(1024)}, f32[640,1024]{1,0:T(8,128)}) fusion(f32[640,1024]{1,0:T(8,128)} %get-tuple-element.634, f32[640]{0:T(1024)S(1)} %broadcast_multiply_fusion.10, f32[640,1024]{1,0:T(8,128)S(1)} %copy-done.8, f32[640]{0:T(1024)S(1)} %broadcast_multiply_fusion.12, ...), kind=kOutput, calls=%fused_computation.67 | convolution fusion | flops 5377882112 | bytes 29386752 | tf_op jit(solution)/shard_map/dot_general | solution.py:450
  518.2 21.9 %attend_back.2 = (bf16[640,3072]{1,0:T(8,128)(2,1)}, f32[16,64,640]{2,1,0:T(8,128)}) custom-call(bf16[640,3072]{1,0:T(8,128)(2,1)} %convolution_convert_fusion.1.q_ref.k_ref.v_ref, bf16[640,3072]{1,0:T(8,128)(2,1)} %convolution_convert_fusion.1.q_ref.k_ref.v_ref, bf16[640,3072]{1,0:T(8,128)(2,1)} %convolution_convert_fusion.1.q_ref.k_ref.v_ref, ...), custom_call_target="tpu_custom_call" | custom-call | flops 4194304000 | bytes 15728640 | tf_op jit(solution)/shard_map/attend_back/pallas_call | solution.py:400
  613.5 8.8 weight_grad.25
  642.3 11.7 %multiply_convert_fusion.refs_0_ = bf16[640,4096]{1,0:T(8,128)(2,1)} fusion(bf16[640,4096]{1,0:T(8,128)(2,1)} %get-tuple-element.394, bf16[640,1024]{1,0:T(8,128)(2,1)S(1)} %copy-done.26, bf16[4096,1024]{1,0:T(8,128)(2,1)} %assemble.8), kind=kOutput, calls=%fused_computation.12 | convolution fusion | flops 5376573440 | bytes 20185088 | tf_op jit(solution)/shard_map/dot_general | solution.py:454
  671.7 9.5 %multiply_reduce_fusion.10 = (f32[1024]{0:T(1024)}, f32[640]{0:T(1024)S(1)}, f32[640]{0:T(1024)S(1)}, f32[1024]{0:T(1024)}, f32[640,1024]{1,0:T(8,128)S(1)}) fusion(f32[640,1024]{1,0:T(8,128)S(1)} %bitcast.380, f32[640]{0:T(1024)S(1)} %add_rsqrt_fusion.2, f32[640]{0:T(1024)S(1)} %copy-done.100, f32[1024]{0:T(1024)S(1)} %bitcast.437, ...), kind=kOutput, calls=%fused_computation.70 | convolution fusion | flops 5374604288 | bytes 18896896 | tf_op jit(solution)/shard_map/dot_general | solution.py:454
  697.2 9.6 %collective-permute-done.76 = f32[256,128]{1,0:T(8,128)} collective-permute-done((f32[256,128]{1,0:T(8,128)}, f32[256,128]{1,0:T(8,128)}, u32[]{:S(2)}, u32[]{:S(2)}) %collective-permute-start.76) | collective-permute-done | bytes 131104 | tf_op jit(solution)/shard_map/ppermute | solution.py:31
  713.2 15.5 %collective-permute-done.75 = bf16[2,4,512,128]{3,2,1,0:T(8,128)(2,1)} collective-permute-done((bf16[2,4,512,128]{3,2,1,0:T(8,128)(2,1)}, bf16[2,4,512,128]{3,2,1,0:T(8,128)(2,1)}, u32[]{:S(2)}, u32[]{:S(2)}) %collective-permute-start.75) | collective-permute-done | bytes 1048608 | tf_op jit(solution)/shard_map/ppermute | solution.py:31
  747.8 21.7 %attend_back.3 = (bf16[768,3072]{1,0:T(8,128)(2,1)}, f32[16,16,512]{2,1,0:T(8,128)}) custom-call(bf16[768,3072]{1,0:T(8,128)(2,1)} %convolution_convert_fusion.q_ref.k_ref.v_ref, bf16[768,3072]{1,0:T(8,128)(2,1)} %convolution_convert_fusion.q_ref.k_ref.v_ref, bf16[768,3072]{1,0:T(8,128)(2,1)} %convolution_convert_fusion.q_ref.k_ref.v_ref, ...), custom_call_target="tpu_custom_call" | custom-call | flops 4026531840 | bytes 17301504 | tf_op jit(solution)/shard_map/attend_back/pallas_call | solution.py:400
  824.1 10.1 %multiply_reduce_fusion = (f32[768]{0:T(1024)S(1)}, f32[1024]{0:T(1024)}, f32[768]{0:T(1024)S(1)}, f32[1024]{0:T(1024)}, f32[768,1024]{1,0:T(8,128)S(1)}) fusion(f32[768,1024]{1,0:T(8,128)S(1)} %bitcast.376, f32[768]{0:T(1024)} %add_rsqrt_fusion.1, f32[768]{0:T(1024)S(1)} %copy-done.98, f32[1024]{0:T(1024)S(1)} %bitcast.434, ...), kind=kOutput, calls=%fused_computation.44 | convolution fusion | flops 4838912000 | bytes 17326080 | tf_op jit(solution)/shard_map/dot_general | solution.py:454
  852.1 10.7 %collective-permute-done.95 = f32[96,128]{1,0:T(8,128)S(1)} collective-permute-done((f32[96,128]{1,0:T(8,128)S(1)}, f32[96,128]{1,0:T(8,128)S(1)}, u32[]{:S(2)}, u32[]{:S(2)}) %collective-permute-start.95) | collective-permute-done | bytes 49184 | tf_op jit(solution)/shard_map/ppermute | solution.py:31
  870.8 11.2 %collective-permute-done.92 = bf16[4,128,128]{2,1,0:T(8,128)(2,1)S(1)} collective-permute-done((bf16[4,128,128]{2,1,0:T(8,128)(2,1)S(1)}, bf16[4,128,128]{2,1,0:T(8,128)(2,1)S(1)}, u32[]{:S(2)}, u32[]{:S(2)}) %collective-permute-start.92) | collective-permute-done | bytes 131104 | tf_op jit(solution)/shard_map/ppermute | solution.py:31
  (788 shorter events, 606.4 us)
Async XLA Ops:
  10.1 60.4 %all-gather.11.cloned.1.call-start = ((), (), s32[]{:S(2)}) async-start(), calls=%async_computation.10 | async-start | bytes 1310720 | tf_op jit(solution)/shard_map/all_gather | solution.py:44
  12.0 98.3 %all-gather.7.cloned.1.call-start = ((), (), s32[]{:S(2)}) async-start(), calls=%async_computation.8 | async-start | bytes 1310720 | tf_op jit(solution)/shard_map/all_gather | solution.py:44
  13.9 148.5 %all-gather.13.cloned.1.call-start = ((), (), s32[]{:S(2)}) async-start(), calls=%async_computation.11 | async-start | bytes 1310720 | tf_op jit(solution)/shard_map/all_gather | solution.py:44
  14.7 215.9 %all-gather.15.cloned.1.call-start = ((), (), s32[]{:S(2)}) async-start(), calls=%async_computation.12 | async-start | bytes 1310720 | tf_op jit(solution)/shard_map/all_gather | solution.py:44
  15.6 255.9 %all-gather.17.cloned.1.call-start = ((), (), s32[]{:S(2)}) async-start(), calls=%async_computation.13 | async-start | bytes 1310720 | tf_op jit(solution)/shard_map/all_gather | solution.py:44
  19.6 885.0 %reduce-scatter.23.cloned.1.call-start = ((), (), s32[]{:S(2)}) async-start(), calls=%async_computation.21 | async-start | bytes 1310720 | tf_op jit(solution)/shard_map/reduce_scatter | solution.py:201
  164.8 39.4 %collective-permute-start.24 = (bf16[2,4,128,512]{3,2,1,0:T(8,128)(2,1)}, bf16[2,4,128,512]{3,2,1,0:T(8,128)(2,1)}, u32[]{:S(2)}, u32[]{:S(2)}) collective-permute-start(bf16[2,4,128,512]{3,2,1,0:T(8,128)(2,1)} %copy-done.63), channel_id=1, source_target_pairs={{0,8},{8,0},{16,24},{24,16},{1,9},{9,1},{17,25},{25,17},{2,10},{10... | collective-permute-start | bytes 3145736 | tf_op jit(solution)/shard_map/ppermute | solution.py:31
  164.8 39.7 %collective-permute-start.25 = (bf16[2,4,128,512]{3,2,1,0:T(8,128)(2,1)}, bf16[2,4,128,512]{3,2,1,0:T(8,128)(2,1)}, u32[]{:S(2)}, u32[]{:S(2)}) collective-permute-start(bf16[2,4,128,512]{3,2,1,0:T(8,128)(2,1)} %collective-permute-done.15.refs_5_), channel_id=1, source_target_pairs={{0,8},{8,0},{16,24},{24,16},{1,9},{9,1},{17,25},{25,17},{2,10},{10... | collective-permute-start | bytes 3145736 | tf_op jit(solution)/shard_map/ppermute | solution.py:31
  515.7 47.6 %collective-permute-start.57 = (bf16[2,4,128,512]{3,2,1,0:T(8,128)(2,1)}, bf16[2,4,128,512]{3,2,1,0:T(8,128)(2,1)}, u32[]{:S(2)}, u32[]{:S(2)}) collective-permute-start(bf16[2,4,128,512]{3,2,1,0:T(8,128)(2,1)} %get-tuple-element.536), channel_id=1, source_target_pairs={{0,1},{1,0},{2,3},{3,2},{4,5},{5,4},{6,7},{7,6},{8,9},{9,8},{10,11... | collective-permute-start | bytes 3145736 | tf_op jit(solution)/shard_map/ppermute | solution.py:31
  517.6 45.8 %collective-permute-start.56 = (bf16[2,4,128,512]{3,2,1,0:T(8,128)(2,1)}, bf16[2,4,128,512]{3,2,1,0:T(8,128)(2,1)}, u32[]{:S(2)}, u32[]{:S(2)}) collective-permute-start(bf16[2,4,128,512]{3,2,1,0:T(8,128)(2,1)} %get-tuple-element.538), channel_id=1, source_target_pairs={{0,16},{8,24},{16,0},{24,8},{1,17},{9,25},{17,1},{25,9},{2,18},{10... | collective-permute-start | bytes 3145736 | tf_op jit(solution)/shard_map/ppermute | solution.py:31
  573.3 333.0 %reduce-scatter.21.cloned.1.call-start = ((), (), s32[]{:S(2)}) async-start(), calls=%async_computation.20 | async-start | bytes 1310720 | tf_op jit(solution)/shard_map/reduce_scatter | solution.py:201
  631.9 39.7 %collective-permute-start.69 = (bf16[2,2,2,4,512,128]{5,4,3,2,1,0:T(8,128)(2,1)}, bf16[2,2,2,4,512,128]{5,4,3,2,1,0:T(8,128)(2,1)}, u32[]{:S(2)}, u32[]{:S(2)}) collective-permute-start(bf16[2,2,2,4,512,128]{5,4,3,2,1,0:T(8,128)(2,1)} %weight_grad.24), channel_id=1, source_target_pairs={{0,8},{8,0},{16,24},{24,16},{1,9},{9,1},{17,25},{25,17},{2,10},{10... | collective-permute-start | bytes 12582920 | tf_op jit(solution)/shard_map/ppermute | solution.py:31
  633.5 274.7 %reduce-scatter.19.cloned.1.call-start = ((), (), s32[]{:S(2)}) async-start(), calls=%async_computation.19 | async-start | bytes 327680 | tf_op jit(solution)/shard_map/reduce_scatter | solution.py:201
  642.3 267.3 %reduce-scatter.17.cloned.1.call-start = ((), (), s32[]{:S(2)}) async-start(), calls=%async_computation.18 | async-start | bytes 983040 | tf_op jit(solution)/shard_map/reduce_scatter | solution.py:201
  671.6 57.2 %collective-permute-start.73 = (bf16[2,2,2,4,128,512]{5,4,3,2,1,0:T(8,128)(2,1)}, bf16[2,2,2,4,128,512]{5,4,3,2,1,0:T(8,128)(2,1)}, u32[]{:S(2)}, u32[]{:S(2)}) collective-permute-start(bf16[2,2,2,4,128,512]{5,4,3,2,1,0:T(8,128)(2,1)} %weight_grad.26), channel_id=1, source_target_pairs={{0,8},{8,0},{16,24},{24,16},{1,9},{9,1},{17,25},{25,17},{2,10},{10... | collective-permute-start | bytes 12582920 | tf_op jit(solution)/shard_map/ppermute | solution.py:31
  696.9 220.7 %reduce-scatter.15.cloned.1.call-start = ((), (), s32[]{:S(2)}) async-start(), calls=%async_computation.17 | async-start | bytes 1310720 | tf_op jit(solution)/shard_map/reduce_scatter | solution.py:201
  737.7 52.7 %collective-permute-start.82 = (f32[256,128]{1,0:T(8,128)S(1)}, f32[256,128]{1,0:T(8,128)}, u32[]{:S(2)}, u32[]{:S(2)}) collective-permute-start(f32[256,128]{1,0:T(8,128)S(1)} %add.1025), channel_id=1, source_target_pairs={{0,2},{1,3},{2,0},{3,1},{4,6},{5,7},{6,4},{7,5},{8,10},{9,11},{10,... | collective-permute-start | bytes 393224 | tf_op jit(solution)/shard_map/ppermute | solution.py:31
  741.4 50.0 %collective-permute-start.81 = (bf16[4,512,128]{2,1,0:T(8,128)(2,1)}, bf16[4,512,128]{2,1,0:T(8,128)(2,1)}, u32[]{:S(2)}, u32[]{:S(2)}) collective-permute-start(bf16[4,512,128]{2,1,0:T(8,128)(2,1)} %get-tuple-element.574), channel_id=1, source_target_pairs={{0,16},{8,24},{16,0},{24,8},{1,17},{9,25},{17,1},{25,9},{2,18},{10... | collective-permute-start | bytes 1572872 | tf_op jit(solution)/shard_map/ppermute | solution.py:31
  742.3 49.2 %collective-permute-start.79 = (bf16[2,4,128,512]{3,2,1,0:T(8,128)(2,1)}, bf16[2,4,128,512]{3,2,1,0:T(8,128)(2,1)}, u32[]{:S(2)}, u32[]{:S(2)}) collective-permute-start(bf16[2,4,128,512]{3,2,1,0:T(8,128)(2,1)} %get-tuple-element.528), channel_id=1, source_target_pairs={{0,1},{1,0},{2,3},{3,2},{4,5},{5,4},{6,7},{7,6},{8,9},{9,8},{10,11... | collective-permute-start | bytes 3145736 | tf_op jit(solution)/shard_map/ppermute | solution.py:31
  743.5 47.9 %collective-permute-start.78 = (bf16[2,4,128,512]{3,2,1,0:T(8,128)(2,1)}, bf16[2,4,128,512]{3,2,1,0:T(8,128)(2,1)}, u32[]{:S(2)}, u32[]{:S(2)}) collective-permute-start(bf16[2,4,128,512]{3,2,1,0:T(8,128)(2,1)} %get-tuple-element.530), channel_id=1, source_target_pairs={{0,16},{8,24},{16,0},{24,8},{1,17},{9,25},{17,1},{25,9},{2,18},{10... | collective-permute-start | bytes 3145736 | tf_op jit(solution)/shard_map/ppermute | solution.py:31
  747.5 43.9 %collective-permute-start.80 = (bf16[4,512,128]{2,1,0:T(8,128)(2,1)}, bf16[4,512,128]{2,1,0:T(8,128)(2,1)}, u32[]{:S(2)}, u32[]{:S(2)}) collective-permute-start(bf16[4,512,128]{2,1,0:T(8,128)(2,1)} %get-tuple-element.576), channel_id=1, source_target_pairs={{0,1},{1,0},{2,3},{3,2},{4,5},{5,4},{6,7},{7,6},{8,9},{9,8},{10,11... | collective-permute-start | bytes 1572872 | tf_op jit(solution)/shard_map/ppermute | solution.py:31
  795.0 124.4 %reduce-scatter.13.cloned.1.call-start = ((), (), s32[]{:S(2)}) async-start(), calls=%async_computation.16 | async-start | bytes 1310720 | tf_op jit(solution)/shard_map/reduce_scatter | solution.py:201
  823.1 103.4 %reduce-scatter.11.cloned.1.call-start = ((), (), s32[]{:S(2)}) async-start(), calls=%async_computation.15 | async-start | bytes 327680 | tf_op jit(solution)/shard_map/reduce_scatter | solution.py:201
  887.0 45.4 %reduce-scatter.9.cloned.1.call-start = ((), (), s32[]{:S(2)}) async-start(), calls=%async_computation.14 | async-start | bytes 983040 | tf_op jit(solution)/shard_map/reduce_scatter | solution.py:201
  (237 other events, 4349.9 us)
Sparse Core Ops, SparseCore 0:
  10.2 30.6 all-gather.8
  43.0 27.4 all-gather.10
  72.1 27.4 all-gather.6
  101.0 27.4 all-gather.12
  129.8 27.4 all-gather.14
  158.7 27.4 all-gather.16
  573.5 26.5 reduce-scatter.22
  633.6 26.2 reduce-scatter.20
  662.1 18.3 reduce-scatter.18
  697.1 23.0 reduce-scatter.16
  795.1 26.2 reduce-scatter.14
  823.5 26.6 reduce-scatter.12
  887.1 19.1 reduce-scatter.10
  908.5 23.8 reduce-scatter.8

commit v2 on v1

--- a/solution.py
+++ b/solution.py
@@ -1,4 +1,5 @@
 from functools import partial
+from typing import NamedTuple
 
 import jax
 import jax.numpy as jnp
@@ -16,6 +17,8 @@
 SLOTS = 3
 VMEM_BYTES = 56 * 1024 * 1024
 
+SMALL = pl.CostEstimate(flops=1, bytes_accessed=1, transcendentals=0)
+
 epsilon = 1e-06
 masked_score = -1000000000.0
 highest = lax.Precision.HIGHEST
@@ -42,164 +45,331 @@
         self.rows = rows
         halves = shard.reshape(2, rows // 2, cols)
         grown = lax.all_gather(halves, "win", axis=1, tiled=False, axis_index_groups=z_groups())
-        self.values = (grown[0], grown[1])
-        self.stage = 0
-
-    def advance(self, values):
-        if self.stage == 0:
-            a0, b0 = values
-            new = (jnp.stack([a0, hop(a0, "y")]), jnp.stack([b0, hop(b0, "x")]))
-        elif self.stage == 1:
-            a1, b1 = values
-            new = (a1, hop(a1, "x"), hop(a1, "core"), b1, hop(b1, "y"), hop(b1, "core"))
+        self.held = {"grown": (grown,)}
+
+    def needs(self, move):
+        return {"near": "grown", "far": "near", "core_near": "own", "core_far": "away"}[move]
+
+    def go(self, move):
+        values = self.held[self.needs(move)]
+        if move == "near":
+            (grown,) = values
+            a0, b0 = grown[0], grown[1]
+            self.held["near"] = (a0, hop(a0, "y"), b0, hop(b0, "x"))
+        elif move == "far":
+            a0, a_came, b0, b_came = values
+            a1, b1 = jnp.stack([a0, a_came]), jnp.stack([b0, b_came])
+            self.held["own"] = (a1, b1)
+            self.held["away"] = (hop(a1, "x"), hop(b1, "y"))
         else:
-            a1, a2, a3, b1, b2, b3 = values
-            new = (a1, a2, a3, hop(a2, "core"), b1, b2, b3, hop(b2, "core"))
-        self.values = new
-        self.stage += 1
-
-
-def assemble_kernel(row_of, y_of, *refs, rows, widths):
+            self.held[move] = tuple(hop(value, "core") for value in values)
+
+    def values(self):
+        pairs = [self.held[name] for name in ("own", "away", "core_near", "core_far")]
+        return [pair[0] for pair in pairs] + [pair[1] for pair in pairs]
+
+
+def gathered_kernel(row_of, y_of, x_ref, *refs, rows, widths, kind):
     count = len(widths)
-    pieces = refs[:8]
-    outs = refs[8 : 8 + count]
-    whole = refs[8 + count : 8 + 2 * count]
-    in_sems, out_sems = refs[8 + 2 * count :]
+    results = 2 if kind == "gelu" else 1
+    pieces, refs = refs[:8], refs[8:]
+    outs, wholes, held = refs[:results], refs[results : results + count], refs[results + count : -2]
+    in_sems, out_sems = refs[-2:]
     half = rows // 2
-    bands = []
-    for part in range(2):
-        for c_rel in range(2):
-            for x_rel in range(2):
-                block = row_of[c_rel * 2 + x_rel]
-                row = pl.multiple_of(block * rows + part * half, half)
-                copies = []
-                for y_rel in range(2):
-                    far, near = (x_rel, y_rel) if part == 0 else (y_rel, x_rel)
-                    source = pieces[part * 4 + c_rel * 2 + far]
-                    for z in range(4):
-                        place = z * 2 + y_of[y_rel]
+    step = pl.program_id(0)
+
+    def arrivals(z):
+        copies = []
+        for part in range(2):
+            for c_rel in range(2):
+                for x_rel in range(2):
+                    row = row_of[c_rel * 2 + x_rel] * rows + part * half
+                    row = pl.multiple_of(row, half)
+                    for y_rel in range(2):
+                        far, near = (x_rel, y_rel) if part == 0 else (y_rel, x_rel)
+                        source = pieces[part * 4 + c_rel * 2 + far]
                         start = 0
-                        for held, width in zip(whole, widths):
-                            col = pl.multiple_of(place * width, 128)
+                        for matrix, width in zip(held, widths):
+                            col = pl.multiple_of((z * 2 + y_of[y_rel]) * width, 128)
                             copies.append(
                                 pltpu.make_async_copy(
                                     source.at[near, z, :, pl.ds(start, width)],
-                                    held.at[pl.ds(row, half), pl.ds(col, width)],
-                                    in_sems.at[len(bands) * 8 * count + len(copies)],
+                                    matrix.at[pl.ds(row, half), pl.ds(col, width)],
+                                    in_sems.at[z * 16 * count + len(copies)],
                                 )
                             )
                             start += width
-                bands.append((row, copies))
-    for row, copies in bands:
-        for copy in copies:
-            copy.start()
-    sent = []
-    for band, (row, copies) in enumerate(bands):
-        for copy in copies:
-            copy.wait()
-        for which, (held, out) in enumerate(zip(whole, outs)):
-            there = pl.ds(row, half)
-            sent.append(
-                pltpu.make_async_copy(held.at[there], out.at[there], out_sems.at[band * count + which])
+        return copies
+
+    def departures(z):
+        copies = []
+        for which, width in enumerate(widths):
+            there = pl.ds(pl.multiple_of(z * 2 * width, 128), 2 * width)
+            copies.append(
+                pltpu.make_async_copy(
+                    held[which].at[:, there], wholes[which].at[:, there], out_sems.at[z * count + which]
+                )
             )
-            sent[-1].start()
-    for copy in sent:
+        return copies
+
+    @pl.when(step == 0)
+    def begin():
+        for z in range(4):
+            for copy in arrivals(z):
+                copy.start()
+
+    for copy in arrivals(step):
         copy.wait()
-
-
-def assemble(values, place, rows, widths):
+    for copy in departures(step):
+        copy.start()
+    wide = 2 * widths[0]
+    chunk = 256 if kind == "gelu" else wide
+    for first in range(0, wide, chunk):
+        col = pl.multiple_of(step * wide + first, 128)
+        there = slice(first, first + chunk)
+        result = jnp.dot(
+            x_ref[...], held[0][:, pl.ds(col, chunk)], preferred_element_type=jnp.float32
+        )
+        if kind == "gelu":
+            outs[0][:, there], outs[1][:, there] = gelu_both(result)
+        else:
+            outs[0][:, there] = result.astype(outs[0].dtype)
+
+    @pl.when(step == 3)
+    def end():
+        for z in range(4):
+            for copy in departures(z):
+                copy.wait()
+
+
+def gathered(values, place, x, rows, widths, kind):
     shapes = [(4 * rows, 8 * width) for width in widths]
+    results = 2 if kind == "gelu" else 1
+    kept = jnp.float32 if kind == "wide" else jnp.bfloat16
+    count = x.shape[0]
     return pl.pallas_call(
-        partial(assemble_kernel, rows=rows, widths=widths),
-        out_shape=[jax.ShapeDtypeStruct(shape, jnp.bfloat16) for shape in shapes],
-        in_specs=[pl.BlockSpec(memory_space=pltpu.SMEM)] * 2 + [pl.BlockSpec(memory_space=pl.ANY)] * 8,
-        out_specs=[pl.BlockSpec(memory_space=pl.ANY)] * len(widths),
+        partial(gathered_kernel, rows=rows, widths=widths, kind=kind),
+        grid=(4,),
+        out_shape=[jax.ShapeDtypeStruct((count, 8 * widths[0]), kept)] * results
+        + [jax.ShapeDtypeStruct(shape, jnp.bfloat16) for shape in shapes],
+        in_specs=[pl.BlockSpec(memory_space=pltpu.SMEM)] * 2
+        + [pl.BlockSpec(x.shape, lambda z: (0, 0))]
+        + [pl.BlockSpec(memory_space=pl.ANY)] * 8,
+        out_specs=[pl.BlockSpec((count, 2 * widths[0]), lambda z: (0, z))] * results
+        + [pl.BlockSpec(memory_space=pl.ANY)] * len(widths),
         scratch_shapes=[pltpu.VMEM(shape, jnp.bfloat16) for shape in shapes]
-        + [pltpu.SemaphoreType.DMA((64 * len(widths),)), pltpu.SemaphoreType.DMA((8 * len(widths),))],
+        + [pltpu.SemaphoreType.DMA((64 * len(widths),)), pltpu.SemaphoreType.DMA((4 * len(widths),))],
         compiler_params=pltpu.CompilerParams(vmem_limit_bytes=VMEM_BYTES),
-        cost_estimate=pl.CostEstimate(
-            flops=0, bytes_accessed=4 * sum(a * b for a, b in shapes), transcendentals=0
-        ),
-        name="assemble",
-    )(place["rows"], place["cols"], *values)
-
-
-def grad_kernel(row_of, y_of, x_ref, *refs, part, rows, widths):
-    dy_refs = refs[: len(widths)]
-    out_ref, turned = refs[len(widths) :]
+        cost_estimate=SMALL,
+        name="gathered",
+    )(place["rows"], place["cols"], x, *values)
+
+
+def product_kernel(left, right, out, *, turned):
+    if turned:
+        result = lax.dot_general(left[...], right[...], NT, preferred_element_type=jnp.float32)
+    else:
+        result = jnp.dot(left[...], right[...], preferred_element_type=jnp.float32)
+    out[...] = result.astype(out.dtype)
+
+
+def scaled_kernel(left, right, factor, out):
+    result = lax.dot_general(left[...], right[...], NT, preferred_element_type=jnp.float32)
+    out[...] = (result * factor[...].astype(jnp.float32)).astype(out.dtype)
+
+
+def tiled(kernel, left, right, columns, kept, turned, *factors):
+    count = left.shape[0]
+    total = right.shape[0] if turned else right.shape[1]
+    block = pl.BlockSpec((count, columns), lambda i: (0, i))
+    if turned:
+        right_spec = pl.BlockSpec((columns, right.shape[1]), lambda i: (i, 0))
+    else:
+        right_spec = pl.BlockSpec((right.shape[0], columns), lambda i: (0, i))
+    return pl.pallas_call(
+        kernel,
+        grid=(total // columns,),
+        out_shape=jax.ShapeDtypeStruct((count, total), kept),
+        in_specs=[pl.BlockSpec(left.shape, lambda i: (0, 0)), right_spec] + [block] * len(factors),
+        out_specs=block,
+        compiler_params=pltpu.CompilerParams(vmem_limit_bytes=VMEM_BYTES),
+        cost_estimate=SMALL,
+        name="product",
+    )(left, right, *factors)
+
+
+def product(left, right):
+    return tiled(partial(product_kernel, turned=False), left, right, 512, jnp.float32, False)
+
+
+def product_turned(left, right, kept=jnp.float32):
+    columns = 512 if right.shape[1] == 1024 else 256
+    return tiled(partial(product_kernel, turned=True), left, right, columns, kept, True)
+
+
+def product_scaled(left, right, factor):
+    return tiled(scaled_kernel, left, right, 1024, jnp.bfloat16, True, factor)
+
+
+def grad_kernel(row_of, y_of, *refs, rows, widths, sources, kinds):
+    count = len(widths)
+    lefts = max(sources) + 1
+    refs = list(refs)
+    x_refs = [refs.pop(0) for _ in range(lefts)]
+    dy_refs = [refs.pop(0) for _ in range(count)]
+    old_refs = [[refs.pop(0) for _ in range(FOLDS[kind].takes)] for kind in kinds]
+    send, keep = refs.pop(0), refs.pop(0)
+    new_refs = [[refs.pop(0) for _ in range(FOLDS[kind].gives)] for kind in kinds]
+    turns = refs
     half = rows // 2
-    total = sum(widths)
 
     @pl.when(pl.program_id(0) == 0)
     def turn():
-        for x_rel in range(2):
-            start = pl.multiple_of(row_of[part * 2 + x_rel] * rows, rows)
-            turned[x_rel * rows : (x_rel + 1) * rows, :] = x_ref[:, pl.ds(start, rows)].T
+        for x_ref, turned in zip(x_refs, turns):
+            for place in range(4):
+                start = pl.multiple_of(row_of[place] * rows, 128)
+                turned[place * rows : (place + 1) * rows, :] = x_ref[:, pl.ds(start, rows)].T
 
     offset = 0
-    for dy_ref, width in zip(dy_refs, widths):
-        product = jnp.dot(turned[...], dy_ref[...], preferred_element_type=jnp.float32)
-        for y in range(2):
+    for dy_ref, width, source in zip(dy_refs, widths, sources):
+        turned = turns[source]
+        sides = [
+            dy_ref[:, pl.ds(pl.multiple_of(y_of[y_rel] * width, 128), width)] for y_rel in range(2)
+        ]
+        product = jnp.dot(
+            turned[...], jnp.concatenate(sides, axis=1), preferred_element_type=jnp.float32
+        ).astype(jnp.bfloat16)
+        for c_rel, out in ((0, keep), (1, send)):
             for x_rel in range(2):
                 for ab in range(2):
-                    first = x_rel * rows + ab * half
-                    out_ref[ab, x_rel, y_of[y], 0, :, offset : offset + width] = product[
-                        first : first + half, y * width : (y + 1) * width
-                    ].astype(jnp.bfloat16)
+                    first = (c_rel * 2 + x_rel) * rows + ab * half
+                    for y_rel in range(2):
+                        out[ab, x_rel, y_rel, 0, :, offset : offset + width] = product[
+                            first : first + half, y_rel * width : (y_rel + 1) * width
+                        ]
         offset += width
-
-
-def weight_grad(x, dys, place, part, rows, widths, starts):
-    count = x.shape[0]
-    total = sum(widths)
-    return pl.pallas_call(
-        partial(grad_kernel, part=part, rows=rows, widths=widths),
+    for kind, old, new in zip(kinds, old_refs, new_refs):
+        FOLDS[kind].kernel(*old, *new)
+
+
+def fold_first(old_keep, old_came, a_send, a_keep, b_send, b_keep):
+    for near in range(2):
+        a_send[near] = old_keep[0, 1, near] + old_came[0, 1, near]
+        a_keep[near] = old_keep[0, 0, near] + old_came[0, 0, near]
+        b_send[near] = old_keep[1, near, 1] + old_came[1, near, 1]
+        b_keep[near] = old_keep[1, near, 0] + old_came[1, near, 0]
+
+
+def fold_second(a_keep, a_came, b_keep, b_came, a_out, a_held, b_out, b_held):
+    a_out[...] = a_keep[1] + a_came[1]
+    a_held[...] = a_keep[0] + a_came[0]
+    b_out[...] = b_keep[1] + b_came[1]
+    b_held[...] = b_keep[0] + b_came[0]
+
+
+def fold_third(a_keep, a_came, b_keep, b_came, both):
+    both[:, 0] = a_keep[...] + a_came[...]
+    both[:, 1] = b_keep[...] + b_came[...]
+
+
+class Part(NamedTuple):
+    lead: tuple
+
+    def shape(self, tail):
+        return jax.ShapeDtypeStruct(self.lead + tail, jnp.bfloat16)
+
+    def spec(self, tail):
+        where = self.lead.index(4)
+        block = tuple(1 if dim == where else size for dim, size in enumerate(self.lead))
+        return pl.BlockSpec(
+            block + tail, lambda z: (0,) * where + (z,) + (0,) * (len(block) + 1 - where)
+        )
+
+
+WHOLE, QUARTER, EIGHTH, TURNED = Part((2, 2, 2, 4)), Part((2, 4)), Part((4,)), Part((4, 2))
+
+
+class Fold(NamedTuple):
+    kernel: object
+    takes: int
+    takes_part: Part
+    gives: int
+    gives_part: Part
+
+
+FOLDS = {
+    1: Fold(fold_first, 2, WHOLE, 4, QUARTER),
+    2: Fold(fold_second, 4, QUARTER, 4, EIGHTH),
+    3: Fold(fold_third, 4, EIGHTH, 1, TURNED),
+}
+
+
+def weight_grad(xs, dys, place, rows, widths, starts, sources, olders):
+    count = xs[0].shape[0]
+    tail = (rows // 2, sum(widths))
+    kinds = tuple(older.stage for older in olders)
+    out_shape, out_specs = [WHOLE.shape(tail)] * 2, [WHOLE.spec(tail)] * 2
+    old_specs, old_values = [], []
+    for older, kind in zip(olders, kinds):
+        fold = FOLDS[kind]
+        old_tail = older.values[0].shape[-2:]
+        old_specs += [fold.takes_part.spec(old_tail)] * fold.takes
+        old_values += older.values
+        out_shape += [fold.gives_part.shape(old_tail)] * fold.gives
+        out_specs += [fold.gives_part.spec(old_tail)] * fold.gives
+    outs = pl.pallas_call(
+        partial(grad_kernel, rows=rows, widths=widths, sources=sources, kinds=kinds),
         grid=(4,),
-        out_shape=jax.ShapeDtypeStruct((2, 2, 2, 4, rows // 2, total), jnp.bfloat16),
+        out_shape=out_shape,
         in_specs=[pl.BlockSpec(memory_space=pltpu.SMEM)] * 2
-        + [pl.BlockSpec((count, 4 * rows), lambda z: (0, 0))]
+        + [pl.BlockSpec((count, 4 * rows), lambda z: (0, 0))] * len(xs)
         + [
             pl.BlockSpec((count, 2 * width), lambda z, s=start: (0, s + z))
             for width, start in zip(widths, starts)
-        ],
-        out_specs=pl.BlockSpec((2, 2, 2, 1, rows // 2, total), lambda z: (0, 0, 0, z, 0, 0)),
-        scratch_shapes=[pltpu.VMEM((2 * rows, count), jnp.bfloat16)],
+        ]
+        + old_specs,
+        out_specs=out_specs,
+        scratch_shapes=[pltpu.VMEM((4 * rows, count), jnp.bfloat16)] * len(xs),
         compiler_params=pltpu.CompilerParams(vmem_limit_bytes=VMEM_BYTES),
-        cost_estimate=pl.CostEstimate(
-            flops=2 * count * 2 * rows * 8 * total,
-            bytes_accessed=2 * count * (4 * rows + 8 * total) + 32 * rows * total,
-            transcendentals=0,
-        ),
+        cost_estimate=SMALL,
         name="weight_grad",
-    )(place["rows"], place["cols"], x, *dys)
+    )(place["rows"], place["cols"], *xs, *dys, *old_values)
+    outs = list(outs)
+    values = tuple(outs.pop(0) for _ in range(2))
+    for older, kind in zip(olders, kinds):
+        older.values = tuple(outs.pop(0) for _ in range(FOLDS[kind].gives))
+    return values
 
 
 class Scatter:
-    def __init__(self, values):
-        self.values = values
+    def __init__(self, xs, dys, place, rows, widths, starts, sources, olders):
+        self.values = weight_grad(xs, dys, place, rows, widths, starts, sources, olders)
         self.stage = 0
+
+    def fold(self):
+        fold = FOLDS[self.stage]
+        outs = pl.pallas_call(
+            fold.kernel,
+            out_shape=[fold.gives_part.shape(self.values[0].shape[-2:])] * fold.gives,
+            compiler_params=pltpu.CompilerParams(vmem_limit_bytes=VMEM_BYTES),
+            cost_estimate=SMALL,
+            name=fold.kernel.__name__,
+        )(*self.values)
+        self.values = tuple(outs)
 
     def advance(self, values):
         if self.stage == 0:
             send, keep = values
             new = (keep, hop(send, "core"))
         elif self.stage == 1:
-            keep, came = values
-            a_send = keep[0, 1] + came[0, 1]
-            b_send = keep[1, :, 1] + came[1, :, 1]
-            a_keep = keep[0, 0] + came[0, 0]
-            b_keep = keep[1, :, 0] + came[1, :, 0]
+            a_send, a_keep, b_send, b_keep = values
             new = (a_keep, hop(a_send, "x"), b_keep, hop(b_send, "y"))
         elif self.stage == 2:
-            a_keep, a_came, b_keep, b_came = values
-            a_send = a_keep[1] + a_came[1]
-            b_send = b_keep[1] + b_came[1]
-            new = (a_keep[0] + a_came[0], hop(a_send, "y"), b_keep[0] + b_came[0], hop(b_send, "x"))
+            a_send, a_keep, b_send, b_keep = values
+            new = (a_keep, hop(a_send, "y"), b_keep, hop(b_send, "x"))
         else:
-            a_keep, a_came, b_keep, b_came = values
-            both = jnp.stack([a_keep + a_came, b_keep + b_came], axis=1)
             mine = lax.psum_scatter(
-                both.reshape(-1, both.shape[-1]),
+                values[0].reshape(-1, values[0].shape[-1]),
                 "win",
                 scatter_dimension=0,
                 tiled=True,
@@ -275,12 +445,16 @@
 
 
 def joint_strip_back(strip):
-    frames = 2 * FR - 1
-    places = HS * HS
-    shaped = strip[:, :, : frames * places].reshape(HEADS, places, frames, places).transpose(0, 2, 1, 3)
-    flat = shaped.reshape(HEADS * frames, places * places)
-    grad = lax.dot_general(flat, joint_onehot(), NT, precision=highest)
-    return grad.reshape(HEADS, frames, 2 * HS - 1, 2 * HS - 1)
+    frames, span, lanes = 2 * FR - 1, 2 * HS - 1, 2 * HS * HS
+    shaped = strip.reshape(HEADS, HS, frames, lanes).transpose(0, 2, 1, 3)
+    table_dims = (span * span, HS * lanes)
+    offset = lax.broadcasted_iota(jnp.int32, table_dims, 0)
+    pair = lax.broadcasted_iota(jnp.int32, table_dims, 1)
+    wanted = pair // HS % (2 * HS) * span + pair % HS - pair // lanes + HS - 1
+    onehot = ((offset == wanted) & (pair // HS % (2 * HS) < span)).astype(jnp.float32)
+    flat = shaped.reshape(HEADS * frames, HS * lanes)
+    grad = lax.dot_general(flat, onehot, NT, precision=highest)
+    return grad.reshape(HEADS, frames, span, span)
 
 
 def head_lanes(which):
@@ -340,17 +514,14 @@
         ],
         scratch_shapes=[pltpu.VMEM((length, length), jnp.float32)],
         compiler_params=pltpu.CompilerParams(vmem_limit_bytes=VMEM_BYTES),
-        cost_estimate=pl.CostEstimate(
-            flops=8 * HEADS * wins * length * length * 64,
-            bytes_accessed=8 * count * width + 2 * HEADS * wins * length * length,
-            transcendentals=HEADS * wins * length * length,
-        ),
+        cost_estimate=SMALL,
         name="attend",
     )(qkv, qkv, qkv, strip, allowed)
 
 
-def attend_back_kernel(q_ref, k_ref, v_ref, g_ref, probs_ref, out_ref, strip_ref, total, *, wins, length):
-    rows, lanes = strip_ref.shape[1:]
+def attend_back_kernel(
+    q_ref, k_ref, v_ref, g_ref, probs_ref, out_ref, strip_ref, total, *, wins, length, rows
+):
     blocks = length // rows
     width = out_ref.shape[1] // 3
     step = pl.program_id(0)
@@ -391,18 +562,30 @@
             offset = (blocks - 1 - block) * rows
             piece = total[block * rows : (block + 1) * rows, :]
             strip = strip + (piece if offset == 0 else pltpu.roll(piece, offset, 1))
-        strip_ref[head] = strip
-
-
-def attend_back(qkv, probs, grad_out, wins, length, rows, lanes):
+        if strip_ref.shape[1] == rows:
+            strip_ref[head] = strip
+            continue
+        lane = lax.broadcasted_iota(jnp.int32, (1, 128), 1)
+        for offset in range(strip_ref.shape[2] // 128):
+            odd = offset % 2
+            there = slice(offset // 2 * 128, offset // 2 * 128 + 128)
+            summed = None
+            for row in range(HS):
+                piece = jnp.where(lane // 64 == odd, strip[row * HS : (row + 1) * HS, there], 0.0)
+                shift = (64 * odd + (HS - 1 - row) * HS) % 128
+                piece = piece if shift == 0 else pltpu.roll(piece, shift, 1)
+                summed = piece if summed is None else summed + piece
+            strip_ref[head, :, offset * 128 : (offset + 1) * 128] = summed
+
+
+def attend_back(qkv, probs, grad_out, wins, length, rows, lanes, strip):
     count, triple = qkv.shape
-    width = triple // 3
     return pl.pallas_call(
-        partial(attend_back_kernel, wins=wins, length=length),
+        partial(attend_back_kernel, wins=wins, length=length, rows=rows),
         grid=(HEADS // 2,),
         out_shape=[
             jax.ShapeDtypeStruct((count, triple), jnp.bfloat16),
-            jax.ShapeDtypeStruct((HEADS, rows, lanes), jnp.float32),
+            jax.ShapeDtypeStruct((HEADS,) + strip, jnp.float32),
         ],
         in_specs=[
             pl.BlockSpec((count, 128), lambda h: (0, h)),
@@ -413,15 +596,11 @@
         ],
         out_specs=[
             pl.BlockSpec((count, triple), lambda h: (0, 0)),
-            pl.BlockSpec((2, rows, lanes), lambda h: (h, 0, 0)),
+            pl.BlockSpec((2,) + strip, lambda h: (h, 0, 0)),
         ],
         scratch_shapes=[pltpu.VMEM((length, lanes), jnp.float32)],
         compiler_params=pltpu.CompilerParams(vmem_limit_bytes=VMEM_BYTES),
-        cost_estimate=pl.CostEstimate(
-            flops=20 * HEADS * wins * length * length * 64,
-            bytes_accessed=14 * count * width + 2 * HEADS * wins * length * length,
-            transcendentals=0,
-        ),
+        cost_estimate=SMALL,
         name="attend_back",
     )(qkv, qkv, qkv, grad_out, probs)
 
@@ -444,14 +623,6 @@
     mean_two = jnp.mean(inner * unit, axis=-1, keepdims=True)
     grad = scale * (inner - mean_one - unit * mean_two)
     return grad, jnp.sum(grad_in, axis=0), jnp.sum(grad_in * unit, axis=0)
-
-
-def product(left, right):
-    return jnp.dot(left, right, preferred_element_type=jnp.float32)
-
-
-def product_turned(left, right):
-    return lax.dot_general(left, right, NT, preferred_element_type=jnp.float32)
 
 
 def gelu_both(upward):
@@ -548,16 +719,28 @@
                 (self.full[7],),
             ]
 
-    def round(self, active, state):
+    def go(self, moves, state, after=()):
         if not self.quick:
             return state
-        return together([self.jobs[unit] for unit in active], state)
-
-    def take(self, unit):
-        if not self.quick:
-            return self.full[unit]
-        job = self.jobs[unit]
-        return assemble(job.values, self.place, job.rows, self.widths[unit])
+        jobs = [(self.jobs[unit], move) for unit, move in moves]
+        known = [(job, job.needs(move)) for job, move in jobs if job.needs(move) in job.held]
+        known += [(self.jobs[unit], name) for unit, name in after]
+        held, state = lax.optimization_barrier(([job.held[name] for job, name in known], state))
+        for (job, name), values in zip(known, held):
+            job.held[name] = values
+        for job, move in jobs:
+            job.go(move)
+        return state
+
+    def apply(self, unit, x, kind):
+        if self.quick:
+            job = self.jobs[unit]
+            return gathered(job.values(), self.place, x, job.rows, self.widths[unit], kind)
+        wholes = self.full[unit]
+        result = jnp.dot(x, wholes[0], preferred_element_type=jnp.float32)
+        if kind == "gelu":
+            return *gelu_both(result), *wholes
+        return result if kind == "wide" else result.astype(jnp.bfloat16), *wholes
 
 
 def body(
@@ -614,124 +797,174 @@
 
     half_tokens = tokens.reshape(pair_windows, half_len, model_width)
     win_input = enter_windows(half_tokens, own_half, pair_windows).astype(jnp.float32)
+    attn_in_a = modulated_norm(win_input, mod[0], mod[1])
+
+    go = weights.go
+    state = go([(0, "near")], (win_input, attn_in_a, sp_table))
+    win_input, attn_in_a, sp_table = go([(0, "far"), (0, "core_near")], state)
     sp_strip = spatial_strip(sp_table)
-    st_strip = joint_strip(st_table)
-    attn_in_a = modulated_norm(win_input, mod[0], mod[1])
-
-    state = (win_input, attn_in_a)
-    state = weights.round([0], state)
-    state = weights.round([0], state)
-    state = weights.round([0, 1], state)
-    win_input, attn_in_a = weights.round([1], state)
-    w_qkv_a, w_out_a = weights.take(0)
-    qkv_a = product(attn_in_a, w_qkv_a).astype(jnp.bfloat16)
-    win_input, qkv_a, w_out_a = weights.round([2], (win_input, qkv_a, w_out_a))
+    state = go([(1, "near")], (win_input, attn_in_a, sp_strip, sp_allowed))
+    win_input, attn_in_a, sp_strip, sp_allowed = go([(0, "core_far")], state)
+    qkv_a, w_qkv_a, w_out_a = weights.apply(0, attn_in_a, "narrow")
+    win_input, qkv_a, w_out_a = go([(1, "far")], (win_input, qkv_a, w_out_a))
+    win_input, qkv_a, w_out_a = go([(2, "near")], (win_input, qkv_a, w_out_a))
     attn_out_a, probs_a = attend(qkv_a, sp_strip, sp_allowed, SLOTS, WS * WS)
-    win_input, attn_out_a, w_out_a = weights.round([1], (win_input, attn_out_a, w_out_a))
+    win_input, attn_out_a, w_out_a = go([(1, "core_near")], (win_input, attn_out_a, w_out_a))
     mixed_a = product(attn_out_a, w_out_a)
     win_middle = win_input + mod[2] * mixed_a
-    middle_a = joint_group(leave_windows(win_middle, own_half, pair_windows))
+    keep_part, send_part = split_windows(win_middle, own_half)
+    send_part = send_part.astype(jnp.bfloat16)
+    keep_part, send_part, st_table = go([(1, "core_far")], (keep_part, send_part, st_table))
+    came_part = from_pair(send_part)
+    keep_part, st_table = go([(2, "far")], (keep_part, st_table))
+    st_strip = joint_strip(st_table)
+    keep_part, came_part, st_strip, st_allowed = lax.optimization_barrier(
+        (keep_part, came_part, st_strip, st_allowed)
+    )
+    middle_a = joint_group(join_halves(keep_part, came_part.astype(jnp.float32), own_half, pair_windows))
     mlp_in_a = modulated_norm(middle_a, mod[3], mod[4])
 
-    middle_a, mlp_in_a = weights.round([2, 3], (middle_a, mlp_in_a))
-    (w_up_a,) = weights.take(1)
-    hidden_a, slope_a = gelu_both(product(mlp_in_a, w_up_a))
-    middle_a, hidden_a, slope_a = weights.round([2], (middle_a, hidden_a, slope_a))
-
-    middle_a, hidden_a = weights.round([3, 4], (middle_a, hidden_a))
-    (w_down_a,) = weights.take(2)
-    downward_a = product(hidden_a, w_down_a)
+    middle_a, mlp_in_a = go([(3, "near")], (middle_a, mlp_in_a))
+    hidden_a, slope_a, w_up_a = weights.apply(1, mlp_in_a, "gelu")
+    middle_a, hidden_a, slope_a = go([(2, "core_near"), (2, "core_far")], (middle_a, hidden_a, slope_a))
+    middle_a, hidden_a, slope_a = go([(4, "near")], (middle_a, hidden_a, slope_a))
+    downward_a, w_down_a = weights.apply(2, hidden_a, "wide")
+    middle_a, downward_a = go([(3, "far")], (middle_a, downward_a))
+    middle_a, downward_a = go([(3, "core_near")], (middle_a, downward_a))
     first_out = middle_a + mod[5] * downward_a
     attn_in_b = modulated_norm(first_out, mod[6], mod[7])
-    first_out, attn_in_b = weights.round([3], (first_out, attn_in_b))
-
-    first_out, attn_in_b = weights.round([4, 5], (first_out, attn_in_b))
-    w_qkv_b, w_out_b = weights.take(3)
-    qkv_b = product(attn_in_b, w_qkv_b).astype(jnp.bfloat16)
-    first_out, qkv_b, w_out_b = weights.round([4], (first_out, qkv_b, w_out_b))
+
+    first_out, attn_in_b = go([(3, "core_far")], (first_out, attn_in_b))
+    first_out, attn_in_b = go([(4, "far")], (first_out, attn_in_b))
+    qkv_b, w_qkv_b, w_out_b = weights.apply(3, attn_in_b, "narrow")
+    first_out, qkv_b, w_out_b = go([(5, "near"), (4, "core_near")], (first_out, qkv_b, w_out_b))
     attn_out_b, probs_b = attend(qkv_b, st_strip, st_allowed, 2, joint_len)
+    first_out, attn_out_b, w_out_b = go([(4, "core_far")], (first_out, attn_out_b, w_out_b))
+    first_out, attn_out_b, w_out_b = go([(5, "far")], (first_out, attn_out_b, w_out_b))
     mixed_b = product(attn_out_b, w_out_b)
     middle_b = first_out + mod[8] * mixed_b
     mlp_in_b = modulated_norm(middle_b, mod[9], mod[10])
-
-    middle_b, mlp_in_b = weights.round([5], (middle_b, mlp_in_b))
-    (w_up_b,) = weights.take(4)
-    hidden_b, slope_b = gelu_both(product(mlp_in_b, w_up_b))
-    middle_b, hidden_b, slope_b = weights.round([5], (middle_b, hidden_b, slope_b))
-    (w_down_b,) = weights.take(5)
-    downward_b = product(hidden_b, w_down_b)
-    out_rows = middle_b + mod[11] * downward_b
-    out_tokens = joint_ungroup(out_rows).reshape(tokens.shape)
-
-    def start_grad(x, dys, rows, widths, starts):
+    hidden_b, slope_b, w_up_b = weights.apply(4, mlp_in_b, "gelu")
+    middle_b, hidden_b, slope_b = go([(5, "core_near"), (5, "core_far")], (middle_b, hidden_b, slope_b))
+
+    def start_grad(xs, dys, rows, widths, starts, sources, olders=()):
         if quick:
-            return Scatter(
-                tuple(weight_grad(x, dys, place, part, rows, widths, starts) for part in (1, 0))
-            )
-        return Plain(x, dys, widths, starts)
+            return Scatter(xs, dys, place, rows, widths, starts, sources, olders)
+        return Plain(xs, dys, widths, starts, sources)
 
     def rounds(jobs, state):
         if quick:
             return together(jobs, state)
         return state
 
+    def hold(jobs, state):
+        if not quick:
+            return state
+        state, held = lax.optimization_barrier((state, [job.values for job in jobs]))
+        for job, values in zip(jobs, held):
+            job.values = values
+        return state
+
+    def settle(jobs, state):
+        state = hold(jobs, state)
+        if quick:
+            for job in jobs:
+                job.fold()
+        return state
+
     grad_out_b = joint_group(grad_output.reshape(-1, model_width)).astype(jnp.float32)
     grad_down_b = (mod[11] * grad_out_b).astype(jnp.bfloat16)
+    d_st_down = start_grad([hidden_b], [grad_down_b], 1024, (128,), (0,), (0,))
+    grad_down_b, hidden_b = rounds([d_st_down], (grad_down_b, hidden_b))
+    downward_b, w_down_b = weights.apply(5, hidden_b, "wide")
+    grad_up_b = product_scaled(grad_down_b, w_down_b, slope_b)
+    d_st_up = start_grad([mlp_in_b], [grad_up_b], 256, (512,), (0,), (0,), [d_st_down])
+    grad_up_b, downward_b = rounds([d_st_up, d_st_down], (grad_up_b, downward_b))
+    out_rows = middle_b + mod[11] * downward_b
+    out_tokens = joint_ungroup(out_rows).reshape(tokens.shape)
     grad_gate_mb = jnp.sum(grad_out_b * downward_b, axis=0)
-    d_st_down = start_grad(hidden_b, [grad_down_b], 1024, (128,), (0,))
-    grad_down_b = rounds([d_st_down], grad_down_b)
-    grad_up_b = (product_turned(grad_down_b, w_down_b) * slope_b).astype(jnp.bfloat16)
-    grad_up_b = rounds([d_st_down], grad_up_b)
-    d_st_up = start_grad(mlp_in_b, [grad_up_b], 256, (512,), (0,))
-    grad_up_b = rounds([d_st_up, d_st_down], grad_up_b)
     grad_mlp_b = product_turned(grad_up_b, w_up_b)
     norm_grad, grad_shift_mb, grad_scale_mb = norm_back(grad_mlp_b, middle_b, mod[10])
     grad_middle_b = grad_out_b + norm_grad
     grad_mixed_b = (mod[8] * grad_middle_b).astype(jnp.bfloat16)
     grad_gate_ab = jnp.sum(grad_middle_b * mixed_b, axis=0)
-    grad_middle_b, grad_mixed_b = rounds([d_st_up, d_st_down], (grad_middle_b, grad_mixed_b))
-    d_st_out = start_grad(attn_out_b, [grad_mixed_b], 256, (128,), (0,))
-    grad_attn_b = product_turned(grad_mixed_b, w_out_b).astype(jnp.bfloat16)
+    state = (grad_middle_b, grad_mixed_b)
+    state = settle([d_st_up, d_st_down], state)
+    grad_middle_b, grad_mixed_b = rounds([d_st_up, d_st_down], state)
+    grad_attn_b = product_turned(grad_mixed_b, w_out_b, jnp.bfloat16)
     grad_qkv_b, strip_grad_b = attend_back(
-        qkv_b, probs_b, grad_attn_b, 2, joint_len, st_strip.shape[1], st_strip.shape[2]
+        qkv_b, probs_b, grad_attn_b, 2, joint_len, *st_strip.shape[1:], (HS, 128 * (2 * FR - 1))
     )
-    grad_middle_b, grad_qkv_b = rounds([d_st_out, d_st_up], (grad_middle_b, grad_qkv_b))
-    st_total = Total(joint_strip_back(strip_grad_b), ("x", "core", "y", "z0", "z1"))
-    d_st_qkv = start_grad(attn_in_b, [grad_qkv_b, grad_qkv_b], 256, (256, 128), (0, 8))
-    grad_middle_b, grad_qkv_b = rounds(
-        [d_st_qkv, d_st_out, d_st_up], (grad_middle_b, grad_qkv_b)
+    grad_middle_b, grad_qkv_b, strip_grad_b = hold(
+        [d_st_down], (grad_middle_b, grad_qkv_b, strip_grad_b)
     )
+    d_st_attn = start_grad(
+        [attn_in_b, attn_out_b],
+        [grad_qkv_b, grad_qkv_b, grad_mixed_b],
+        256,
+        (256, 128, 128),
+        (0, 8, 0),
+        (0, 0, 1),
+        [d_st_down],
+    )
+    state = hold([d_st_attn], (grad_middle_b, grad_qkv_b, strip_grad_b))
+    state = settle([d_st_up], state)
+    grad_middle_b, grad_qkv_b, strip_grad_b = rounds([d_st_attn, d_st_up, d_st_down], state)
     grad_in_b = product_turned(grad_qkv_b, w_qkv_b)
     norm_grad, grad_shift_ab, grad_scale_ab = norm_back(grad_in_b, first_out, mod[7])
     grad_first = grad_middle_b + norm_grad
     grad_down_a = (mod[5] * grad_first).astype(jnp.bfloat16)
     grad_gate_ma = jnp.sum(grad_first * downward_a, axis=0)
-    grad_first, grad_down_a = rounds([d_st_qkv, d_st_out, st_total], (grad_first, grad_down_a))
-
-    d_sp_down = start_grad(hidden_a, [grad_down_a], 1024, (128,), (0,))
-    grad_first, grad_down_a = rounds(
-        [d_sp_down, d_st_qkv, d_st_out, st_total], (grad_first, grad_down_a)
+    grad_first, grad_down_a = hold([d_st_attn, d_st_up], (grad_first, grad_down_a))
+    d_sp_down = start_grad(
+        [hidden_a], [grad_down_a], 1024, (128,), (0,), (0,), [d_st_attn, d_st_up]
     )
-    grad_up_a = (product_turned(grad_down_a, w_down_a) * slope_a).astype(jnp.bfloat16)
-    d_sp_up = start_grad(mlp_in_a, [grad_up_a], 256, (512,), (0,))
-    grad_first, grad_up_a = rounds([d_sp_down, d_sp_up, d_st_qkv, st_total], (grad_first, grad_up_a))
+    grad_first, grad_down_a = rounds([d_sp_down, d_st_attn, d_st_up], (grad_first, grad_down_a))
+    grad_up_a = product_scaled(grad_down_a, w_down_a, slope_a)
+    grad_first, grad_up_a = hold([d_sp_down], (grad_first, grad_up_a))
+    d_sp_up = start_grad([mlp_in_a], [grad_up_a], 256, (512,), (0,), (0,), [d_sp_down])
+    grad_first, grad_up_a = hold([d_sp_up], (grad_first, grad_up_a))
+    grad_first, grad_up_a = settle([d_st_attn], (grad_first, grad_up_a))
+    grad_first, grad_up_a = rounds([d_sp_up, d_st_attn], (grad_first, grad_up_a))
     grad_mlp_a = product_turned(grad_up_a, w_up_a)
     norm_grad, grad_shift_ma, grad_scale_ma = norm_back(grad_mlp_a, middle_a, mod[4])
     grad_middle_a = joint_ungroup(grad_first + norm_grad)
-    grad_win = enter_windows(grad_middle_a, own_half, pair_windows)
+    half_rows = grad_middle_a.reshape(pair_windows, -1, model_width)
+    keep_part, send_part = split_halves(half_rows, own_half)
+    send_part = send_part.astype(jnp.bfloat16)
+    keep_part, send_part, strip_grad_b = hold(
+        [d_sp_up, d_st_attn], (keep_part, send_part, strip_grad_b)
+    )
+    came_part = from_pair(send_part)
+    strip_grad_b = rounds([d_sp_down], strip_grad_b)
+    if quick:
+        d_st_attn.fold()
+        d_sp_up.fold()
+    rounds([d_st_attn], ())
+    st_sum = joint_strip_back(strip_grad_b)
+    keep_part, came_part, st_sum = lax.optimization_barrier((keep_part, came_part, st_sum))
+    grad_win = join_windows(keep_part, came_part.astype(jnp.float32), own_half)
     grad_mixed_a = (mod[2] * grad_win).astype(jnp.bfloat16)
     grad_gate_aa = jnp.sum(grad_win * mixed_a, axis=0)
-    grad_win, grad_mixed_a = rounds([d_sp_up, d_sp_down, st_total], (grad_win, grad_mixed_a))
-    d_sp_out = start_grad(attn_out_a, [grad_mixed_a], 256, (128,), (0,))
-    grad_attn_a = product_turned(grad_mixed_a, w_out_a).astype(jnp.bfloat16)
+    grad_win, grad_mixed_a = rounds([d_sp_up], (grad_win, grad_mixed_a))
+    grad_attn_a = product_turned(grad_mixed_a, w_out_a, jnp.bfloat16)
     grad_qkv_a, strip_grad_a = attend_back(
-        qkv_a, probs_a, grad_attn_a, SLOTS, WS * WS, sp_strip.shape[1], sp_strip.shape[2]
+        qkv_a, probs_a, grad_attn_a, SLOTS, WS * WS, *sp_strip.shape[1:], sp_strip.shape[1:]
     )
-    grad_win, grad_qkv_a = rounds([d_sp_out, d_sp_up, d_sp_down, st_total], (grad_win, grad_qkv_a))
-    sp_total = Total(spatial_strip_back(strip_grad_a), ("x", "core", "y", "z0", "z1"))
-    d_sp_qkv = start_grad(attn_in_a, [grad_qkv_a], 256, (384,), (0,))
-    grad_win, grad_qkv_a = rounds([d_sp_qkv, d_sp_out, d_sp_up, sp_total], (grad_win, grad_qkv_a))
+    grad_win, grad_qkv_a, strip_grad_a = settle([d_sp_down], (grad_win, grad_qkv_a, strip_grad_a))
+    grad_win, grad_qkv_a, strip_grad_a = rounds([d_sp_down], (grad_win, grad_qkv_a, strip_grad_a))
+    d_sp_attn = start_grad(
+        [attn_in_a, attn_out_a], [grad_qkv_a, grad_mixed_a], 256, (384, 128), (0, 0), (0, 1)
+    )
+    state = hold([d_sp_attn, d_sp_up, d_sp_down], (grad_win, grad_qkv_a, strip_grad_a, st_sum))
+    if quick:
+        d_sp_up.fold()
+        d_sp_down.fold()
+    grad_win, grad_qkv_a, strip_grad_a, st_sum = rounds([d_sp_attn, d_sp_up, d_sp_down], state)
     grad_in_a = product_turned(grad_qkv_a, w_qkv_a)
+    state = (grad_win, grad_in_a, strip_grad_a, st_sum)
+    state = settle([d_sp_attn, d_sp_up], state)
+    grad_win, grad_in_a, strip_grad_a, st_sum = rounds([d_sp_attn, d_sp_up], state)
     norm_grad, grad_shift_aa, grad_scale_aa = norm_back(grad_in_a, win_input, mod[1])
     mod_rows = [
         grad_shift_aa,
@@ -747,34 +980,46 @@
         grad_scale_mb,
         grad_gate_mb,
     ]
-    mod_total = Total(jnp.stack(mod_rows, axis=0), ("y", "z0", "z1"))
     win_sum = grad_win + norm_grad
-    win_sum = rounds([d_sp_qkv, d_sp_out, sp_total, mod_total], win_sum)
-    grad_tokens = leave_windows(win_sum, own_half, pair_windows).reshape(tokens.shape)
-    grad_tokens = rounds([d_sp_qkv, d_sp_out, sp_total, mod_total], grad_tokens)
-    rounds([d_sp_qkv, sp_total, mod_total], ())
-    rounds([sp_total], ())
+    keep_part, send_part = split_windows(win_sum, own_half)
+    send_part = send_part.astype(jnp.bfloat16)
+    sp_sum = spatial_strip_back(strip_grad_a)
+    tables = jnp.concatenate([sp_sum.reshape(-1), st_sum.reshape(-1)])
+    table_total = Total(tables, ("core", "z1", "z0", "y", "x"))
+    mod_total = Total(jnp.stack(mod_rows, axis=0), ("z1", "z0", "y"))
+    keep_part, send_part = settle([d_sp_attn], (keep_part, send_part))
+    keep_part, send_part = rounds([d_sp_attn, table_total, mod_total], (keep_part, send_part))
+    keep_part, send_part = settle([d_sp_attn], (keep_part, send_part))
+    keep_part, send_part = rounds([d_sp_attn, table_total, mod_total], (keep_part, send_part))
+    came_part = from_pair(send_part)
+    rounds([table_total, mod_total], ())
+    rounds([table_total], ())
+    rounds([table_total], ())
+    came_part = came_part.astype(jnp.float32)
+    grad_tokens = join_halves(keep_part, came_part, own_half, pair_windows).reshape(tokens.shape)
     if quick:
         grad_modulation = mod_total.result()[None]
-        grad_sp_table = sp_total.result()
-        grad_st_table = st_total.result()
+        table_sums = table_total.result()
     else:
         grad_modulation = lax.psum(jnp.stack(mod_rows, axis=0), "win")[None]
-        grad_sp_table = lax.psum(sp_total.result(), ("clip", "win"))
-        grad_st_table = lax.psum(st_total.result(), ("clip", "win"))
-    value_width = d_st_out.values.shape[1]
+        table_sums = lax.psum(table_total.result(), ("clip", "win"))
+    grad_sp_table = table_sums[: sp_table.size].reshape(sp_table.shape)
+    grad_st_table = table_sums[sp_table.size :].reshape(st_table.shape)
+    wide = d_st_attn.values
+    wide_a = d_sp_attn.values
+    out_width = wide.shape[1] // 4
     return (
         out_tokens,
         grad_tokens,
         grad_modulation,
-        d_sp_qkv.values,
-        d_sp_out.values,
+        wide_a[:, : 3 * out_width],
+        wide_a[:, 3 * out_width :],
         d_sp_up.values,
         d_sp_down.values,
         grad_sp_table,
-        d_st_qkv.values[:, :-value_width],
-        d_st_qkv.values[:, -value_width:],
-        d_st_out.values,
+        wide[:, : 2 * out_width],
+        wide[:, 2 * out_width : 3 * out_width],
+        wide[:, 3 * out_width :],
         d_st_up.values,
         d_st_down.values,
         grad_st_table,
@@ -782,10 +1027,10 @@
 
 
 class Plain:
-    def __init__(self, x, dys, widths, starts):
-        win = lax.axis_size("win")
+    def __init__(self, xs, dys, widths, starts, sources):
         grads = []
-        for dy, width, start in zip(dys, widths, starts):
+        for dy, width, start, source in zip(dys, widths, starts, sources):
+            x = xs[source]
             part = dy[:, start * 2 * width : start * 2 * width + 8 * width]
             full = lax.dot_general(x, part, TN, preferred_element_type=jnp.float32)
             full = lax.psum_scatter(

time: 950 us -> 806 us (0.85)
  matrix products: 161 us -> 12.1 us
  Pallas kernels: 238 us -> 367 us
  other arithmetic: 164 us -> 115 us
  waiting for transfers between devices: 162 us -> 132 us
  local copies, waits for them, and re-layouts: 110 us -> 84.7 us
  starting transfers between devices: 87.9 us -> 72 us
    dot_general x17 -> x1, matrix products: 154 us -> 3.14 us  [joint_strip_back(): grad = lax.dot_general(flat, onehot, NT, precision=highest)]
    pallas_call x24 -> x37, Pallas kernels: 207 us -> 336 us  [the longest x10 82.6 us: tiled(): pl.pallas_call(kernel, grid=(total // columns,), out_shape=jax.ShapeDtype...]
    add x32 -> x0, other arithmetic: 58.1 us -> none  [the longest x8 18.7 us: advance(): b_send = keep[1, :, 1] + came[1, :, 1]]
    ppermute x101 -> x86, waiting for transfers between devices: 140 us -> 96.3 us  [hop(): lax.ppermute(value, axis, [(i, i ^ mask) for i in range(lax.axis_size(axi...]
    another operation x37 -> x13, other arithmetic: 41.6 us -> 23.2 us  [the longest x12 21.5 us: go(): a1, b1 = (jnp.stack([a0, a_came]), jnp.stack([b0, b_came]))]
    reduce_sum x0 -> x5, other arithmetic: none -> 18.2 us  [the longest x4 13.5 us: norm_back(): return (grad, jnp.sum(grad_in, axis=0), jnp.sum(grad_in * unit, axis=0))]
    ppermute x4, waiting for transfers between devices: 14.7 us -> 32 us  [from_pair(): return lax.ppermute(value, 'win', pairs)]
    reshape x7 -> x3, local copies, waits for them, and re-layouts: 17.6 us -> 2.05 us  [the longest x1 1.39 us: body(): grad_st_table = table_sums[sp_table.size:].reshape(st_table.shape)]
  transfers between devices with their start and end apart: 119 -> 102, of which waited for: 31 -> 28; matrix products, arithmetic and copies ran while one was open for 43% -> 23% of each run, Pallas kernels for 22% -> 38%
where the time goes in v2:
time: 806 us; the launch traced here: 800 us
  Pallas kernels  367 us (46%)
  waiting for transfers between devices  132 us (16%)
  other arithmetic  115 us (14%)
  local copies, waits for them, and re-layouts  84.7 us (11%)
  starting transfers between devices  72 us (9%)
  between operations  17.4 us (2%)
  matrix products  12.1 us (2%)
    ppermute x86, waiting for transfers between devices, hop(): lax.ppermute(value, axis, [(i, i ^ mask) for i in range(lax.axis_size(axi...  96.3 us
    pallas_call x10, Pallas kernels, tiled(): pl.pallas_call(kernel, grid=(total // columns,), out_shape=jax.ShapeDtype...  82.6 us
    pallas_call x6, Pallas kernels, weight_grad(): pl.pallas_call(partial(grad_kernel, rows=rows, widths=widths, sources=sou...  81.2 us
    pallas_call x6, Pallas kernels, gathered(): pl.pallas_call(partial(gathered_kernel, rows=rows, widths=widths, kind=ki...  76.9 us
    ppermute x86, starting transfers between devices, hop(): lax.ppermute(value, axis, [(i, i ^ mask) for i in range(lax.axis_size(axi...  64.9 us
    pallas_call x13, Pallas kernels, fold(): pl.pallas_call(fold.kernel, out_shape=[fold.gives_part.shape(self.values[...  50.4 us
    pallas_call x2, Pallas kernels, attend_back(): pl.pallas_call(partial(attend_back_kernel, wins=wins, length=length, rows...  44.5 us
    ppermute x4, waiting for transfers between devices, from_pair(): return lax.ppermute(value, 'win', pairs)  32 us
  transfers between devices with their start and end apart: 102, of which 28 were waited for; matrix products, arithmetic and copies ran while one was open for 23% of the time, Pallas kernels for 38%

profile of v2, /device:TPU:0, one launch (start us, length us, event | category | flops | bytes accessed | tf_op | source)
XLA Modules:
  0.0 800.4 jit_solution(4376650382172654376)
XLA Ops:
  18.4 16.0 %collective-permute-done = bf16[3,128,1024]{2,1,0:T(8,128)(2,1)S(1)} collective-permute-done((bf16[3,128,1024]{2,1,0:T(8,128)(2,1)S(1)}, bf16[3,128,1024]{2,1,0:T(8,128)(2,1)S(1)}, u32[]{:S(2)}, u32[]{:S(2)}) %collective-permute-start) | collective-permute-done | bytes 786464 | tf_op jit(solution)/shard_map/ppermute | solution.py:683
  45.3 10.5 %collective-permute-done.1 = bf16[4,128,512]{2,1,0:T(8,128)(2,1)S(1)} collective-permute-done((bf16[4,128,512]{2,1,0:T(8,128)(2,1)S(1)}, bf16[4,128,512]{2,1,0:T(8,128)(2,1)S(1)}, u32[]{:S(2)}, u32[]{:S(2)}) %collective-permute-start.1) | collective-permute-done | bytes 524320 | tf_op jit(solution)/shard_map/ppermute | solution.py:34
  94.9 11.6 %gathered.6 = (bf16[768,3072]{1,0:T(8,128)(2,1)}, bf16[1024,3072]{1,0:T(8,128)(2,1)}, bf16[1024,1024]{1,0:T(8,128)(2,1)}) custom-call(s32[4]{0:T(128)} %pad_add_fusion.row_of, s32[2]{0:T(128)} %pad_add_fusion.1.y_of, bf16[768,1024]{1,0:T(8,128)(2,1)} %add_convert_fusion.x_ref.refs_0_, bf16[2,4,128,512]{3,2,1,0:T(8,128)(2,1)} %pad_maximum_fusion.3.refs_0_, ...), custom_call_target="tpu_custom_call" | custom-call | flops 1 | bytes 1 | tf_op jit(solution)/shard_map/gathered/pallas_call | solution.py:150
  117.9 13.4 %attend.2 = (bf16[768,1024]{1,0:T(8,128)(2,1)}, bf16[16,3,256,256]{3,2,1,0:T(8,128)(2,1)}) custom-call(bf16[768,3072]{1,0:T(8,128)(2,1)} %get-tuple-element.449.q_ref.k_ref.v_ref, bf16[768,3072]{1,0:T(8,128)(2,1)} %get-tuple-element.449.q_ref.k_ref.v_ref, bf16[768,3072]{1,0:T(8,128)(2,1)} %get-tuple-element.449.q_ref.k_ref.v_ref, ...), custom_call_target="tpu_custom_call" | custom-call | flops 1 | bytes 1 | tf_op jit(solution)/shard_map/attend/pallas_call | solution.py:497
  183.4 14.8 %gathered.7 = (bf16[640,4096]{1,0:T(8,128)(2,1)}, bf16[640,4096]{1,0:T(8,128)(2,1)}, bf16[1024,4096]{1,0:T(8,128)(2,1)}) custom-call(s32[4]{0:T(128)} %pad_add_fusion.row_of, s32[2]{0:T(128)} %pad_add_fusion.1.y_of, bf16[640,1024]{1,0:T(8,128)(2,1)} %add_convert_fusion.3.x_ref.refs_0_, bf16[2,4,128,512]{3,2,1,0:T(8,128)(2,1)} %pad_maximum_fusion.5.refs_0_, ...), custom_call_target="tpu_custom_call" | custom-call | flops 1 | bytes 1 | tf_op jit(solution)/shard_map/gathered/pallas_call | solution.py:150
  207.8 12.6 %gathered.8 = (f32[640,1024]{1,0:T(8,128)}, bf16[4096,1024]{1,0:T(8,128)(2,1)}) custom-call(s32[4]{0:T(128)} %pad_add_fusion.row_of, s32[2]{0:T(128)} %pad_add_fusion.1.y_of, bf16[640,4096]{1,0:T(8,128)(2,1)} %get-tuple-element.482.x_ref.refs_0_, bf16[2,4,512,128]{3,2,1,0:T(8,128)(2,1)} %pad_maximum_fusion.7.refs_0_, ...), custom_call_target="tpu_custom_call" | custom-call | flops 1 | bytes 1 | tf_op jit(solution)/shard_map/gathered/pallas_call | solution.py:150
  232.4 17.3 %collective-permute-done.30.refs_1_ = bf16[2,4,128,512]{3,2,1,0:T(8,128)(2,1)} collective-permute-done((bf16[2,4,128,512]{3,2,1,0:T(8,128)(2,1)}, bf16[2,4,128,512]{3,2,1,0:T(8,128)(2,1)}, u32[]{:S(2)}, u32[]{:S(2)}) %collective-permute-start.30) | collective-permute-done | bytes 1048608 | tf_op jit(solution)/shard_map/ppermute | solution.py:34
  259.6 10.8 %gathered.9 = (bf16[640,3072]{1,0:T(8,128)(2,1)}, bf16[1024,3072]{1,0:T(8,128)(2,1)}, bf16[1024,1024]{1,0:T(8,128)(2,1)}) custom-call(s32[4]{0:T(128)} %pad_add_fusion.row_of, s32[2]{0:T(128)} %pad_add_fusion.1.y_of, bf16[640,1024]{1,0:T(8,128)(2,1)} %add_convert_fusion.2.x_ref.refs_0_, bf16[2,4,128,512]{3,2,1,0:T(8,128)(2,1)} %pad_maximum_fusion.9.refs_0_, ...), custom_call_target="tpu_custom_call" | custom-call | flops 1 | bytes 1 | tf_op jit(solution)/shard_map/gathered/pallas_call | solution.py:150
  277.0 17.6 %attend.3 = (bf16[640,1024]{1,0:T(8,128)(2,1)}, bf16[16,2,320,320]{3,2,1,0:T(8,128)(2,1)}) custom-call(bf16[640,3072]{1,0:T(8,128)(2,1)} %get-tuple-element.512.q_ref.k_ref.v_ref, bf16[640,3072]{1,0:T(8,128)(2,1)} %get-tuple-element.512.q_ref.k_ref.v_ref, bf16[640,3072]{1,0:T(8,128)(2,1)} %get-tuple-element.512.q_ref.k_ref.v_ref, ...), custom_call_target="tpu_custom_call" | custom-call | flops 1 | bytes 1 | tf_op jit(solution)/shard_map/attend/pallas_call | solution.py:497
  310.3 14.9 %gathered.10 = (bf16[640,4096]{1,0:T(8,128)(2,1)}, bf16[640,4096]{1,0:T(8,128)(2,1)}, bf16[1024,4096]{1,0:T(8,128)(2,1)}) custom-call(s32[4]{0:T(128)} %pad_add_fusion.row_of, s32[2]{0:T(128)} %pad_add_fusion.1.y_of, bf16[640,1024]{1,0:T(8,128)(2,1)} %add_convert_fusion.1.x_ref.refs_0_, bf16[2,4,128,512]{3,2,1,0:T(8,128)(2,1)} %pad_maximum_fusion.11.refs_0_, ...), custom_call_target="tpu_custom_call" | custom-call | flops 1 | bytes 1 | tf_op jit(solution)/shard_map/gathered/pallas_call | solution.py:150
  330.2 12.8 %weight_grad.6 = (bf16[2,2,2,4,512,128]{5,4,3,2,1,0:T(8,128)(2,1)}, bf16[2,2,2,4,512,128]{5,4,3,2,1,0:T(8,128)(2,1)}) custom-call(s32[4]{0:T(128)} %pad_add_fusion.row_of, s32[2]{0:T(128)} %pad_add_fusion.1.y_of, bf16[640,4096]{1,0:T(8,128)(2,1)} %get-tuple-element.538.refs_0_.x_ref, bf16[640,1024]{1,0:T(8,128)(2,1)} %fusion.10.refs_1_.left), custom_call_target="tpu_custom_call" | custom-call | flops 1 | bytes 1 | tf_op jit(solution)/shard_map/weight_grad/pallas_call | solution.py:320
  356.5 12.3 %gathered.11 = (f32[640,1024]{1,0:T(8,128)}, bf16[4096,1024]{1,0:T(8,128)(2,1)}) custom-call(s32[4]{0:T(128)} %pad_add_fusion.row_of, s32[2]{0:T(128)} %pad_add_fusion.1.y_of, bf16[640,4096]{1,0:T(8,128)(2,1)} %get-tuple-element.538.refs_0_.x_ref, bf16[2,4,512,128]{3,2,1,0:T(8,128)(2,1)} %copy-done.24, ...), custom_call_target="tpu_custom_call" | custom-call | flops 1 | bytes 1 | tf_op jit(solution)/shard_map/gathered/pallas_call | solution.py:150
  368.8 11.5 %product.12.refs_1_.left = bf16[640,4096]{1,0:T(8,128)(2,1)} custom-call(bf16[640,1024]{1,0:T(8,128)(2,1)} %fusion.10.refs_1_.left, bf16[4096,1024]{1,0:T(8,128)(2,1)} %get-tuple-element.543.right, bf16[640,4096]{1,0:T(8,128)(2,1)} %get-tuple-element.544.factor), custom_call_target="tpu_custom_call" | custom-call | flops 1 | bytes 1 | tf_op jit(solution)/shard_map/product/pallas_call | solution.py:189
  382.2 13.8 %weight_grad.7 = (bf16[2,2,2,4,128,512]{5,4,3,2,1,0:T(8,128)(2,1)}, bf16[2,2,2,4,128,512]{5,4,3,2,1,0:T(8,128)(2,1)}, bf16[2,4,512,128]{3,2,1,0:T(8,128)(2,1)}, ...) custom-call(s32[4]{0:T(128)} %pad_add_fusion.row_of, ...), custom_call_target="tpu_custom_call" | custom-call | flops 1 | bytes 1 | tf_op jit(solution)/shard_map/weight_grad/pallas_call | solution.py:320
  398.9 10.9 %product.13 = f32[640,1024]{1,0:T(8,128)} custom-call(bf16[640,4096]{1,0:T(8,128)(2,1)} %product.12.refs_1_.left, bf16[1024,4096]{1,0:T(8,128)(2,1)} %get-tuple-element.556.right), custom_call_target="tpu_custom_call" | custom-call | flops 1 | bytes 1 | tf_op jit(solution)/shard_map/product/pallas_call | solution.py:189
  441.7 22.8 %attend_back.2 = (bf16[640,3072]{1,0:T(8,128)(2,1)}, f32[16,8,1152]{2,1,0:T(8,128)}) custom-call(bf16[640,3072]{1,0:T(8,128)(2,1)} %get-tuple-element.512.q_ref.k_ref.v_ref, bf16[640,3072]{1,0:T(8,128)(2,1)} %get-tuple-element.512.q_ref.k_ref.v_ref, bf16[640,3072]{1,0:T(8,128)(2,1)} %get-tuple-element.512.q_ref.k_ref.v_ref, ...), custom_call_target="tpu_custom_call" | custom-call | flops 1 | bytes 1 | tf_op jit(solution)/shard_map/attend_back/pallas_call | solution.py:583
  470.5 12.8 %weight_grad.8 = (bf16[2,2,2,4,128,512]{5,4,3,2,1,0:T(8,128)(2,1)}, bf16[2,2,2,4,128,512]{5,4,3,2,1,0:T(8,128)(2,1)}, bf16[4,2,512,128]{3,2,1,0:T(8,128)(2,1)}) custom-call(s32[4]{0:T(128)} %pad_add_fusion.row_of, s32[2]{0:T(128)} %pad_add_fusion.1.y_of, bf16[640,1024]{1,0:T(8,128)(2,1)} %add_convert_fusion.2.x_ref.refs_0_, ...), custom_call_target="tpu_custom_call" | custom-call | flops 1 | bytes 1 | tf_op jit(solution)/shard_map/weight_grad/pallas_call | solution.py:320
  508.9 15.7 %weight_grad.9 = (bf16[2,2,2,4,512,128]{5,4,3,2,1,0:T(8,128)(2,1)}, bf16[2,2,2,4,512,128]{5,4,3,2,1,0:T(8,128)(2,1)}, bf16[2,4,128,512]{3,2,1,0:T(8,128)(2,1)}, ...) custom-call(s32[4]{0:T(128)} %pad_add_fusion.row_of, ...), custom_call_target="tpu_custom_call" | custom-call | flops 1 | bytes 1 | tf_op jit(solution)/shard_map/weight_grad/pallas_call | solution.py:320
  526.6 11.4 %product.16.refs_1_.left = bf16[640,4096]{1,0:T(8,128)(2,1)} custom-call(bf16[640,1024]{1,0:T(8,128)(2,1)} %multiply_convert_fusion.1.refs_1_.left, bf16[4096,1024]{1,0:T(8,128)(2,1)} %get-tuple-element.644.right, bf16[640,4096]{1,0:T(8,128)(2,1)} %get-tuple-element.645.factor), custom_call_target="tpu_custom_call" | custom-call | flops 1 | bytes 1 | tf_op jit(solution)/shard_map/product/pallas_call | solution.py:189
  540.1 13.9 %weight_grad.10 = (bf16[2,2,2,4,128,512]{5,4,3,2,1,0:T(8,128)(2,1)}, bf16[2,2,2,4,128,512]{5,4,3,2,1,0:T(8,128)(2,1)}, bf16[2,4,512,128]{3,2,1,0:T(8,128)(2,1)},...) custom-call(s32[4]{0:T(128)} %pad_add_fusion.row_of, ...), custom_call_target="tpu_custom_call" | custom-call | flops 1 | bytes 1 | tf_op jit(solution)/shard_map/weight_grad/pallas_call | solution.py:320
  559.9 11.0 %product.17 = f32[640,1024]{1,0:T(8,128)} custom-call(bf16[640,4096]{1,0:T(8,128)(2,1)} %product.16.refs_1_.left, bf16[1024,4096]{1,0:T(8,128)(2,1)} %get-tuple-element.674.right), custom_call_target="tpu_custom_call" | custom-call | flops 1 | bytes 1 | tf_op jit(solution)/shard_map/product/pallas_call | solution.py:189
  608.7 21.8 %attend_back.3 = (bf16[768,3072]{1,0:T(8,128)(2,1)}, f32[16,16,512]{2,1,0:T(8,128)}) custom-call(bf16[768,3072]{1,0:T(8,128)(2,1)} %get-tuple-element.449.q_ref.k_ref.v_ref, bf16[768,3072]{1,0:T(8,128)(2,1)} %get-tuple-element.449.q_ref.k_ref.v_ref, bf16[768,3072]{1,0:T(8,128)(2,1)} %get-tuple-element.449.q_ref.k_ref.v_ref, ...), custom_call_target="tpu_custom_call" | custom-call | flops 1 | bytes 1 | tf_op jit(solution)/shard_map/attend_back/pallas_call | solution.py:583
  637.0 12.3 %weight_grad.11 = (bf16[2,2,2,4,128,512]{5,4,3,2,1,0:T(8,128)(2,1)}, bf16[2,2,2,4,128,512]{5,4,3,2,1,0:T(8,128)(2,1)}) custom-call(s32[4]{0:T(128)} %pad_add_fusion.row_of, s32[2]{0:T(128)} %pad_add_fusion.1.y_of, bf16[768,1024]{1,0:T(8,128)(2,1)} %add_convert_fusion.x_ref.refs_0_, bf16[768,1024]{1,0:T(8,128)(2,1)} %get-tuple-element.455.left.refs_1_, ...), custom_call_target="tpu_custom_call" | custom-call | flops 1 | bytes 1 | tf_op jit(solution)/shard_map/weight_grad/pallas_call | solution.py:320
  664.7 10.2 %product.19 = f32[768,1024]{1,0:T(8,128)} custom-call(bf16[768,3072]{1,0:T(8,128)(2,1)} %get-tuple-element.751.refs_2_.left, bf16[1024,3072]{1,0:T(8,128)(2,1)} %get-tuple-element.752.right), custom_call_target="tpu_custom_call" | custom-call | flops 1 | bytes 1 | tf_op jit(solution)/shard_map/product/pallas_call | solution.py:189
  (601 shorter events, 450.6 us)
Async XLA Ops:
  10.1 76.8 %all-gather.13.cloned.1.call-start = ((), (), s32[]{:S(2)}) async-start(), calls=%async_computation.9 | async-start | bytes 1310720 | tf_op jit(solution)/shard_map/all_gather | solution.py:47
  12.0 96.2 %all-gather.11.cloned.1.call-start = ((), (), s32[]{:S(2)}) async-start(), calls=%async_computation.8 | async-start | bytes 1310720 | tf_op jit(solution)/shard_map/all_gather | solution.py:47
  12.8 170.6 %all-gather.17.cloned.1.call-start = ((), (), s32[]{:S(2)}) async-start(), calls=%async_computation.11 | async-start | bytes 1310720 | tf_op jit(solution)/shard_map/all_gather | solution.py:47
  13.7 189.7 %all-gather.9.cloned.1.call-start = ((), (), s32[]{:S(2)}) async-start(), calls=%async_computation.7 | async-start | bytes 1310720 | tf_op jit(solution)/shard_map/all_gather | solution.py:47
  17.7 252.7 %all-gather.7.cloned.1.call-start = ((), (), s32[]{:S(2)}) async-start(), calls=%async_computation.6 | async-start | bytes 1310720 | tf_op jit(solution)/shard_map/all_gather | solution.py:47
  110.5 39.6 %collective-permute-start.11 = (bf16[4,512,128]{2,1,0:T(8,128)(2,1)}, bf16[4,512,128]{2,1,0:T(8,128)(2,1)}, u32[]{:S(2)}, u32[]{:S(2)}) collective-permute-start(bf16[4,512,128]{2,1,0:T(8,128)(2,1)} %get-tuple-element.459), channel_id=1, source_target_pairs={{0,1},{1,0},{2,3},{3,2},{4,5},{5,4},{6,7},{7,6},{8,9},{9,8},{10,11... | collective-permute-start | bytes 1572872 | tf_op jit(solution)/shard_map/ppermute | solution.py:34
  111.1 39.0 %collective-permute-start.12 = (bf16[4,512,128]{2,1,0:T(8,128)(2,1)}, bf16[4,512,128]{2,1,0:T(8,128)(2,1)}, u32[]{:S(2)}, u32[]{:S(2)}) collective-permute-start(bf16[4,512,128]{2,1,0:T(8,128)(2,1)} %get-tuple-element.461), channel_id=1, source_target_pairs={{0,16},{8,24},{16,0},{24,8},{1,17},{9,25},{17,1},{25,9},{2,18},{10... | collective-permute-start | bytes 1572872 | tf_op jit(solution)/shard_map/ppermute | solution.py:34
  152.4 45.9 %collective-permute-start.15 = (bf16[2,4,512,128]{3,2,1,0:T(8,128)(2,1)}, bf16[2,4,512,128]{3,2,1,0:T(8,128)(2,1)}, u32[]{:S(2)}, u32[]{:S(2)}) collective-permute-start(bf16[2,4,512,128]{3,2,1,0:T(8,128)(2,1)} %pad_maximum_fusion.7.refs_0_), channel_id=1, source_target_pairs={{0,16},{8,24},{16,0},{24,8},{1,17},{9,25},{17,1},{25,9},{2,18},{10... | collective-permute-start | bytes 3145736 | tf_op jit(solution)/shard_map/ppermute | solution.py:34
  156.2 42.1 %collective-permute-start.16 = (bf16[2,4,512,128]{3,2,1,0:T(8,128)(2,1)}, bf16[2,4,512,128]{3,2,1,0:T(8,128)(2,1)}, u32[]{:S(2)}, u32[]{:S(2)}) collective-permute-start(bf16[2,4,512,128]{3,2,1,0:T(8,128)(2,1)} %pad_maximum_fusion.8.refs_4_), channel_id=1, source_target_pairs={{0,1},{1,0},{2,3},{3,2},{4,5},{5,4},{6,7},{7,6},{8,9},{9,8},{10,11... | collective-permute-start | bytes 3145736 | tf_op jit(solution)/shard_map/ppermute | solution.py:34
  203.3 556.3 %reduce-scatter.17.cloned.1.call-start = ((), (), s32[]{:S(2)}) async-start(), calls=%async_computation.17 | async-start | bytes 1310720 | tf_op jit(solution)/shard_map/reduce_scatter | solution.py:371
  205.4 44.8 %collective-permute-start.22 = (bf16[4,128,512]{2,1,0:T(8,128)(2,1)}, bf16[4,128,512]{2,1,0:T(8,128)(2,1)}, u32[]{:S(2)}, u32[]{:S(2)}) collective-permute-start(bf16[4,128,512]{2,1,0:T(8,128)(2,1)} %get-tuple-element.498), channel_id=1, source_target_pairs={{0,1},{1,0},{2,3},{3,2},{4,5},{5,4},{6,7},{7,6},{8,9},{9,8},{10,11... | collective-permute-start | bytes 1572872 | tf_op jit(solution)/shard_map/ppermute | solution.py:34
  206.4 44.2 %collective-permute-start.23 = (bf16[4,128,512]{2,1,0:T(8,128)(2,1)S(1)}, bf16[4,128,512]{2,1,0:T(8,128)(2,1)}, u32[]{:S(2)}, u32[]{:S(2)}) collective-permute-start(bf16[4,128,512]{2,1,0:T(8,128)(2,1)S(1)} %get-tuple-element.500), channel_id=1, source_target_pairs={{0,16},{8,24},{16,0},{24,8},{1,17},{9,25},{17,1},{25,9},{2,18},{10... | collective-permute-start | bytes 1572872 | tf_op jit(solution)/shard_map/ppermute | solution.py:34
  252.8 41.8 %collective-permute-start.38 = (bf16[2,4,128,512]{3,2,1,0:T(8,128)(2,1)}, bf16[2,4,128,512]{3,2,1,0:T(8,128)(2,1)}, u32[]{:S(2)}, u32[]{:S(2)}) collective-permute-start(bf16[2,4,128,512]{3,2,1,0:T(8,128)(2,1)} %pad_maximum_fusion.11.refs_0_), channel_id=1, source_target_pairs={{0,16},{8,24},{16,0},{24,8},{1,17},{9,25},{17,1},{25,9},{2,18},{10... | collective-permute-start | bytes 3145736 | tf_op jit(solution)/shard_map/ppermute | solution.py:34
  433.3 50.0 %collective-permute-start.56 = (bf16[2,4,128,512]{3,2,1,0:T(8,128)(2,1)S(1)}, bf16[2,4,128,512]{3,2,1,0:T(8,128)(2,1)S(1)}, u32[]{:S(2)}, u32[]{:S(2)}) collective-permute-start(bf16[2,4,128,512]{3,2,1,0:T(8,128)(2,1)S(1)} %copy-done.94), channel_id=1, source_target_pairs={{0,16},{8,24},{16,0},{24,8},{1,17},{9,25},{17,1},{25,9},{2,18},{10... | collective-permute-start | bytes 3145736 | tf_op jit(solution)/shard_map/ppermute | solution.py:34
  434.3 49.0 %collective-permute-start.57 = (bf16[2,4,128,512]{3,2,1,0:T(8,128)(2,1)S(1)}, bf16[2,4,128,512]{3,2,1,0:T(8,128)(2,1)S(1)}, u32[]{:S(2)}, u32[]{:S(2)}) collective-permute-start(bf16[2,4,128,512]{3,2,1,0:T(8,128)(2,1)S(1)} %copy-done.93), channel_id=1, source_target_pairs={{0,1},{1,0},{2,3},{3,2},{4,5},{5,4},{6,7},{7,6},{8,9},{9,8},{10,11... | collective-permute-start | bytes 3145736 | tf_op jit(solution)/shard_map/ppermute | solution.py:34
  557.6 203.7 %reduce-scatter.15.cloned.1.call-start = ((), (), s32[]{:S(2)}) async-start(), calls=%async_computation.16 | async-start | bytes 1310720 | tf_op jit(solution)/shard_map/reduce_scatter | solution.py:371
  576.8 53.8 %collective-permute-start.68 = (bf16[2,4,512,128]{3,2,1,0:T(8,128)(2,1)}, bf16[2,4,512,128]{3,2,1,0:T(8,128)(2,1)}, u32[]{:S(2)}, u32[]{:S(2)}) collective-permute-start(bf16[2,4,512,128]{3,2,1,0:T(8,128)(2,1)} %get-tuple-element.704), channel_id=1, source_target_pairs={{0,16},{8,24},{16,0},{24,8},{1,17},{9,25},{17,1},{25,9},{2,18},{10... | collective-permute-start | bytes 3145736 | tf_op jit(solution)/shard_map/ppermute | solution.py:34
  577.8 52.8 %collective-permute-start.69 = (bf16[2,4,512,128]{3,2,1,0:T(8,128)(2,1)}, bf16[2,4,512,128]{3,2,1,0:T(8,128)(2,1)}, u32[]{:S(2)}, u32[]{:S(2)}) collective-permute-start(bf16[2,4,512,128]{3,2,1,0:T(8,128)(2,1)} %get-tuple-element.706), channel_id=1, source_target_pairs={{0,1},{1,0},{2,3},{3,2},{4,5},{5,4},{6,7},{7,6},{8,9},{9,8},{10,11... | collective-permute-start | bytes 3145736 | tf_op jit(solution)/shard_map/ppermute | solution.py:34
  602.0 49.3 %collective-permute-start.70 = (bf16[2,4,128,512]{3,2,1,0:T(8,128)(2,1)}, bf16[2,4,128,512]{3,2,1,0:T(8,128)(2,1)S(1)}, u32[]{:S(2)}, u32[]{:S(2)}) collective-permute-start(bf16[2,4,128,512]{3,2,1,0:T(8,128)(2,1)} %get-tuple-element.725), channel_id=1, source_target_pairs={{0,16},{8,24},{16,0},{24,8},{1,17},{9,25},{17,1},{25,9},{2,18},{10... | collective-permute-start | bytes 3145736 | tf_op jit(solution)/shard_map/ppermute | solution.py:34
  602.8 48.5 %collective-permute-start.71 = (bf16[2,4,128,512]{3,2,1,0:T(8,128)(2,1)}, bf16[2,4,128,512]{3,2,1,0:T(8,128)(2,1)}, u32[]{:S(2)}, u32[]{:S(2)}) collective-permute-start(bf16[2,4,128,512]{3,2,1,0:T(8,128)(2,1)} %get-tuple-element.727), channel_id=1, source_target_pairs={{0,1},{1,0},{2,3},{3,2},{4,5},{5,4},{6,7},{7,6},{8,9},{9,8},{10,11... | collective-permute-start | bytes 3145736 | tf_op jit(solution)/shard_map/ppermute | solution.py:34
  603.8 161.6 %reduce-scatter.13.cloned.1.call-start = ((), (), s32[]{:S(2)}) async-start(), calls=%async_computation.15 | async-start | bytes 1310720 | tf_op jit(solution)/shard_map/reduce_scatter | solution.py:371
  661.4 107.2 %reduce-scatter.11.cloned.1.call-start = ((), (), s32[]{:S(2)}) async-start(), calls=%async_computation.14 | async-start | bytes 1310720 | tf_op jit(solution)/shard_map/reduce_scatter | solution.py:371
  662.0 110.3 %reduce-scatter.9.cloned.1.call-start = ((), (), s32[]{:S(2)}) async-start(), calls=%async_computation.13 | async-start | bytes 1310720 | tf_op jit(solution)/shard_map/reduce_scatter | solution.py:371
  706.1 84.0 %reduce-scatter.7.cloned.1.call-start = ((), (), s32[]{:S(2)}) async-start(), calls=%async_computation.12 | async-start | bytes 1310720 | tf_op jit(solution)/shard_map/reduce_scatter | solution.py:371
  (175 other events, 2170.4 us)
Sparse Core Ops, SparseCore 0:
  10.2 30.6 all-gather.14
  43.0 27.4 all-gather.12
  72.1 27.4 all-gather.10
  101.0 27.4 all-gather.16
  129.8 27.4 all-gather.8
  203.4 27.1 all-gather.6
  557.7 26.2 reduce-scatter.16
  603.9 26.0 reduce-scatter.14
  661.5 25.9 reduce-scatter.12
  689.7 25.7 reduce-scatter.10
  717.8 30.9 reduce-scatter.8
  763.2 25.5 reduce-scatter.6

commit v3 on v2

--- a/solution.py
+++ b/solution.py
@@ -3,6 +3,7 @@
 
 import jax
 import jax.numpy as jnp
+import numpy as np
 from jax import lax
 from jax.experimental import pallas as pl
 from jax.experimental.pallas import tpu as pltpu
@@ -40,14 +41,16 @@
 
 
 class Gather:
-    def __init__(self, shard):
-        rows, cols = shard.shape
+    def __init__(self, halves, rows, early):
         self.rows = rows
-        halves = shard.reshape(2, rows // 2, cols)
-        grown = lax.all_gather(halves, "win", axis=1, tiled=False, axis_index_groups=z_groups())
+        self.early = early
+        axis = halves.ndim - 2
+        grown = lax.all_gather(halves, "win", axis=axis, tiled=False, axis_index_groups=z_groups())
         self.held = {"grown": (grown,)}
 
     def needs(self, move):
+        if move == "far" and self.early:
+            return "grown"
         return {"near": "grown", "far": "near", "core_near": "own", "core_far": "away"}[move]
 
     def go(self, move):
@@ -57,8 +60,11 @@
             a0, b0 = grown[0], grown[1]
             self.held["near"] = (a0, hop(a0, "y"), b0, hop(b0, "x"))
         elif move == "far":
-            a0, a_came, b0, b_came = values
-            a1, b1 = jnp.stack([a0, a_came]), jnp.stack([b0, b_came])
+            if self.early:
+                a1, b1 = values[0][0], values[0][1]
+            else:
+                a0, a_came, b0, b_came = values
+                a1, b1 = jnp.stack([a0, a_came]), jnp.stack([b0, b_came])
             self.held["own"] = (a1, b1)
             self.held["away"] = (hop(a1, "x"), hop(b1, "y"))
         else:
@@ -419,21 +425,17 @@
 
 def spatial_strip_back(strip):
     side = 2 * WS - 1
-    onehot = pair_table(WS).transpose(2, 1, 0).reshape(side, WS * WS)
-    shaped = strip[:, :, : side * WS].reshape(HEADS, WS, side, WS).transpose(0, 2, 1, 3)
-    flat = shaped.reshape(HEADS * side, WS * WS)
-    return lax.dot_general(flat, onehot, NT, precision=highest).reshape(HEADS, side, side)
+    shaped = strip.reshape(HEADS, 2, WS, 2 * WS).transpose(0, 2, 1, 3)
+    return shaped.reshape(HEADS, 2 * WS, 2 * WS)[:, :side, :side]
 
 
 def joint_onehot():
     span = 2 * HS - 1
-    table_dims = (span * span, HS**4)
-    offset = lax.broadcasted_iota(jnp.int32, table_dims, 0)
-    pair = lax.broadcasted_iota(jnp.int32, table_dims, 1)
-    key_row, key_col = pair // HS**3, pair // HS**2 % HS
-    query_row, query_col = pair // HS % HS, pair % HS
-    wanted = (query_row - key_row + HS - 1) * span + query_col - key_col + HS - 1
-    return (offset == wanted).astype(jnp.float32)
+    place = np.arange(HS)
+    apart = place[None, :] - place[:, None] + HS - 1
+    wanted = apart[:, None, :, None] * span + apart[None, :, None, :]
+    offset = np.arange(span * span)[:, None]
+    return jnp.asarray((offset == wanted.reshape(1, -1)).astype(np.float32))
 
 
 def joint_strip(table):
@@ -445,16 +447,9 @@
 
 
 def joint_strip_back(strip):
-    frames, span, lanes = 2 * FR - 1, 2 * HS - 1, 2 * HS * HS
-    shaped = strip.reshape(HEADS, HS, frames, lanes).transpose(0, 2, 1, 3)
-    table_dims = (span * span, HS * lanes)
-    offset = lax.broadcasted_iota(jnp.int32, table_dims, 0)
-    pair = lax.broadcasted_iota(jnp.int32, table_dims, 1)
-    wanted = pair // HS % (2 * HS) * span + pair % HS - pair // lanes + HS - 1
-    onehot = ((offset == wanted) & (pair // HS % (2 * HS) < span)).astype(jnp.float32)
-    flat = shaped.reshape(HEADS * frames, HS * lanes)
-    grad = lax.dot_general(flat, onehot, NT, precision=highest)
-    return grad.reshape(HEADS, frames, span, span)
+    span = 2 * HS - 1
+    shaped = strip.reshape(HEADS, 2, 2 * FR - 1, HS, 2 * HS).transpose(0, 2, 3, 1, 4)
+    return shaped.reshape(HEADS, 2 * FR - 1, 2 * HS, 2 * HS)[:, :, :span, :span]
 
 
 def head_lanes(which):
@@ -562,20 +557,38 @@
             offset = (blocks - 1 - block) * rows
             piece = total[block * rows : (block + 1) * rows, :]
             strip = strip + (piece if offset == 0 else pltpu.roll(piece, offset, 1))
-        if strip_ref.shape[1] == rows:
-            strip_ref[head] = strip
-            continue
-        lane = lax.broadcasted_iota(jnp.int32, (1, 128), 1)
-        for offset in range(strip_ref.shape[2] // 128):
-            odd = offset % 2
-            there = slice(offset // 2 * 128, offset // 2 * 128 + 128)
-            summed = None
-            for row in range(HS):
-                piece = jnp.where(lane // 64 == odd, strip[row * HS : (row + 1) * HS, there], 0.0)
-                shift = (64 * odd + (HS - 1 - row) * HS) % 128
-                piece = piece if shift == 0 else pltpu.roll(piece, shift, 1)
-                summed = piece if summed is None else summed + piece
-            strip_ref[head, :, offset * 128 : (offset + 1) * 128] = summed
+        if rows > WS:
+            strip = split_rows(strip)
+        skew(strip, strip_ref, head)
+
+
+def split_rows(strip):
+    lane = lax.broadcasted_iota(jnp.int32, (1, 128), 1)
+    groups = []
+    for offset in range(2 * FR - 1):
+        odd = offset % 2
+        there = slice(offset // 2 * 128, offset // 2 * 128 + 128)
+        summed = None
+        for row in range(HS):
+            piece = jnp.where(lane // 64 == odd, strip[row * HS : (row + 1) * HS, there], 0.0)
+            shift = (64 * odd + (HS - 1 - row) * HS) % 128
+            piece = piece if shift == 0 else pltpu.roll(piece, shift, 1)
+            summed = piece if summed is None else summed + piece
+        groups.append(summed)
+    return jnp.concatenate(groups, axis=1)
+
+
+def skew(strip, out_ref, head):
+    columns, lanes = strip.shape
+    lane = lax.broadcasted_iota(jnp.int32, (1, lanes), 1)
+    for odd in range(2):
+        part = jnp.where(lane // columns % 2 == odd, strip, 0.0)
+        if odd:
+            part = pltpu.roll(part, lanes - columns, 1)
+        summed = part[columns - 1 :, :]
+        for column in range(columns - 1):
+            summed = summed + pltpu.roll(part[column : column + 1, :], columns - 1 - column, 1)
+        out_ref[head, odd : odd + 1, :] = summed
 
 
 def attend_back(qkv, probs, grad_out, wins, length, rows, lanes, strip):
@@ -616,13 +629,69 @@
     return (plain_norm(values)[0] * (1.0 + scale_vec) + shift_vec).astype(jnp.bfloat16)
 
 
-def norm_back(grad_in, values, scale_vec):
-    unit, scale = plain_norm(values)
-    inner = grad_in * (1.0 + scale_vec)
+def row_call(kernel, wide, vectors, kept, sums, name):
+    count, width = wide[0].shape
+    block = pl.BlockSpec((count // 2, width), lambda i: (i, 0))
+    whole = pl.BlockSpec((1, width), lambda i: (0, 0))
+    out_shape = [jax.ShapeDtypeStruct((count, width), kind) for kind in kept]
+    out_specs = [block] * len(kept)
+    if sums:
+        out_shape.append(jax.ShapeDtypeStruct((8, width), jnp.float32))
+        out_specs.append(pl.BlockSpec((8, width), lambda i: (0, 0)))
+    return pl.pallas_call(
+        kernel,
+        grid=(2,),
+        out_shape=out_shape,
+        in_specs=[block] * len(wide) + [whole] * len(vectors),
+        out_specs=out_specs,
+        compiler_params=pltpu.CompilerParams(vmem_limit_bytes=VMEM_BYTES),
+        cost_estimate=SMALL,
+        name=name,
+    )(*wide, *[vector.reshape(1, width) for vector in vectors])
+
+
+def residual_kernel(rows, branch, gate, shift, scale, out, unit):
+    values = rows[...] + gate[...] * branch[...]
+    out[...] = values
+    unit[...] = modulated_norm(values, shift[...], scale[...])
+
+
+def add_branch(rows, branch, gate, shift, scale):
+    kept = (jnp.float32, jnp.bfloat16)
+    return row_call(residual_kernel, [rows, branch], [gate, shift, scale], kept, False, "add_branch")
+
+
+def norm_back_kernel(grad_in, values, grad_rows, *refs):
+    if len(refs) == 6:
+        branch, scale, gate, out, gated, sums = refs
+    else:
+        scale, out, sums = refs
+    unit, rate = plain_norm(values[...])
+    grads = grad_in[...]
+    inner = grads * (1.0 + scale[...])
     mean_one = jnp.mean(inner, axis=-1, keepdims=True)
     mean_two = jnp.mean(inner * unit, axis=-1, keepdims=True)
-    grad = scale * (inner - mean_one - unit * mean_two)
-    return grad, jnp.sum(grad_in, axis=0), jnp.sum(grad_in * unit, axis=0)
+    total = grad_rows[...] + rate * (inner - mean_one - unit * mean_two)
+    out[...] = total
+
+    @pl.when(pl.program_id(0) == 0)
+    def clear():
+        sums[...] = jnp.zeros_like(sums)
+
+    sums[0:1, :] += jnp.sum(grads, axis=0, keepdims=True)
+    sums[1:2, :] += jnp.sum(grads * unit, axis=0, keepdims=True)
+    if len(refs) == 6:
+        gated[...] = (gate[...] * total).astype(jnp.bfloat16)
+        sums[2:3, :] += jnp.sum(total * branch[...], axis=0, keepdims=True)
+
+
+def norm_back(grad_in, values, grad_rows, scale, branch=None, gate=None):
+    if branch is None:
+        kept = (jnp.float32,)
+        return row_call(norm_back_kernel, [grad_in, values, grad_rows], [scale], kept, True, "norm_back")
+    kept = (jnp.float32, jnp.bfloat16)
+    wide = [grad_in, values, grad_rows, branch]
+    return row_call(norm_back_kernel, wide, [scale, gate], kept, True, "norm_back")
 
 
 def gelu_both(upward):
@@ -681,19 +750,6 @@
 def from_pair(value):
     pairs = [(i, i ^ 1) for i in range(lax.axis_size("win"))]
     return lax.ppermute(value, "win", pairs)
-
-
-def leave_windows(win_rows, own_half, pair_windows):
-    keep_part, send_part = split_windows(win_rows, own_half)
-    came_part = from_pair(send_part.astype(jnp.bfloat16)).astype(send_part.dtype)
-    return join_halves(keep_part, came_part, own_half, pair_windows)
-
-
-def enter_windows(flat_rows, own_half, pair_windows):
-    half_rows = flat_rows.reshape(pair_windows, -1, flat_rows.shape[-1])
-    keep_part, send_part = split_halves(half_rows, own_half)
-    came_part = from_pair(send_part.astype(jnp.bfloat16)).astype(send_part.dtype)
-    return join_windows(keep_part, came_part, own_half)
 
 
 class Weights:
@@ -707,7 +763,9 @@
                 qkv, out, up, down = low[4 * block : 4 * block + 4]
                 shards += [jnp.concatenate([qkv, out], axis=1), up, down]
             self.widths = [(384, 128), (512,), (128,)] * 2
-            self.jobs = [Gather(shard) for shard in shards]
+            halves = [shard.reshape(2, shard.shape[0] // 2, -1) for shard in shards]
+            self.jobs = [Gather(value, 2 * value.shape[1], False) for value in halves[:2]] + [None] * 4
+            self.later = [(units, jnp.stack([halves[unit] for unit in units], axis=1)) for units in ((2, 5), (3, 4))]
         else:
             self.full = [
                 lax.all_gather(lax.all_gather(shard, "win", axis=1, tiled=True), "clip", axis=0, tiled=True)
@@ -723,6 +781,7 @@
         if not self.quick:
             return state
         jobs = [(self.jobs[unit], move) for unit, move in moves]
+        jobs = [(job, move) for job, move in jobs if not (job.early and move == "near")]
         known = [(job, job.needs(move)) for job, move in jobs if job.needs(move) in job.held]
         known += [(self.jobs[unit], name) for unit, name in after]
         held, state = lax.optimization_barrier(([job.held[name] for job, name in known], state))
@@ -730,6 +789,18 @@
             job.held[name] = values
         for job, move in jobs:
             job.go(move)
+        return state
+
+    def begin(self, state):
+        if not self.quick:
+            return state
+        state, held = lax.optimization_barrier((state, [value for units, value in self.later]))
+        for (units, unused), (a0, b0) in zip(self.later, held):
+            a_came, b_came = hop(a0, "y"), hop(b0, "x")
+            for place, unit in enumerate(units):
+                near = [a0[place], a_came[place], b0[place], b_came[place]]
+                halves = jnp.stack(near).reshape(2, 2, *near[0].shape)
+                self.jobs[unit] = Gather(halves, 2 * near[0].shape[0], True)
         return state
 
     def apply(self, unit, x, kind):
@@ -796,11 +867,14 @@
     st_allowed = (st_valid[:, :, None] | jnp.eye(joint_len, dtype=bool)[None]).astype(jnp.float32)
 
     half_tokens = tokens.reshape(pair_windows, half_len, model_width)
-    win_input = enter_windows(half_tokens, own_half, pair_windows).astype(jnp.float32)
+    keep_part, send_part = split_halves(half_tokens, own_half)
+    came_part = weights.begin(from_pair(send_part))
+    came_part = weights.go([(0, "near")], came_part)
+    win_input = join_windows(keep_part, came_part, own_half).astype(jnp.float32)
     attn_in_a = modulated_norm(win_input, mod[0], mod[1])
 
     go = weights.go
-    state = go([(0, "near")], (win_input, attn_in_a, sp_table))
+    state = (win_input, attn_in_a, sp_table)
     win_input, attn_in_a, sp_table = go([(0, "far"), (0, "core_near")], state)
     sp_strip = spatial_strip(sp_table)
     state = go([(1, "near")], (win_input, attn_in_a, sp_strip, sp_allowed))
@@ -816,7 +890,7 @@
     send_part = send_part.astype(jnp.bfloat16)
     keep_part, send_part, st_table = go([(1, "core_far")], (keep_part, send_part, st_table))
     came_part = from_pair(send_part)
-    keep_part, st_table = go([(2, "far")], (keep_part, st_table))
+    keep_part, st_table = go([(2, "far"), (2, "core_near")], (keep_part, st_table))
     st_strip = joint_strip(st_table)
     keep_part, came_part, st_strip, st_allowed = lax.optimization_barrier(
         (keep_part, came_part, st_strip, st_allowed)
@@ -824,26 +898,22 @@
     middle_a = joint_group(join_halves(keep_part, came_part.astype(jnp.float32), own_half, pair_windows))
     mlp_in_a = modulated_norm(middle_a, mod[3], mod[4])
 
-    middle_a, mlp_in_a = go([(3, "near")], (middle_a, mlp_in_a))
     hidden_a, slope_a, w_up_a = weights.apply(1, mlp_in_a, "gelu")
-    middle_a, hidden_a, slope_a = go([(2, "core_near"), (2, "core_far")], (middle_a, hidden_a, slope_a))
-    middle_a, hidden_a, slope_a = go([(4, "near")], (middle_a, hidden_a, slope_a))
+    state = go([(2, "core_far")], (middle_a, hidden_a, slope_a))
+    middle_a, hidden_a, slope_a = go([(3, "far")], state)
     downward_a, w_down_a = weights.apply(2, hidden_a, "wide")
-    middle_a, downward_a = go([(3, "far")], (middle_a, downward_a))
     middle_a, downward_a = go([(3, "core_near")], (middle_a, downward_a))
-    first_out = middle_a + mod[5] * downward_a
-    attn_in_b = modulated_norm(first_out, mod[6], mod[7])
+    first_out, attn_in_b = add_branch(middle_a, downward_a, mod[5], mod[6], mod[7])
 
     first_out, attn_in_b = go([(3, "core_far")], (first_out, attn_in_b))
     first_out, attn_in_b = go([(4, "far")], (first_out, attn_in_b))
     qkv_b, w_qkv_b, w_out_b = weights.apply(3, attn_in_b, "narrow")
-    first_out, qkv_b, w_out_b = go([(5, "near"), (4, "core_near")], (first_out, qkv_b, w_out_b))
+    first_out, qkv_b, w_out_b = go([(4, "core_near")], (first_out, qkv_b, w_out_b))
     attn_out_b, probs_b = attend(qkv_b, st_strip, st_allowed, 2, joint_len)
     first_out, attn_out_b, w_out_b = go([(4, "core_far")], (first_out, attn_out_b, w_out_b))
     first_out, attn_out_b, w_out_b = go([(5, "far")], (first_out, attn_out_b, w_out_b))
     mixed_b = product(attn_out_b, w_out_b)
-    middle_b = first_out + mod[8] * mixed_b
-    mlp_in_b = modulated_norm(middle_b, mod[9], mod[10])
+    middle_b, mlp_in_b = add_branch(first_out, mixed_b, mod[8], mod[9], mod[10])
     hidden_b, slope_b, w_up_b = weights.apply(4, mlp_in_b, "gelu")
     middle_b, hidden_b, slope_b = go([(5, "core_near"), (5, "core_far")], (middle_b, hidden_b, slope_b))
 
@@ -884,19 +954,18 @@
     out_tokens = joint_ungroup(out_rows).reshape(tokens.shape)
     grad_gate_mb = jnp.sum(grad_out_b * downward_b, axis=0)
     grad_mlp_b = product_turned(grad_up_b, w_up_b)
-    norm_grad, grad_shift_mb, grad_scale_mb = norm_back(grad_mlp_b, middle_b, mod[10])
-    grad_middle_b = grad_out_b + norm_grad
-    grad_mixed_b = (mod[8] * grad_middle_b).astype(jnp.bfloat16)
-    grad_gate_ab = jnp.sum(grad_middle_b * mixed_b, axis=0)
+    grad_middle_b, grad_mixed_b, sums_mb = norm_back(
+        grad_mlp_b, middle_b, grad_out_b, mod[10], mixed_b, mod[8]
+    )
     state = (grad_middle_b, grad_mixed_b)
     state = settle([d_st_up, d_st_down], state)
     grad_middle_b, grad_mixed_b = rounds([d_st_up, d_st_down], state)
     grad_attn_b = product_turned(grad_mixed_b, w_out_b, jnp.bfloat16)
     grad_qkv_b, strip_grad_b = attend_back(
-        qkv_b, probs_b, grad_attn_b, 2, joint_len, *st_strip.shape[1:], (HS, 128 * (2 * FR - 1))
+        qkv_b, probs_b, grad_attn_b, 2, joint_len, *st_strip.shape[1:], (2, 128 * (2 * FR - 1))
     )
-    grad_middle_b, grad_qkv_b, strip_grad_b = hold(
-        [d_st_down], (grad_middle_b, grad_qkv_b, strip_grad_b)
+    grad_middle_b, grad_qkv_b, strip_grad_b, grad_gate_mb = hold(
+        [d_st_down], (grad_middle_b, grad_qkv_b, strip_grad_b, grad_gate_mb)
     )
     d_st_attn = start_grad(
         [attn_in_b, attn_out_b],
@@ -911,10 +980,9 @@
     state = settle([d_st_up], state)
     grad_middle_b, grad_qkv_b, strip_grad_b = rounds([d_st_attn, d_st_up, d_st_down], state)
     grad_in_b = product_turned(grad_qkv_b, w_qkv_b)
-    norm_grad, grad_shift_ab, grad_scale_ab = norm_back(grad_in_b, first_out, mod[7])
-    grad_first = grad_middle_b + norm_grad
-    grad_down_a = (mod[5] * grad_first).astype(jnp.bfloat16)
-    grad_gate_ma = jnp.sum(grad_first * downward_a, axis=0)
+    grad_first, grad_down_a, sums_ab = norm_back(
+        grad_in_b, first_out, grad_middle_b, mod[7], downward_a, mod[5]
+    )
     grad_first, grad_down_a = hold([d_st_attn, d_st_up], (grad_first, grad_down_a))
     d_sp_down = start_grad(
         [hidden_a], [grad_down_a], 1024, (128,), (0,), (0,), [d_st_attn, d_st_up]
@@ -925,76 +993,72 @@
     d_sp_up = start_grad([mlp_in_a], [grad_up_a], 256, (512,), (0,), (0,), [d_sp_down])
     grad_first, grad_up_a = hold([d_sp_up], (grad_first, grad_up_a))
     grad_first, grad_up_a = settle([d_st_attn], (grad_first, grad_up_a))
+    grad_first, grad_up_a = hold([d_sp_up], (grad_first, grad_up_a))
     grad_first, grad_up_a = rounds([d_sp_up, d_st_attn], (grad_first, grad_up_a))
     grad_mlp_a = product_turned(grad_up_a, w_up_a)
-    norm_grad, grad_shift_ma, grad_scale_ma = norm_back(grad_mlp_a, middle_a, mod[4])
-    grad_middle_a = joint_ungroup(grad_first + norm_grad)
+    grad_middle_a, sums_ma = norm_back(grad_mlp_a, middle_a, grad_first, mod[4])
+    grad_middle_a = joint_ungroup(grad_middle_a)
     half_rows = grad_middle_a.reshape(pair_windows, -1, model_width)
     keep_part, send_part = split_halves(half_rows, own_half)
     send_part = send_part.astype(jnp.bfloat16)
-    keep_part, send_part, strip_grad_b = hold(
-        [d_sp_up, d_st_attn], (keep_part, send_part, strip_grad_b)
-    )
+    keep_part, send_part = hold([d_sp_up, d_st_attn], (keep_part, send_part))
     came_part = from_pair(send_part)
-    strip_grad_b = rounds([d_sp_down], strip_grad_b)
+    keep_part = rounds([d_sp_down], keep_part)
     if quick:
         d_st_attn.fold()
         d_sp_up.fold()
-    rounds([d_st_attn], ())
-    st_sum = joint_strip_back(strip_grad_b)
-    keep_part, came_part, st_sum = lax.optimization_barrier((keep_part, came_part, st_sum))
+    keep_part, came_part = rounds([d_st_attn], (keep_part, came_part))
     grad_win = join_windows(keep_part, came_part.astype(jnp.float32), own_half)
     grad_mixed_a = (mod[2] * grad_win).astype(jnp.bfloat16)
     grad_gate_aa = jnp.sum(grad_win * mixed_a, axis=0)
     grad_win, grad_mixed_a = rounds([d_sp_up], (grad_win, grad_mixed_a))
     grad_attn_a = product_turned(grad_mixed_a, w_out_a, jnp.bfloat16)
     grad_qkv_a, strip_grad_a = attend_back(
-        qkv_a, probs_a, grad_attn_a, SLOTS, WS * WS, *sp_strip.shape[1:], sp_strip.shape[1:]
+        qkv_a, probs_a, grad_attn_a, SLOTS, WS * WS, *sp_strip.shape[1:], (2, 2 * WS * WS)
     )
     grad_win, grad_qkv_a, strip_grad_a = settle([d_sp_down], (grad_win, grad_qkv_a, strip_grad_a))
+    grad_win, grad_qkv_a, strip_grad_a = hold([d_st_attn], (grad_win, grad_qkv_a, strip_grad_a))
     grad_win, grad_qkv_a, strip_grad_a = rounds([d_sp_down], (grad_win, grad_qkv_a, strip_grad_a))
     d_sp_attn = start_grad(
         [attn_in_a, attn_out_a], [grad_qkv_a, grad_mixed_a], 256, (384, 128), (0, 0), (0, 1)
     )
-    state = hold([d_sp_attn, d_sp_up, d_sp_down], (grad_win, grad_qkv_a, strip_grad_a, st_sum))
+    state = hold([d_sp_attn, d_sp_up, d_sp_down], (grad_win, grad_qkv_a, strip_grad_a, strip_grad_b))
     if quick:
         d_sp_up.fold()
         d_sp_down.fold()
-    grad_win, grad_qkv_a, strip_grad_a, st_sum = rounds([d_sp_attn, d_sp_up, d_sp_down], state)
+    grad_win, grad_qkv_a, strip_grad_a, strip_grad_b = state
+    tables = jnp.concatenate([strip_grad_a, strip_grad_b], axis=2)
+    table_total = Total(tables, ("core", "z1", "z0", "y", "x"))
+    state = (grad_win, grad_qkv_a)
+    state = rounds([d_sp_attn, d_sp_up, d_sp_down, table_total], state)
+    state = settle([d_sp_attn, d_sp_up], state)
+    grad_win, grad_qkv_a = rounds([d_sp_attn, d_sp_up, table_total], state)
     grad_in_a = product_turned(grad_qkv_a, w_qkv_a)
-    state = (grad_win, grad_in_a, strip_grad_a, st_sum)
-    state = settle([d_sp_attn, d_sp_up], state)
-    grad_win, grad_in_a, strip_grad_a, st_sum = rounds([d_sp_attn, d_sp_up], state)
-    norm_grad, grad_shift_aa, grad_scale_aa = norm_back(grad_in_a, win_input, mod[1])
+    win_sum, sums_aa = norm_back(grad_in_a, win_input, grad_win, mod[1])
+    win_sum, sums_aa = settle([d_sp_attn], (win_sum, sums_aa))
     mod_rows = [
-        grad_shift_aa,
-        grad_scale_aa,
+        sums_aa[0],
+        sums_aa[1],
         grad_gate_aa,
-        grad_shift_ma,
-        grad_scale_ma,
-        grad_gate_ma,
-        grad_shift_ab,
-        grad_scale_ab,
-        grad_gate_ab,
-        grad_shift_mb,
-        grad_scale_mb,
+        sums_ma[0],
+        sums_ma[1],
+        sums_ab[2],
+        sums_ab[0],
+        sums_ab[1],
+        sums_mb[2],
+        sums_mb[0],
+        sums_mb[1],
         grad_gate_mb,
     ]
-    win_sum = grad_win + norm_grad
+    mod_total = Total(jnp.stack(mod_rows, axis=0), ("z1", "z0", "y"))
+    win_sum = rounds([d_sp_attn, table_total], win_sum)
     keep_part, send_part = split_windows(win_sum, own_half)
     send_part = send_part.astype(jnp.bfloat16)
-    sp_sum = spatial_strip_back(strip_grad_a)
-    tables = jnp.concatenate([sp_sum.reshape(-1), st_sum.reshape(-1)])
-    table_total = Total(tables, ("core", "z1", "z0", "y", "x"))
-    mod_total = Total(jnp.stack(mod_rows, axis=0), ("z1", "z0", "y"))
-    keep_part, send_part = settle([d_sp_attn], (keep_part, send_part))
-    keep_part, send_part = rounds([d_sp_attn, table_total, mod_total], (keep_part, send_part))
     keep_part, send_part = settle([d_sp_attn], (keep_part, send_part))
     keep_part, send_part = rounds([d_sp_attn, table_total, mod_total], (keep_part, send_part))
     came_part = from_pair(send_part)
     rounds([table_total, mod_total], ())
-    rounds([table_total], ())
-    rounds([table_total], ())
+    rounds([mod_total], ())
     came_part = came_part.astype(jnp.float32)
     grad_tokens = join_halves(keep_part, came_part, own_half, pair_windows).reshape(tokens.shape)
     if quick:
@@ -1003,8 +1067,8 @@
     else:
         grad_modulation = lax.psum(jnp.stack(mod_rows, axis=0), "win")[None]
         table_sums = lax.psum(table_total.result(), ("clip", "win"))
-    grad_sp_table = table_sums[: sp_table.size].reshape(sp_table.shape)
-    grad_st_table = table_sums[sp_table.size :].reshape(st_table.shape)
+    grad_sp_table = spatial_strip_back(table_sums[:, :, : 2 * WS * WS])
+    grad_st_table = joint_strip_back(table_sums[:, :, 2 * WS * WS :])
     wide = d_st_attn.values
     wide_a = d_sp_attn.values
     out_width = wide.shape[1] // 4

time: 806 us -> 769 us (0.954)
  other arithmetic: 115 us -> 67.4 us
  Pallas kernels: 367 us -> 401 us
  waiting for transfers between devices: 132 us -> 108 us
    pallas_call x0 -> x6, Pallas kernels: none -> 32.9 us  [row_call(): pl.pallas_call(kernel, grid=(2,), out_shape=out_shape, in_specs=[block] *...]
    ppermute x86 -> x82, waiting for transfers between devices: 96.3 us -> 77.2 us  [hop(): lax.ppermute(value, axis, [(i, i ^ mask) for i in range(lax.axis_size(axi...]
    reduce_sum x6 -> x1, other arithmetic: 21.1 us -> 3.32 us  [body(): grad_gate_mb = jnp.sum(grad_out_b * downward_b, axis=0)]
    another operation x12 -> x4, other arithmetic: 21.5 us -> 6.64 us  [go(): a1, b1 = (jnp.stack([a0, a_came]), jnp.stack([b0, b_came]))]
    eq x2 -> x0, other arithmetic: 9.6 us -> none  [the longest x1 8.88 us: joint_onehot(): return (offset == wanted).astype(jnp.float32)]
    squeeze x0 -> x4, local copies, waits for them, and re-layouts: none -> 9.3 us  [go(): a1, b1 = (values[0][0], values[0][1])]
    ppermute x86 -> x82, starting transfers between devices: 64.9 us -> 62.1 us  [hop(): lax.ppermute(value, axis, [(i, i ^ mask) for i in range(lax.axis_size(axi...]
    unnamed x196 -> x148, local copies, waits for them, and re-layouts: 25 us -> 25.3 us
  transfers between devices with their start and end apart: 102 -> 98, of which waited for: 28 -> 27; matrix products, arithmetic and copies ran while one was open for 23% -> 18% of each run, Pallas kernels for 38% -> 45%
where the time goes in v3:
time: 769 us; the launch traced here: 763 us
  Pallas kernels  401 us (52%)
  waiting for transfers between devices  108 us (14%)
  local copies, waits for them, and re-layouts  86.2 us (11%)
  starting transfers between devices  69.8 us (9%)
  other arithmetic  67.4 us (9%)
  between operations  17.3 us (2%)
  matrix products  12.8 us (2%)
    pallas_call x10, Pallas kernels, tiled(): pl.pallas_call(kernel, grid=(total // columns,), out_shape=jax.ShapeDtype...  81.9 us
    pallas_call x6, Pallas kernels, weight_grad(): pl.pallas_call(partial(grad_kernel, rows=rows, widths=widths, sources=sou...  81.6 us
    ppermute x82, waiting for transfers between devices, hop(): lax.ppermute(value, axis, [(i, i ^ mask) for i in range(lax.axis_size(axi...  77.2 us
    pallas_call x6, Pallas kernels, gathered(): pl.pallas_call(partial(gathered_kernel, rows=rows, widths=widths, kind=ki...  77 us
    ppermute x82, starting transfers between devices, hop(): lax.ppermute(value, axis, [(i, i ^ mask) for i in range(lax.axis_size(axi...  62.1 us
    pallas_call x13, Pallas kernels, fold(): pl.pallas_call(fold.kernel, out_shape=[fold.gives_part.shape(self.values[...  49.8 us
    pallas_call x2, Pallas kernels, attend_back(): pl.pallas_call(partial(attend_back_kernel, wins=wins, length=length, rows...  46.7 us
    pallas_call x6, Pallas kernels, row_call(): pl.pallas_call(kernel, grid=(2,), out_shape=out_shape, in_specs=[block] *...  32.9 us
  transfers between devices with their start and end apart: 98, of which 27 were waited for; matrix products, arithmetic and copies ran while one was open for 18% of the time, Pallas kernels for 45%

profile of v3, /device:TPU:0, one launch (start us, length us, event | category | flops | bytes accessed | tf_op | source)
XLA Modules:
  0.0 762.8 jit_solution(2176478948602572127)
XLA Ops:
  17.6 14.4 %collective-permute-done = bf16[3,128,1024]{2,1,0:T(8,128)(2,1)S(1)} collective-permute-done((bf16[3,128,1024]{2,1,0:T(8,128)(2,1)S(1)}, bf16[3,128,1024]{2,1,0:T(8,128)(2,1)S(1)}, u32[]{:S(2)}, u32[]{:S(2)}) %collective-permute-start) | collective-permute-done | bytes 786464 | tf_op jit(solution)/shard_map/ppermute | solution.py:752
  102.5 11.7 %gathered.6 = (bf16[768,3072]{1,0:T(8,128)(2,1)}, bf16[1024,3072]{1,0:T(8,128)(2,1)}, bf16[1024,1024]{1,0:T(8,128)(2,1)}) custom-call(s32[4]{0:T(128)} %pad_add_fusion.row_of, s32[2]{0:T(128)} %pad_add_fusion.1.y_of, bf16[768,1024]{1,0:T(8,128)(2,1)} %add_convert_fusion.x_ref.refs_0_, bf16[2,4,128,512]{3,2,1,0:T(8,128)(2,1)} %pad_maximum_fusion.3.refs_0_, ...), custom_call_target="tpu_custom_call" | custom-call | flops 1 | bytes 1 | tf_op jit(solution)/shard_map/gathered/pallas_call | solution.py:156
  118.7 13.4 %attend.2 = (bf16[768,1024]{1,0:T(8,128)(2,1)}, bf16[16,3,256,256]{3,2,1,0:T(8,128)(2,1)}) custom-call(bf16[768,3072]{1,0:T(8,128)(2,1)} %get-tuple-element.444.q_ref.k_ref.v_ref, bf16[768,3072]{1,0:T(8,128)(2,1)} %get-tuple-element.444.q_ref.k_ref.v_ref, bf16[768,3072]{1,0:T(8,128)(2,1)} %get-tuple-element.444.q_ref.k_ref.v_ref, ...), custom_call_target="tpu_custom_call" | custom-call | flops 1 | bytes 1 | tf_op jit(solution)/shard_map/attend/pallas_call | solution.py:492
  181.2 14.9 %gathered.7 = (bf16[640,4096]{1,0:T(8,128)(2,1)}, bf16[640,4096]{1,0:T(8,128)(2,1)}, bf16[1024,4096]{1,0:T(8,128)(2,1)}) custom-call(s32[4]{0:T(128)} %pad_add_fusion.row_of, s32[2]{0:T(128)} %pad_add_fusion.1.y_of, bf16[640,1024]{1,0:T(8,128)(2,1)} %add_convert_fusion.1.x_ref.refs_0_, bf16[2,4,128,512]{3,2,1,0:T(8,128)(2,1)} %pad_maximum_fusion.5.refs_0_, ...), custom_call_target="tpu_custom_call" | custom-call | flops 1 | bytes 1 | tf_op jit(solution)/shard_map/gathered/pallas_call | solution.py:156
  202.2 12.0 %gathered.8 = (f32[640,1024]{1,0:T(8,128)}, bf16[4096,1024]{1,0:T(8,128)(2,1)}) custom-call(s32[4]{0:T(128)} %pad_add_fusion.row_of, s32[2]{0:T(128)} %pad_add_fusion.1.y_of, bf16[640,4096]{1,0:T(8,128)(2,1)} %get-tuple-element.471.x_ref.refs_0_, bf16[2,4,512,128]{3,2,1,0:T(8,128)(2,1)} %get-tuple-element.829.refs_0_, ...), custom_call_target="tpu_custom_call" | custom-call | flops 1 | bytes 1 | tf_op jit(solution)/shard_map/gathered/pallas_call | solution.py:156
  230.1 11.0 %gathered.9 = (bf16[640,3072]{1,0:T(8,128)(2,1)}, bf16[1024,3072]{1,0:T(8,128)(2,1)}, bf16[1024,1024]{1,0:T(8,128)(2,1)}) custom-call(s32[4]{0:T(128)} %pad_add_fusion.row_of, s32[2]{0:T(128)} %pad_add_fusion.1.y_of, bf16[640,1024]{1,0:T(8,128)(2,1)} %get-tuple-element.483.x_ref.refs_0_, bf16[2,4,128,512]{3,2,1,0:T(8,128)(2,1)} %get-tuple-element.484.refs_0_, ...), custom_call_target="tpu_custom_call" | custom-call | flops 1 | bytes 1 | tf_op jit(solution)/shard_map/gathered/pallas_call | solution.py:156
  241.6 17.6 %attend.3 = (bf16[640,1024]{1,0:T(8,128)(2,1)}, bf16[16,2,320,320]{3,2,1,0:T(8,128)(2,1)}) custom-call(bf16[640,3072]{1,0:T(8,128)(2,1)} %get-tuple-element.491.q_ref.k_ref.v_ref, bf16[640,3072]{1,0:T(8,128)(2,1)} %get-tuple-element.491.q_ref.k_ref.v_ref, bf16[640,3072]{1,0:T(8,128)(2,1)} %get-tuple-element.491.q_ref.k_ref.v_ref, ...), custom_call_target="tpu_custom_call" | custom-call | flops 1 | bytes 1 | tf_op jit(solution)/shard_map/attend/pallas_call | solution.py:492
  277.1 14.7 %gathered.10 = (bf16[640,4096]{1,0:T(8,128)(2,1)}, bf16[640,4096]{1,0:T(8,128)(2,1)}, bf16[1024,4096]{1,0:T(8,128)(2,1)}) custom-call(s32[4]{0:T(128)} %pad_add_fusion.row_of, s32[2]{0:T(128)} %pad_add_fusion.1.y_of, bf16[640,1024]{1,0:T(8,128)(2,1)} %get-tuple-element.504.x_ref.refs_0_, bf16[2,4,128,512]{3,2,1,0:T(8,128)(2,1)} %copy-done.16, ...), custom_call_target="tpu_custom_call" | custom-call | flops 1 | bytes 1 | tf_op jit(solution)/shard_map/gathered/pallas_call | solution.py:156
  291.9 13.2 %weight_grad.6 = (bf16[2,2,2,4,512,128]{5,4,3,2,1,0:T(8,128)(2,1)}, bf16[2,2,2,4,512,128]{5,4,3,2,1,0:T(8,128)(2,1)}) custom-call(s32[4]{0:T(128)} %pad_add_fusion.row_of, s32[2]{0:T(128)} %pad_add_fusion.1.y_of, bf16[640,4096]{1,0:T(8,128)(2,1)} %get-tuple-element.516.refs_0_.x_ref, bf16[640,1024]{1,0:T(8,128)(2,1)} %multiply_convert_fusion.1.refs_1_.left), custom_call_target="tpu_custom_call" | custom-call | flops 1 | bytes 1 | tf_op jit(solution)/shard_map/weight_grad/pallas_call | solution.py:326
  318.9 12.6 %gathered.11 = (f32[640,1024]{1,0:T(8,128)}, bf16[4096,1024]{1,0:T(8,128)(2,1)}) custom-call(s32[4]{0:T(128)} %pad_add_fusion.row_of, s32[2]{0:T(128)} %pad_add_fusion.1.y_of, bf16[640,4096]{1,0:T(8,128)(2,1)} %get-tuple-element.516.refs_0_.x_ref, bf16[2,4,512,128]{3,2,1,0:T(8,128)(2,1)} %copy-done.22, bf16[2,4,512,128]{3,2,1,0:T(8,128)(2,1)} %copy-done.38, ...), custom_call_target="tpu_custom_call" | custom-call | flops 1 | bytes 1 | tf_op jit(solution)/shard_map/gathered/pallas_call | solution.py:156
  331.5 11.5 %product.12.refs_1_.left = bf16[640,4096]{1,0:T(8,128)(2,1)} custom-call(bf16[640,1024]{1,0:T(8,128)(2,1)} %multiply_convert_fusion.1.refs_1_.left, bf16[4096,1024]{1,0:T(8,128)(2,1)} %get-tuple-element.521.right, bf16[640,4096]{1,0:T(8,128)(2,1)} %get-tuple-element.522.factor), custom_call_target="tpu_custom_call" | custom-call | flops 1 | bytes 1 | tf_op jit(solution)/shard_map/product/pallas_call | solution.py:195
  344.9 13.8 %weight_grad.7 = (bf16[2,2,2,4,128,512]{5,4,3,2,1,0:T(8,128)(2,1)}, bf16[2,2,2,4,128,512]{5,4,3,2,1,0:T(8,128)(2,1)}, bf16[2,4,512,128]{3,2,1,0:T(8,128)(2,1)}, ...) custom-call(s32[4]{0:T(128)} %pad_add_fusion.row_of, ...), custom_call_target="tpu_custom_call" | custom-call | flops 1 | bytes 1 | tf_op jit(solution)/shard_map/weight_grad/pallas_call | solution.py:326
  361.2 10.6 %product.13.grad_in = f32[640,1024]{1,0:T(8,128)} custom-call(bf16[640,4096]{1,0:T(8,128)(2,1)} %product.12.refs_1_.left, bf16[1024,4096]{1,0:T(8,128)(2,1)} %get-tuple-element.534.right), custom_call_target="tpu_custom_call" | custom-call | flops 1 | bytes 1 | tf_op jit(solution)/shard_map/product/pallas_call | solution.py:195
  409.4 23.6 %attend_back.2 = (bf16[640,3072]{1,0:T(8,128)(2,1)}, f32[16,2,1152]{2,1,0:T(2,128)}) custom-call(bf16[640,3072]{1,0:T(8,128)(2,1)} %get-tuple-element.491.q_ref.k_ref.v_ref, bf16[640,3072]{1,0:T(8,128)(2,1)} %get-tuple-element.491.q_ref.k_ref.v_ref, bf16[640,3072]{1,0:T(8,128)(2,1)} %get-tuple-element.491.q_ref.k_ref.v_ref, ...), custom_call_target="tpu_custom_call" | custom-call | flops 1 | bytes 1 | tf_op jit(solution)/shard_map/attend_back/pallas_call | solution.py:596
  434.3 12.7 %weight_grad.8 = (bf16[2,2,2,4,128,512]{5,4,3,2,1,0:T(8,128)(2,1)}, bf16[2,2,2,4,128,512]{5,4,3,2,1,0:T(8,128)(2,1)}, bf16[4,2,512,128]{3,2,1,0:T(8,128)(2,1)}) custom-call(s32[4]{0:T(128)} %pad_add_fusion.row_of, s32[2]{0:T(128)} %pad_add_fusion.1.y_of, bf16[640,1024]{1,0:T(8,128)(2,1)} %get-tuple-element.483.x_ref.refs_0_, ...), custom_call_target="tpu_custom_call" | custom-call | flops 1 | bytes 1 | tf_op jit(solution)/shard_map/weight_grad/pallas_call | solution.py:326
  472.2 15.7 %weight_grad.9 = (bf16[2,2,2,4,512,128]{5,4,3,2,1,0:T(8,128)(2,1)}, bf16[2,2,2,4,512,128]{5,4,3,2,1,0:T(8,128)(2,1)}, bf16[2,4,128,512]{3,2,1,0:T(8,128)(2,1)}, ...) custom-call(s32[4]{0:T(128)} %pad_add_fusion.row_of, ...), custom_call_target="tpu_custom_call" | custom-call | flops 1 | bytes 1 | tf_op jit(solution)/shard_map/weight_grad/pallas_call | solution.py:326
  490.0 11.5 %product.16.refs_1_.left = bf16[640,4096]{1,0:T(8,128)(2,1)} custom-call(bf16[640,1024]{1,0:T(8,128)(2,1)} %get-tuple-element.625.refs_1_.left, bf16[4096,1024]{1,0:T(8,128)(2,1)} %get-tuple-element.626.right, bf16[640,4096]{1,0:T(8,128)(2,1)} %get-tuple-element.627.factor), custom_call_target="tpu_custom_call" | custom-call | flops 1 | bytes 1 | tf_op jit(solution)/shard_map/product/pallas_call | solution.py:195
  503.4 14.0 %weight_grad.10 = (bf16[2,2,2,4,128,512]{5,4,3,2,1,0:T(8,128)(2,1)}, bf16[2,2,2,4,128,512]{5,4,3,2,1,0:T(8,128)(2,1)}, bf16[2,4,512,128]{3,2,1,0:T(8,128)(2,1)},...) custom-call(s32[4]{0:T(128)} %pad_add_fusion.row_of, ...), custom_call_target="tpu_custom_call" | custom-call | flops 1 | bytes 1 | tf_op jit(solution)/shard_map/weight_grad/pallas_call | solution.py:326
  523.0 10.5 %product.17.grad_in = f32[640,1024]{1,0:T(8,128)} custom-call(bf16[640,4096]{1,0:T(8,128)(2,1)} %product.16.refs_1_.left, bf16[1024,4096]{1,0:T(8,128)(2,1)} %get-tuple-element.659.right), custom_call_target="tpu_custom_call" | custom-call | flops 1 | bytes 1 | tf_op jit(solution)/shard_map/product/pallas_call | solution.py:195
  546.7 15.4 %collective-permute-done.63 = bf16[3,128,1024]{2,1,0:T(8,128)(2,1)S(1)} collective-permute-done((bf16[3,128,1024]{2,1,0:T(8,128)(2,1)S(1)}, bf16[3,128,1024]{2,1,0:T(8,128)(2,1)S(1)}, u32[]{:S(2)}, u32[]{:S(2)}) %collective-permute-start.63) | collective-permute-done | bytes 786464 | tf_op jit(solution)/shard_map/ppermute | solution.py:752
  582.1 23.1 %attend_back.3 = (bf16[768,3072]{1,0:T(8,128)(2,1)}, f32[16,2,512]{2,1,0:T(2,128)}) custom-call(bf16[768,3072]{1,0:T(8,128)(2,1)} %get-tuple-element.444.q_ref.k_ref.v_ref, bf16[768,3072]{1,0:T(8,128)(2,1)} %get-tuple-element.444.q_ref.k_ref.v_ref, bf16[768,3072]{1,0:T(8,128)(2,1)} %get-tuple-element.444.q_ref.k_ref.v_ref, bf16[768,1024]{1,0:T(8,128)(2,1)} %product.18.g_ref, ...), custom_call_target="tpu_custom_call" | custom-call | flops 1 | bytes 1 | tf_op jit(solution)/shard_map/attend_back/pallas_call | solution.py:596
  613.6 12.3 %weight_grad.11 = (bf16[2,2,2,4,128,512]{5,4,3,2,1,0:T(8,128)(2,1)}, bf16[2,2,2,4,128,512]{5,4,3,2,1,0:T(8,128)(2,1)}) custom-call(s32[4]{0:T(128)} %pad_add_fusion.row_of, s32[2]{0:T(128)} %pad_add_fusion.1.y_of, bf16[768,1024]{1,0:T(8,128)(2,1)} %add_convert_fusion.x_ref.refs_0_, bf16[768,1024]{1,0:T(8,128)(2,1)} %get-tuple-element.450.left.refs_1_, ...), custom_call_target="tpu_custom_call" | custom-call | flops 1 | bytes 1 | tf_op jit(solution)/shard_map/weight_grad/pallas_call | solution.py:326
  668.5 10.3 %product.19.grad_in = f32[768,1024]{1,0:T(8,128)} custom-call(bf16[768,3072]{1,0:T(8,128)(2,1)} %get-tuple-element.764.refs_2_.left, bf16[1024,3072]{1,0:T(8,128)(2,1)} %get-tuple-element.765.right), custom_call_target="tpu_custom_call" | custom-call | flops 1 | bytes 1 | tf_op jit(solution)/shard_map/product/pallas_call | solution.py:195
  720.9 10.9 %collective-permute-done.81 = f32[416,128]{1,0:T(8,128)S(1)} collective-permute-done((f32[416,128]{1,0:T(8,128)S(1)}, f32[416,128]{1,0:T(8,128)S(1)}, u32[]{:S(2)}, u32[]{:S(2)}) %collective-permute-start.81) | collective-permute-done | bytes 213024 | tf_op jit(solution)/shard_map/ppermute | solution.py:35
  (508 shorter events, 414.1 us)
Async XLA Ops:
  7.2 46.6 %all-gather.17.cloned.1.call-start = ((), (), s32[]{:S(2)}) async-start(), calls=%async_computation.11 | async-start | bytes 1310720 | tf_op jit(solution)/shard_map/all_gather | solution.py:48
  10.1 83.5 %all-gather.15.cloned.1.call-start = ((), (), s32[]{:S(2)}) async-start(), calls=%async_computation.10 | async-start | bytes 1310720 | tf_op jit(solution)/shard_map/all_gather | solution.py:48
  15.2 129.2 %all-gather.13.cloned.1.call-start = ((), (), s32[]{:S(2)}) async-start(), calls=%async_computation.9 | async-start | bytes 2621440 | tf_op jit(solution)/shard_map/all_gather | solution.py:48
  42.4 154.3 %all-gather.11.cloned.1.call-start = ((), (), s32[]{:S(2)}) async-start(), calls=%async_computation.8 | async-start | bytes 2621440 | tf_op jit(solution)/shard_map/all_gather | solution.py:48
  50.5 175.6 %all-gather.9.cloned.1.call-start = ((), (), s32[]{:S(2)}) async-start(), calls=%async_computation.7 | async-start | bytes 2621440 | tf_op jit(solution)/shard_map/all_gather | solution.py:48
  77.0 184.1 %all-gather.7.cloned.1.call-start = ((), (), s32[]{:S(2)}) async-start(), calls=%async_computation.6 | async-start | bytes 2621440 | tf_op jit(solution)/shard_map/all_gather | solution.py:48
  143.8 466.6 %reduce-scatter.7.cloned.1.call-start = ((), (), s32[]{:S(2)}) async-start(), calls=%async_computation.12 | async-start | bytes 1310720 | tf_op jit(solution)/shard_map/reduce_scatter | solution.py:377
  147.5 48.6 %collective-permute-start.18 = (bf16[2,4,512,128]{3,2,1,0:T(8,128)(2,1)}, bf16[2,4,512,128]{3,2,1,0:T(8,128)(2,1)}, u32[]{:S(2)}, u32[]{:S(2)}) collective-permute-start(bf16[2,4,512,128]{3,2,1,0:T(8,128)(2,1)} %get-tuple-element.828.refs_4_), channel_id=1, source_target_pairs={{0,1},{1,0},{2,3},{3,2},{4,5},{5,4},{6,7},{7,6},{8,9},{9,8},{10,11... | collective-permute-start | bytes 3145736 | tf_op jit(solution)/shard_map/ppermute | solution.py:35
  148.4 47.7 %collective-permute-start.17 = (bf16[2,4,512,128]{3,2,1,0:T(8,128)(2,1)}, bf16[2,4,512,128]{3,2,1,0:T(8,128)(2,1)}, u32[]{:S(2)}, u32[]{:S(2)}) collective-permute-start(bf16[2,4,512,128]{3,2,1,0:T(8,128)(2,1)} %get-tuple-element.829.refs_0_), channel_id=1, source_target_pairs={{0,16},{8,24},{16,0},{24,8},{1,17},{9,25},{17,1},{25,9},{2,18},{10... | collective-permute-start | bytes 3145736 | tf_op jit(solution)/shard_map/ppermute | solution.py:35
  241.3 35.8 %collective-permute-start.40 = (bf16[2,4,128,512]{3,2,1,0:T(8,128)(2,1)S(1)}, bf16[2,4,128,512]{3,2,1,0:T(8,128)(2,1)}, u32[]{:S(2)}, u32[]{:S(2)}) collective-permute-start(bf16[2,4,128,512]{3,2,1,0:T(8,128)(2,1)S(1)} %get-tuple-element.507.refs_4_), channel_id=1, source_target_pairs={{0,8},{8,0},{16,24},{24,16},{1,9},{9,1},{17,25},{25,17},{2,10},{10... | collective-permute-start | bytes 3145736 | tf_op jit(solution)/shard_map/ppermute | solution.py:35
  305.1 37.9 %collective-permute-start.46 = (bf16[2,2,2,4,512,128]{5,4,3,2,1,0:T(8,128)(2,1)}, bf16[2,2,2,4,512,128]{5,4,3,2,1,0:T(8,128)(2,1)S(1)}, u32[]{:S(2)}, u32[]{:S(2)}) collective-permute-start(bf16[2,2,2,4,512,128]{5,4,3,2,1,0:T(8,128)(2,1)} %get-tuple-element.524), channel_id=1, source_target_pairs={{0,8},{8,0},{16,24},{24,16},{1,9},{9,1},{17,25},{25,17},{2,10},{10... | collective-permute-start | bytes 12582920 | tf_op jit(solution)/shard_map/ppermute | solution.py:35
  397.7 49.3 %collective-permute-start.52 = (bf16[2,4,128,512]{3,2,1,0:T(8,128)(2,1)}, bf16[2,4,128,512]{3,2,1,0:T(8,128)(2,1)S(1)}, u32[]{:S(2)}, u32[]{:S(2)}) collective-permute-start(bf16[2,4,128,512]{3,2,1,0:T(8,128)(2,1)} %get-tuple-element.583), channel_id=1, source_target_pairs={{0,16},{8,24},{16,0},{24,8},{1,17},{9,25},{17,1},{25,9},{2,18},{10... | collective-permute-start | bytes 3145736 | tf_op jit(solution)/shard_map/ppermute | solution.py:35
  398.3 48.7 %collective-permute-start.53 = (bf16[2,4,128,512]{3,2,1,0:T(8,128)(2,1)}, bf16[2,4,128,512]{3,2,1,0:T(8,128)(2,1)S(1)}, u32[]{:S(2)}, u32[]{:S(2)}) collective-permute-start(bf16[2,4,128,512]{3,2,1,0:T(8,128)(2,1)} %get-tuple-element.585), channel_id=1, source_target_pairs={{0,1},{1,0},{2,3},{3,2},{4,5},{5,4},{6,7},{7,6},{8,9},{9,8},{10,11... | collective-permute-start | bytes 3145736 | tf_op jit(solution)/shard_map/ppermute | solution.py:35
  399.7 33.8 %collective-permute-start.50 = (bf16[4,512,128]{2,1,0:T(8,128)(2,1)}, bf16[4,512,128]{2,1,0:T(8,128)(2,1)S(1)}, u32[]{:S(2)}, u32[]{:S(2)}) collective-permute-start(bf16[4,512,128]{2,1,0:T(8,128)(2,1)} %get-tuple-element.565), channel_id=1, source_target_pairs={{0,1},{1,0},{2,3},{3,2},{4,5},{5,4},{6,7},{7,6},{8,9},{9,8},{10,11... | collective-permute-start | bytes 1572872 | tf_op jit(solution)/shard_map/ppermute | solution.py:35
  562.1 172.6 %reduce-scatter.17.cloned.1.call-start = ((), (), s32[]{:S(2)}) async-start(), calls=%async_computation.17 | async-start | bytes 1310720 | tf_op jit(solution)/shard_map/reduce_scatter | solution.py:377
  562.9 173.7 %reduce-scatter.15.cloned.1.call-start = ((), (), s32[]{:S(2)}) async-start(), calls=%async_computation.16 | async-start | bytes 1310720 | tf_op jit(solution)/shard_map/reduce_scatter | solution.py:377
  562.9 42.3 %collective-permute-start.64 = (bf16[2,4,512,128]{3,2,1,0:T(8,128)(2,1)}, bf16[2,4,512,128]{3,2,1,0:T(8,128)(2,1)S(1)}, u32[]{:S(2)}, u32[]{:S(2)}) collective-permute-start(bf16[2,4,512,128]{3,2,1,0:T(8,128)(2,1)} %get-tuple-element.693), channel_id=1, source_target_pairs={{0,16},{8,24},{16,0},{24,8},{1,17},{9,25},{17,1},{25,9},{2,18},{10... | collective-permute-start | bytes 3145736 | tf_op jit(solution)/shard_map/ppermute | solution.py:35
  564.4 40.8 %collective-permute-start.65 = (bf16[2,4,512,128]{3,2,1,0:T(8,128)(2,1)}, bf16[2,4,512,128]{3,2,1,0:T(8,128)(2,1)S(1)}, u32[]{:S(2)}, u32[]{:S(2)}) collective-permute-start(bf16[2,4,512,128]{3,2,1,0:T(8,128)(2,1)} %get-tuple-element.695), channel_id=1, source_target_pairs={{0,1},{1,0},{2,3},{3,2},{4,5},{5,4},{6,7},{7,6},{8,9},{9,8},{10,11... | collective-permute-start | bytes 3145736 | tf_op jit(solution)/shard_map/ppermute | solution.py:35
  575.2 50.7 %collective-permute-start.66 = (bf16[2,4,128,512]{3,2,1,0:T(8,128)(2,1)}, bf16[2,4,128,512]{3,2,1,0:T(8,128)(2,1)}, u32[]{:S(2)}, u32[]{:S(2)}) collective-permute-start(bf16[2,4,128,512]{3,2,1,0:T(8,128)(2,1)} %get-tuple-element.718), channel_id=1, source_target_pairs={{0,16},{8,24},{16,0},{24,8},{1,17},{9,25},{17,1},{25,9},{2,18},{10... | collective-permute-start | bytes 3145736 | tf_op jit(solution)/shard_map/ppermute | solution.py:35
  576.6 49.3 %collective-permute-start.67 = (bf16[2,4,128,512]{3,2,1,0:T(8,128)(2,1)}, bf16[2,4,128,512]{3,2,1,0:T(8,128)(2,1)}, u32[]{:S(2)}, u32[]{:S(2)}) collective-permute-start(bf16[2,4,128,512]{3,2,1,0:T(8,128)(2,1)} %get-tuple-element.720), channel_id=1, source_target_pairs={{0,1},{1,0},{2,3},{3,2},{4,5},{5,4},{6,7},{7,6},{8,9},{9,8},{10,11... | collective-permute-start | bytes 3145736 | tf_op jit(solution)/shard_map/ppermute | solution.py:35
  635.2 106.8 %reduce-scatter.13.cloned.1.call-start = ((), (), s32[]{:S(2)}) async-start(), calls=%async_computation.15 | async-start | bytes 1310720 | tf_op jit(solution)/shard_map/reduce_scatter | solution.py:377
  635.8 111.4 %reduce-scatter.11.cloned.1.call-start = ((), (), s32[]{:S(2)}) async-start(), calls=%async_computation.14 | async-start | bytes 1310720 | tf_op jit(solution)/shard_map/reduce_scatter | solution.py:377
  660.0 92.3 %reduce-scatter.9.cloned.1.call-start = ((), (), s32[]{:S(2)}) async-start(), calls=%async_computation.13 | async-start | bytes 1310720 | tf_op jit(solution)/shard_map/reduce_scatter | solution.py:377
  710.1 38.9 %collective-permute-start.80 = (bf16[3,128,1024]{2,1,0:T(8,128)(2,1)}, bf16[3,128,1024]{2,1,0:T(8,128)(2,1)}, u32[]{:S(2)}, u32[]{:S(2)}) collective-permute-start(bf16[3,128,1024]{2,1,0:T(8,128)(2,1)} %select_convert_fusion), channel_id=1, source_target_pairs={{0,1},{1,0},{2,3},{3,2},{4,5},{5,4},{6,7},{7,6},{8,9},{9,8},{10,11... | collective-permute-start | bytes 2359304 | tf_op jit(solution)/shard_map/ppermute | solution.py:752
  (148 other events, 1709.2 us)
Sparse Core Ops, SparseCore 0:
  10.2 30.6 all-gather.16
  43.0 27.4 all-gather.14
  72.6 45.3 all-gather.12
  120.0 44.6 all-gather.10
  166.1 44.6 all-gather.8
  212.8 44.6 all-gather.6
  562.2 27.4 reduce-scatter.6
  592.1 25.7 reduce-scatter.16
  635.3 27.5 reduce-scatter.14
  665.1 28.1 reduce-scatter.12
  695.6 26.4 reduce-scatter.10
  724.3 26.9 reduce-scatter.8

commit v4 on v3

--- a/solution.py
+++ b/solution.py
@@ -16,7 +16,7 @@
 PAIR_LOCS = 1
 HS = 8
 SLOTS = 3
-VMEM_BYTES = 56 * 1024 * 1024
+MIB = 1024 * 1024
 
 SMALL = pl.CostEstimate(flops=1, bytes_accessed=1, transcendentals=0)
 
@@ -165,7 +165,7 @@
         + [pl.BlockSpec(memory_space=pl.ANY)] * len(widths),
         scratch_shapes=[pltpu.VMEM(shape, jnp.bfloat16) for shape in shapes]
         + [pltpu.SemaphoreType.DMA((64 * len(widths),)), pltpu.SemaphoreType.DMA((4 * len(widths),))],
-        compiler_params=pltpu.CompilerParams(vmem_limit_bytes=VMEM_BYTES),
+        compiler_params=pltpu.CompilerParams(vmem_limit_bytes=56 * MIB),
         cost_estimate=SMALL,
         name="gathered",
     )(place["rows"], place["cols"], x, *values)
@@ -198,7 +198,7 @@
         out_shape=jax.ShapeDtypeStruct((count, total), kept),
         in_specs=[pl.BlockSpec(left.shape, lambda i: (0, 0)), right_spec] + [block] * len(factors),
         out_specs=block,
-        compiler_params=pltpu.CompilerParams(vmem_limit_bytes=VMEM_BYTES),
+        compiler_params=pltpu.CompilerParams(vmem_limit_bytes=56 * MIB),
         cost_estimate=SMALL,
         name="product",
     )(left, right, *factors)
@@ -336,7 +336,7 @@
         + old_specs,
         out_specs=out_specs,
         scratch_shapes=[pltpu.VMEM((4 * rows, count), jnp.bfloat16)] * len(xs),
-        compiler_params=pltpu.CompilerParams(vmem_limit_bytes=VMEM_BYTES),
+        compiler_params=pltpu.CompilerParams(vmem_limit_bytes=56 * MIB),
         cost_estimate=SMALL,
         name="weight_grad",
     )(place["rows"], place["cols"], *xs, *dys, *old_values)
@@ -357,7 +357,7 @@
         outs = pl.pallas_call(
             fold.kernel,
             out_shape=[fold.gives_part.shape(self.values[0].shape[-2:])] * fold.gives,
-            compiler_params=pltpu.CompilerParams(vmem_limit_bytes=VMEM_BYTES),
+            compiler_params=pltpu.CompilerParams(vmem_limit_bytes=16 * MIB),
             cost_estimate=SMALL,
             name=fold.kernel.__name__,
         )(*self.values)
@@ -461,14 +461,14 @@
     rows, lanes = strip_ref.shape[1:]
     blocks = length // rows
     masks = mask_ref.shape[0]
+    mixed = [None] * wins
     for head in range(2):
         strip = strip_ref[head]
         for block in range(blocks):
             offset = (blocks - 1 - block) * rows
             turned = strip if offset == 0 else pltpu.roll(strip, lanes - offset, 1)
             bias[block * rows : (block + 1) * rows, :] = turned[:, :length]
-        chosen = head_lanes(head)
-        low = chosen.astype(jnp.bfloat16)
+        low = head_lanes(head).astype(jnp.bfloat16)
         for win in range(wins):
             here = slice(win * length, (win + 1) * length)
             queries = q_ref[here, :] * jnp.bfloat16(0.125)
@@ -478,11 +478,11 @@
             probs = raised * (1.0 / jnp.sum(raised, axis=0, keepdims=True))
             probs = probs.astype(jnp.bfloat16)
             probs_ref[head, win] = probs
-            mixed = lax.dot_general(probs, v_ref[here, :] * low, TN, preferred_element_type=jnp.float32)
-            if head == 0:
-                out_ref[here, :] = mixed.astype(jnp.bfloat16)
-            else:
-                out_ref[here, :] = out_ref[here, :] + mixed.astype(jnp.bfloat16)
+            turned = (v_ref[here, :] * low).T
+            part = jnp.dot(turned, probs, preferred_element_type=jnp.float32)
+            mixed[win] = part if head == 0 else mixed[win] + part
+    for win in range(wins):
+        out_ref[win * length : (win + 1) * length, :] = mixed[win].T.astype(jnp.bfloat16)
 
 
 def attend(qkv, strip, allowed, wins, length):
@@ -508,7 +508,7 @@
             pl.BlockSpec((2, wins, length, length), lambda h: (h, 0, 0, 0)),
         ],
         scratch_shapes=[pltpu.VMEM((length, length), jnp.float32)],
-        compiler_params=pltpu.CompilerParams(vmem_limit_bytes=VMEM_BYTES),
+        compiler_params=pltpu.CompilerParams(vmem_limit_bytes=56 * MIB),
         cost_estimate=SMALL,
         name="attend",
     )(qkv, qkv, qkv, strip, allowed)
@@ -520,7 +520,7 @@
     blocks = length // rows
     width = out_ref.shape[1] // 3
     step = pl.program_id(0)
-    grads = [[None] * 3 for _ in range(wins)]
+    query_grads = [None] * wins
     total[...] = jnp.zeros_like(total)
     for head in range(2):
         chosen = head_lanes(head)
@@ -539,12 +539,19 @@
                 total[:, :length] = grad_scores.astype(jnp.float32)
             else:
                 total[:, :length] = total[:, :length] + grad_scores.astype(jnp.float32)
+            part = jnp.dot((key_rows * low).T, grad_scores, preferred_element_type=jnp.float32)
+            if head == 0:
+                query_grads[win] = part
+            else:
+                column = pl.multiple_of(step * 128, 128)
+                both = (query_grads[win] + part) * 0.125
+                out_ref[here, pl.ds(column, 128)] = both.T.astype(jnp.bfloat16)
             new = (
-                lax.dot_general(grad_scores, key_rows, TN, preferred_element_type=jnp.float32) * 0.125,
+                None,
                 jnp.dot(grad_scores, queries, preferred_element_type=jnp.float32),
                 jnp.dot(probs, outer, preferred_element_type=jnp.float32),
             )
-            for kind in range(3):
+            for kind in range(1, 3):
                 column = pl.multiple_of(step * 128 + kind * width, 128)
                 if head == 0:
                     out_ref[here, pl.ds(column, 128)] = (new[kind] * chosen).astype(jnp.bfloat16)
@@ -612,7 +619,7 @@
             pl.BlockSpec((2,) + strip, lambda h: (h, 0, 0)),
         ],
         scratch_shapes=[pltpu.VMEM((length, lanes), jnp.float32)],
-        compiler_params=pltpu.CompilerParams(vmem_limit_bytes=VMEM_BYTES),
+        compiler_params=pltpu.CompilerParams(vmem_limit_bytes=56 * MIB),
         cost_estimate=SMALL,
         name="attend_back",
     )(qkv, qkv, qkv, grad_out, probs)
@@ -644,7 +651,7 @@
         out_shape=out_shape,
         in_specs=[block] * len(wide) + [whole] * len(vectors),
         out_specs=out_specs,
-        compiler_params=pltpu.CompilerParams(vmem_limit_bytes=VMEM_BYTES),
+        compiler_params=pltpu.CompilerParams(vmem_limit_bytes=56 * MIB),
         cost_estimate=SMALL,
         name=name,
     )(*wide, *[vector.reshape(1, width) for vector in vectors])

time: 769 us -> 748 us (0.973)
  Pallas kernels: 401 us -> 359 us
  waiting for transfers between devices: 108 us -> 121 us
  local copies, waits for them, and re-layouts: 86.2 us -> 98.3 us
    pallas_call x13, Pallas kernels: 49.8 us -> 15.9 us  [fold(): pl.pallas_call(fold.kernel, out_shape=[fold.gives_part.shape(self.values[...]
    unnamed x148 -> x178, local copies, waits for them, and re-layouts: 25.3 us -> 34.5 us
  transfers between devices with their start and end apart: 98 -> 98, of which waited for: 27 -> 30; matrix products, arithmetic and copies ran while one was open for 18% -> 18% of each run, Pallas kernels for 45% -> 42%
where the time goes in v4:
time: 748 us; the launch traced here: 741 us
  Pallas kernels  359 us (48%)
  waiting for transfers between devices  121 us (16%)
  local copies, waits for them, and re-layouts  98.3 us (13%)
  starting transfers between devices  70.1 us (9%)
  other arithmetic  61.8 us (8%)
  between operations  17.5 us (2%)
  matrix products  12.8 us (2%)
    ppermute x82, waiting for transfers between devices, hop(): lax.ppermute(value, axis, [(i, i ^ mask) for i in range(lax.axis_size(axi...  83.5 us
    pallas_call x6, Pallas kernels, weight_grad(): pl.pallas_call(partial(grad_kernel, rows=rows, widths=widths, sources=sou...  81.8 us
    pallas_call x10, Pallas kernels, tiled(): pl.pallas_call(kernel, grid=(total // columns,), out_shape=jax.ShapeDtype...  81.6 us
    pallas_call x6, Pallas kernels, gathered(): pl.pallas_call(partial(gathered_kernel, rows=rows, widths=widths, kind=ki...  77 us
    ppermute x82, starting transfers between devices, hop(): lax.ppermute(value, axis, [(i, i ^ mask) for i in range(lax.axis_size(axi...  61.9 us
    pallas_call x2, Pallas kernels, attend_back(): pl.pallas_call(partial(attend_back_kernel, wins=wins, length=length, rows...  42.9 us
    unnamed x178, local copies, waits for them, and re-layouts  34.5 us
    pallas_call x6, Pallas kernels, row_call(): pl.pallas_call(kernel, grid=(2,), out_shape=out_shape, in_specs=[block] *...  33.2 us
  transfers between devices with their start and end apart: 98, of which 30 were waited for; matrix products, arithmetic and copies ran while one was open for 18% of the time, Pallas kernels for 42%

profile of v4, /device:TPU:0, one launch (start us, length us, event | category | flops | bytes accessed | tf_op | source)
XLA Modules:
  0.0 741.0 jit_solution(11360372647256141949)
XLA Ops:
  17.6 14.4 %collective-permute-done = bf16[3,128,1024]{2,1,0:T(8,128)(2,1)S(1)} collective-permute-done((bf16[3,128,1024]{2,1,0:T(8,128)(2,1)S(1)}, bf16[3,128,1024]{2,1,0:T(8,128)(2,1)S(1)}, u32[]{:S(2)}, u32[]{:S(2)}) %collective-permute-start) | collective-permute-done | bytes 786464 | tf_op jit(solution)/shard_map/ppermute | solution.py:759
  102.6 11.6 %gathered.6 = (bf16[768,3072]{1,0:T(8,128)(2,1)}, bf16[1024,3072]{1,0:T(8,128)(2,1)}, bf16[1024,1024]{1,0:T(8,128)(2,1)}) custom-call(s32[4]{0:T(128)} %pad_add_fusion.row_of, s32[2]{0:T(128)} %pad_add_fusion.1.y_of, bf16[768,1024]{1,0:T(8,128)(2,1)} %add_convert_fusion.x_ref.refs_0_, bf16[2,4,128,512]{3,2,1,0:T(8,128)(2,1)} %pad_maximum_fusion.3.refs_0_, ...), custom_call_target="tpu_custom_call" | custom-call | flops 1 | bytes 1 | tf_op jit(solution)/shard_map/gathered/pallas_call | solution.py:156
  118.7 11.5 %attend.2 = (bf16[768,1024]{1,0:T(8,128)(2,1)}, bf16[16,3,256,256]{3,2,1,0:T(8,128)(2,1)}) custom-call(bf16[768,3072]{1,0:T(8,128)(2,1)} %get-tuple-element.444.q_ref.k_ref.v_ref, bf16[768,3072]{1,0:T(8,128)(2,1)} %get-tuple-element.444.q_ref.k_ref.v_ref, bf16[768,3072]{1,0:T(8,128)(2,1)} %get-tuple-element.444.q_ref.k_ref.v_ref, ...), custom_call_target="tpu_custom_call" | custom-call | flops 1 | bytes 1 | tf_op jit(solution)/shard_map/attend/pallas_call | solution.py:492
  181.2 14.9 %gathered.7 = (bf16[640,4096]{1,0:T(8,128)(2,1)}, bf16[640,4096]{1,0:T(8,128)(2,1)}, bf16[1024,4096]{1,0:T(8,128)(2,1)}) custom-call(s32[4]{0:T(128)} %pad_add_fusion.row_of, s32[2]{0:T(128)} %pad_add_fusion.1.y_of, bf16[640,1024]{1,0:T(8,128)(2,1)} %add_convert_fusion.1.x_ref.refs_0_, bf16[2,4,128,512]{3,2,1,0:T(8,128)(2,1)} %pad_maximum_fusion.5.refs_0_, ...), custom_call_target="tpu_custom_call" | custom-call | flops 1 | bytes 1 | tf_op jit(solution)/shard_map/gathered/pallas_call | solution.py:156
  203.6 12.0 %gathered.8 = (f32[640,1024]{1,0:T(8,128)}, bf16[4096,1024]{1,0:T(8,128)(2,1)}) custom-call(s32[4]{0:T(128)} %pad_add_fusion.row_of, s32[2]{0:T(128)} %pad_add_fusion.1.y_of, bf16[640,4096]{1,0:T(8,128)(2,1)} %get-tuple-element.471.x_ref.refs_0_, bf16[2,4,512,128]{3,2,1,0:T(8,128)(2,1)} %get-tuple-element.829.refs_0_, ...), custom_call_target="tpu_custom_call" | custom-call | flops 1 | bytes 1 | tf_op jit(solution)/shard_map/gathered/pallas_call | solution.py:156
  230.3 11.0 %gathered.9 = (bf16[640,3072]{1,0:T(8,128)(2,1)}, bf16[1024,3072]{1,0:T(8,128)(2,1)}, bf16[1024,1024]{1,0:T(8,128)(2,1)}) custom-call(s32[4]{0:T(128)} %pad_add_fusion.row_of, s32[2]{0:T(128)} %pad_add_fusion.1.y_of, bf16[640,1024]{1,0:T(8,128)(2,1)} %get-tuple-element.483.x_ref.refs_0_, bf16[2,4,128,512]{3,2,1,0:T(8,128)(2,1)} %get-tuple-element.484.refs_0_, ...), custom_call_target="tpu_custom_call" | custom-call | flops 1 | bytes 1 | tf_op jit(solution)/shard_map/gathered/pallas_call | solution.py:156
  241.9 15.4 %attend.3 = (bf16[640,1024]{1,0:T(8,128)(2,1)}, bf16[16,2,320,320]{3,2,1,0:T(8,128)(2,1)}) custom-call(bf16[640,3072]{1,0:T(8,128)(2,1)} %get-tuple-element.491.q_ref.k_ref.v_ref, bf16[640,3072]{1,0:T(8,128)(2,1)} %get-tuple-element.491.q_ref.k_ref.v_ref, bf16[640,3072]{1,0:T(8,128)(2,1)} %get-tuple-element.491.q_ref.k_ref.v_ref, ...), custom_call_target="tpu_custom_call" | custom-call | flops 1 | bytes 1 | tf_op jit(solution)/shard_map/attend/pallas_call | solution.py:492
  275.3 14.7 %gathered.10 = (bf16[640,4096]{1,0:T(8,128)(2,1)}, bf16[640,4096]{1,0:T(8,128)(2,1)}, bf16[1024,4096]{1,0:T(8,128)(2,1)}) custom-call(s32[4]{0:T(128)} %pad_add_fusion.row_of, s32[2]{0:T(128)} %pad_add_fusion.1.y_of, bf16[640,1024]{1,0:T(8,128)(2,1)} %get-tuple-element.504.x_ref.refs_0_, bf16[2,4,128,512]{3,2,1,0:T(8,128)(2,1)} %copy-done.47, ...), custom_call_target="tpu_custom_call" | custom-call | flops 1 | bytes 1 | tf_op jit(solution)/shard_map/gathered/pallas_call | solution.py:156
  290.1 13.2 %weight_grad.6 = (bf16[2,2,2,4,512,128]{5,4,3,2,1,0:T(8,128)(2,1)}, bf16[2,2,2,4,512,128]{5,4,3,2,1,0:T(8,128)(2,1)}) custom-call(s32[4]{0:T(128)} %pad_add_fusion.row_of, s32[2]{0:T(128)} %pad_add_fusion.1.y_of, bf16[640,4096]{1,0:T(8,128)(2,1)} %get-tuple-element.516.refs_0_.x_ref, bf16[640,1024]{1,0:T(8,128)(2,1)} %multiply_convert_fusion.1.refs_1_.left), custom_call_target="tpu_custom_call" | custom-call | flops 1 | bytes 1 | tf_op jit(solution)/shard_map/weight_grad/pallas_call | solution.py:326
  317.0 12.7 %gathered.11 = (f32[640,1024]{1,0:T(8,128)}, bf16[4096,1024]{1,0:T(8,128)(2,1)}) custom-call(s32[4]{0:T(128)} %pad_add_fusion.row_of, s32[2]{0:T(128)} %pad_add_fusion.1.y_of, bf16[640,4096]{1,0:T(8,128)(2,1)} %get-tuple-element.516.refs_0_.x_ref, bf16[2,4,512,128]{3,2,1,0:T(8,128)(2,1)} %copy-done.51, bf16[2,4,512,128]{3,2,1,0:T(8,128)(2,1)} %copy-done.61, ...), custom_call_target="tpu_custom_call" | custom-call | flops 1 | bytes 1 | tf_op jit(solution)/shard_map/gathered/pallas_call | solution.py:156
  329.7 11.4 %product.12.refs_1_.left = bf16[640,4096]{1,0:T(8,128)(2,1)} custom-call(bf16[640,1024]{1,0:T(8,128)(2,1)} %multiply_convert_fusion.1.refs_1_.left, bf16[4096,1024]{1,0:T(8,128)(2,1)} %get-tuple-element.521.right, bf16[640,4096]{1,0:T(8,128)(2,1)} %get-tuple-element.522.factor), custom_call_target="tpu_custom_call" | custom-call | flops 1 | bytes 1 | tf_op jit(solution)/shard_map/product/pallas_call | solution.py:195
  343.1 13.8 %weight_grad.7 = (bf16[2,2,2,4,128,512]{5,4,3,2,1,0:T(8,128)(2,1)}, bf16[2,2,2,4,128,512]{5,4,3,2,1,0:T(8,128)(2,1)}, bf16[2,4,512,128]{3,2,1,0:T(8,128)(2,1)}, ...) custom-call(s32[4]{0:T(128)} %pad_add_fusion.row_of, ...), custom_call_target="tpu_custom_call" | custom-call | flops 1 | bytes 1 | tf_op jit(solution)/shard_map/weight_grad/pallas_call | solution.py:326
  359.4 10.6 %product.13.grad_in = f32[640,1024]{1,0:T(8,128)} custom-call(bf16[640,4096]{1,0:T(8,128)(2,1)} %product.12.refs_1_.left, bf16[1024,4096]{1,0:T(8,128)(2,1)} %get-tuple-element.534.right), custom_call_target="tpu_custom_call" | custom-call | flops 1 | bytes 1 | tf_op jit(solution)/shard_map/product/pallas_call | solution.py:195
  401.6 21.5 %attend_back.2 = (bf16[640,3072]{1,0:T(8,128)(2,1)}, f32[16,2,1152]{2,1,0:T(2,128)}) custom-call(bf16[640,3072]{1,0:T(8,128)(2,1)} %get-tuple-element.491.q_ref.k_ref.v_ref, bf16[640,3072]{1,0:T(8,128)(2,1)} %get-tuple-element.491.q_ref.k_ref.v_ref, bf16[640,3072]{1,0:T(8,128)(2,1)} %get-tuple-element.491.q_ref.k_ref.v_ref, ...), custom_call_target="tpu_custom_call" | custom-call | flops 1 | bytes 1 | tf_op jit(solution)/shard_map/attend_back/pallas_call | solution.py:603
  427.7 12.7 %weight_grad.8 = (bf16[2,2,2,4,128,512]{5,4,3,2,1,0:T(8,128)(2,1)}, bf16[2,2,2,4,128,512]{5,4,3,2,1,0:T(8,128)(2,1)}, bf16[4,2,512,128]{3,2,1,0:T(8,128)(2,1)}) custom-call(s32[4]{0:T(128)} %pad_add_fusion.row_of, s32[2]{0:T(128)} %pad_add_fusion.1.y_of, bf16[640,1024]{1,0:T(8,128)(2,1)} %get-tuple-element.483.x_ref.refs_0_, ...), custom_call_target="tpu_custom_call" | custom-call | flops 1 | bytes 1 | tf_op jit(solution)/shard_map/weight_grad/pallas_call | solution.py:326
  459.7 15.7 %weight_grad.9 = (bf16[2,2,2,4,512,128]{5,4,3,2,1,0:T(8,128)(2,1)}, bf16[2,2,2,4,512,128]{5,4,3,2,1,0:T(8,128)(2,1)}, bf16[2,4,128,512]{3,2,1,0:T(8,128)(2,1)}, ...) custom-call(s32[4]{0:T(128)} %pad_add_fusion.row_of, ...), custom_call_target="tpu_custom_call" | custom-call | flops 1 | bytes 1 | tf_op jit(solution)/shard_map/weight_grad/pallas_call | solution.py:326
  477.6 11.5 %product.16.refs_1_.left = bf16[640,4096]{1,0:T(8,128)(2,1)} custom-call(bf16[640,1024]{1,0:T(8,128)(2,1)} %get-tuple-element.625.refs_1_.left, bf16[4096,1024]{1,0:T(8,128)(2,1)} %get-tuple-element.626.right, bf16[640,4096]{1,0:T(8,128)(2,1)} %get-tuple-element.627.factor), custom_call_target="tpu_custom_call" | custom-call | flops 1 | bytes 1 | tf_op jit(solution)/shard_map/product/pallas_call | solution.py:195
  489.1 14.2 %weight_grad.10 = (bf16[2,2,2,4,128,512]{5,4,3,2,1,0:T(8,128)(2,1)}, bf16[2,2,2,4,128,512]{5,4,3,2,1,0:T(8,128)(2,1)}, bf16[2,4,512,128]{3,2,1,0:T(8,128)(2,1)},...) custom-call(s32[4]{0:T(128)} %pad_add_fusion.row_of, ...), custom_call_target="tpu_custom_call" | custom-call | flops 1 | bytes 1 | tf_op jit(solution)/shard_map/weight_grad/pallas_call | solution.py:326
  505.7 10.5 %product.17.grad_in = f32[640,1024]{1,0:T(8,128)} custom-call(bf16[640,4096]{1,0:T(8,128)(2,1)} %product.16.refs_1_.left, bf16[1024,4096]{1,0:T(8,128)(2,1)} %get-tuple-element.659.right), custom_call_target="tpu_custom_call" | custom-call | flops 1 | bytes 1 | tf_op jit(solution)/shard_map/product/pallas_call | solution.py:195
  529.9 16.7 %collective-permute-done.63 = bf16[3,128,1024]{2,1,0:T(8,128)(2,1)S(1)} collective-permute-done((bf16[3,128,1024]{2,1,0:T(8,128)(2,1)S(1)}, bf16[3,128,1024]{2,1,0:T(8,128)(2,1)S(1)}, u32[]{:S(2)}, u32[]{:S(2)}) %collective-permute-start.63) | collective-permute-done | bytes 786464 | tf_op jit(solution)/shard_map/ppermute | solution.py:759
  567.2 21.4 %attend_back.3 = (bf16[768,3072]{1,0:T(8,128)(2,1)}, f32[16,2,512]{2,1,0:T(2,128)}) custom-call(bf16[768,3072]{1,0:T(8,128)(2,1)} %get-tuple-element.444.q_ref.k_ref.v_ref, bf16[768,3072]{1,0:T(8,128)(2,1)} %get-tuple-element.444.q_ref.k_ref.v_ref, bf16[768,3072]{1,0:T(8,128)(2,1)} %get-tuple-element.444.q_ref.k_ref.v_ref, bf16[768,1024]{1,0:T(8,128)(2,1)} %product.18.g_ref, ...), custom_call_target="tpu_custom_call" | custom-call | flops 1 | bytes 1 | tf_op jit(solution)/shard_map/attend_back/pallas_call | solution.py:603
  596.4 12.3 %weight_grad.11 = (bf16[2,2,2,4,128,512]{5,4,3,2,1,0:T(8,128)(2,1)}, bf16[2,2,2,4,128,512]{5,4,3,2,1,0:T(8,128)(2,1)}) custom-call(s32[4]{0:T(128)} %pad_add_fusion.row_of, s32[2]{0:T(128)} %pad_add_fusion.1.y_of, bf16[768,1024]{1,0:T(8,128)(2,1)} %add_convert_fusion.x_ref.refs_0_, bf16[768,1024]{1,0:T(8,128)(2,1)} %get-tuple-element.450.left.refs_1_, ...), custom_call_target="tpu_custom_call" | custom-call | flops 1 | bytes 1 | tf_op jit(solution)/shard_map/weight_grad/pallas_call | solution.py:326
  646.0 10.1 %product.19.grad_in = f32[768,1024]{1,0:T(8,128)} custom-call(bf16[768,3072]{1,0:T(8,128)(2,1)} %get-tuple-element.764.refs_2_.left, bf16[1024,3072]{1,0:T(8,128)(2,1)} %get-tuple-element.765.right), custom_call_target="tpu_custom_call" | custom-call | flops 1 | bytes 1 | tf_op jit(solution)/shard_map/product/pallas_call | solution.py:195
  691.7 11.8 %collective-permute-done.81 = f32[416,128]{1,0:T(8,128)S(1)} collective-permute-done((f32[416,128]{1,0:T(8,128)S(1)}, f32[416,128]{1,0:T(8,128)S(1)}, u32[]{:S(2)}, u32[]{:S(2)}) %collective-permute-start.81) | collective-permute-done | bytes 213024 | tf_op jit(solution)/shard_map/ppermute | solution.py:35
  (538 shorter events, 397.9 us)
Async XLA Ops:
  7.2 46.8 %all-gather.17.cloned.1.call-start = ((), (), s32[]{:S(2)}) async-start(), calls=%async_computation.11 | async-start | bytes 1310720 | tf_op jit(solution)/shard_map/all_gather | solution.py:48
  10.1 83.5 %all-gather.15.cloned.1.call-start = ((), (), s32[]{:S(2)}) async-start(), calls=%async_computation.10 | async-start | bytes 1310720 | tf_op jit(solution)/shard_map/all_gather | solution.py:48
  15.2 129.2 %all-gather.13.cloned.1.call-start = ((), (), s32[]{:S(2)}) async-start(), calls=%async_computation.9 | async-start | bytes 2621440 | tf_op jit(solution)/shard_map/all_gather | solution.py:48
  42.4 154.3 %all-gather.11.cloned.1.call-start = ((), (), s32[]{:S(2)}) async-start(), calls=%async_computation.8 | async-start | bytes 2621440 | tf_op jit(solution)/shard_map/all_gather | solution.py:48
  50.5 175.8 %all-gather.9.cloned.1.call-start = ((), (), s32[]{:S(2)}) async-start(), calls=%async_computation.7 | async-start | bytes 2621440 | tf_op jit(solution)/shard_map/all_gather | solution.py:48
  77.0 182.3 %all-gather.7.cloned.1.call-start = ((), (), s32[]{:S(2)}) async-start(), calls=%async_computation.6 | async-start | bytes 2621440 | tf_op jit(solution)/shard_map/all_gather | solution.py:48
  143.8 448.4 %reduce-scatter.7.cloned.1.call-start = ((), (), s32[]{:S(2)}) async-start(), calls=%async_computation.12 | async-start | bytes 1310720 | tf_op jit(solution)/shard_map/reduce_scatter | solution.py:377
  147.6 48.6 %collective-permute-start.18 = (bf16[2,4,512,128]{3,2,1,0:T(8,128)(2,1)}, bf16[2,4,512,128]{3,2,1,0:T(8,128)(2,1)}, u32[]{:S(2)}, u32[]{:S(2)}) collective-permute-start(bf16[2,4,512,128]{3,2,1,0:T(8,128)(2,1)} %get-tuple-element.828.refs_4_), channel_id=1, source_target_pairs={{0,1},{1,0},{2,3},{3,2},{4,5},{5,4},{6,7},{7,6},{8,9},{9,8},{10,11... | collective-permute-start | bytes 3145736 | tf_op jit(solution)/shard_map/ppermute | solution.py:35
  148.4 47.7 %collective-permute-start.17 = (bf16[2,4,512,128]{3,2,1,0:T(8,128)(2,1)}, bf16[2,4,512,128]{3,2,1,0:T(8,128)(2,1)}, u32[]{:S(2)}, u32[]{:S(2)}) collective-permute-start(bf16[2,4,512,128]{3,2,1,0:T(8,128)(2,1)} %get-tuple-element.829.refs_0_), channel_id=1, source_target_pairs={{0,16},{8,24},{16,0},{24,8},{1,17},{9,25},{17,1},{25,9},{2,18},{10... | collective-permute-start | bytes 3145736 | tf_op jit(solution)/shard_map/ppermute | solution.py:35
  241.6 33.7 %collective-permute-start.40 = (bf16[2,4,128,512]{3,2,1,0:T(8,128)(2,1)S(1)}, bf16[2,4,128,512]{3,2,1,0:T(8,128)(2,1)}, u32[]{:S(2)}, u32[]{:S(2)}) collective-permute-start(bf16[2,4,128,512]{3,2,1,0:T(8,128)(2,1)S(1)} %get-tuple-element.507.refs_4_), channel_id=1, source_target_pairs={{0,8},{8,0},{16,24},{24,16},{1,9},{9,1},{17,25},{25,17},{2,10},{10... | collective-permute-start | bytes 3145736 | tf_op jit(solution)/shard_map/ppermute | solution.py:35
  303.2 37.9 %collective-permute-start.46 = (bf16[2,2,2,4,512,128]{5,4,3,2,1,0:T(8,128)(2,1)}, bf16[2,2,2,4,512,128]{5,4,3,2,1,0:T(8,128)(2,1)S(1)}, u32[]{:S(2)}, u32[]{:S(2)}) collective-permute-start(bf16[2,2,2,4,512,128]{5,4,3,2,1,0:T(8,128)(2,1)} %get-tuple-element.524), channel_id=1, source_target_pairs={{0,8},{8,0},{16,24},{24,16},{1,9},{9,1},{17,25},{25,17},{2,10},{10... | collective-permute-start | bytes 12582920 | tf_op jit(solution)/shard_map/ppermute | solution.py:35
  390.9 49.5 %collective-permute-start.52 = (bf16[2,4,128,512]{3,2,1,0:T(8,128)(2,1)}, bf16[2,4,128,512]{3,2,1,0:T(8,128)(2,1)S(1)}, u32[]{:S(2)}, u32[]{:S(2)}) collective-permute-start(bf16[2,4,128,512]{3,2,1,0:T(8,128)(2,1)} %get-tuple-element.583), channel_id=1, source_target_pairs={{0,16},{8,24},{16,0},{24,8},{1,17},{9,25},{17,1},{25,9},{2,18},{10... | collective-permute-start | bytes 3145736 | tf_op jit(solution)/shard_map/ppermute | solution.py:35
  391.4 49.0 %collective-permute-start.53 = (bf16[2,4,128,512]{3,2,1,0:T(8,128)(2,1)}, bf16[2,4,128,512]{3,2,1,0:T(8,128)(2,1)S(1)}, u32[]{:S(2)}, u32[]{:S(2)}) collective-permute-start(bf16[2,4,128,512]{3,2,1,0:T(8,128)(2,1)} %get-tuple-element.585), channel_id=1, source_target_pairs={{0,1},{1,0},{2,3},{3,2},{4,5},{5,4},{6,7},{7,6},{8,9},{9,8},{10,11... | collective-permute-start | bytes 3145736 | tf_op jit(solution)/shard_map/ppermute | solution.py:35
  392.9 33.9 %collective-permute-start.50 = (bf16[4,512,128]{2,1,0:T(8,128)(2,1)S(1)}, bf16[4,512,128]{2,1,0:T(8,128)(2,1)S(1)}, u32[]{:S(2)}, u32[]{:S(2)}) collective-permute-start(bf16[4,512,128]{2,1,0:T(8,128)(2,1)S(1)} %get-tuple-element.565), channel_id=1, source_target_pairs={{0,1},{1,0},{2,3},{3,2},{4,5},{5,4},{6,7},{7,6},{8,9},{9,8},{10,11... | collective-permute-start | bytes 1572872 | tf_op jit(solution)/shard_map/ppermute | solution.py:35
  546.6 160.8 %reduce-scatter.17.cloned.1.call-start = ((), (), s32[]{:S(2)}) async-start(), calls=%async_computation.17 | async-start | bytes 1310720 | tf_op jit(solution)/shard_map/reduce_scatter | solution.py:377
  547.4 161.8 %reduce-scatter.15.cloned.1.call-start = ((), (), s32[]{:S(2)}) async-start(), calls=%async_computation.16 | async-start | bytes 1310720 | tf_op jit(solution)/shard_map/reduce_scatter | solution.py:377
  547.4 41.1 %collective-permute-start.64 = (bf16[2,4,512,128]{3,2,1,0:T(8,128)(2,1)}, bf16[2,4,512,128]{3,2,1,0:T(8,128)(2,1)S(1)}, u32[]{:S(2)}, u32[]{:S(2)}) collective-permute-start(bf16[2,4,512,128]{3,2,1,0:T(8,128)(2,1)} %get-tuple-element.693), channel_id=1, source_target_pairs={{0,16},{8,24},{16,0},{24,8},{1,17},{9,25},{17,1},{25,9},{2,18},{10... | collective-permute-start | bytes 3145736 | tf_op jit(solution)/shard_map/ppermute | solution.py:35
  548.9 39.7 %collective-permute-start.65 = (bf16[2,4,512,128]{3,2,1,0:T(8,128)(2,1)}, bf16[2,4,512,128]{3,2,1,0:T(8,128)(2,1)S(1)}, u32[]{:S(2)}, u32[]{:S(2)}) collective-permute-start(bf16[2,4,512,128]{3,2,1,0:T(8,128)(2,1)} %get-tuple-element.695), channel_id=1, source_target_pairs={{0,1},{1,0},{2,3},{3,2},{4,5},{5,4},{6,7},{7,6},{8,9},{9,8},{10,11... | collective-permute-start | bytes 3145736 | tf_op jit(solution)/shard_map/ppermute | solution.py:35
  560.5 48.1 %collective-permute-start.66 = (bf16[2,4,128,512]{3,2,1,0:T(8,128)(2,1)}, bf16[2,4,128,512]{3,2,1,0:T(8,128)(2,1)S(1)}, u32[]{:S(2)}, u32[]{:S(2)}) collective-permute-start(bf16[2,4,128,512]{3,2,1,0:T(8,128)(2,1)} %get-tuple-element.718), channel_id=1, source_target_pairs={{0,16},{8,24},{16,0},{24,8},{1,17},{9,25},{17,1},{25,9},{2,18},{10... | collective-permute-start | bytes 3145736 | tf_op jit(solution)/shard_map/ppermute | solution.py:35
  561.9 46.7 %collective-permute-start.67 = (bf16[2,4,128,512]{3,2,1,0:T(8,128)(2,1)}, bf16[2,4,128,512]{3,2,1,0:T(8,128)(2,1)}, u32[]{:S(2)}, u32[]{:S(2)}) collective-permute-start(bf16[2,4,128,512]{3,2,1,0:T(8,128)(2,1)} %get-tuple-element.720), channel_id=1, source_target_pairs={{0,1},{1,0},{2,3},{3,2},{4,5},{5,4},{6,7},{7,6},{8,9},{9,8},{10,11... | collective-permute-start | bytes 3145736 | tf_op jit(solution)/shard_map/ppermute | solution.py:35
  614.9 99.6 %reduce-scatter.13.cloned.1.call-start = ((), (), s32[]{:S(2)}) async-start(), calls=%async_computation.15 | async-start | bytes 1310720 | tf_op jit(solution)/shard_map/reduce_scatter | solution.py:377
  615.5 105.9 %reduce-scatter.11.cloned.1.call-start = ((), (), s32[]{:S(2)}) async-start(), calls=%async_computation.14 | async-start | bytes 1310720 | tf_op jit(solution)/shard_map/reduce_scatter | solution.py:377
  637.4 93.0 %reduce-scatter.9.cloned.1.call-start = ((), (), s32[]{:S(2)}) async-start(), calls=%async_computation.13 | async-start | bytes 1310720 | tf_op jit(solution)/shard_map/reduce_scatter | solution.py:377
  681.8 41.5 %collective-permute-start.80 = (bf16[3,128,1024]{2,1,0:T(8,128)(2,1)}, bf16[3,128,1024]{2,1,0:T(8,128)(2,1)S(1)}, u32[]{:S(2)}, u32[]{:S(2)}) collective-permute-start(bf16[3,128,1024]{2,1,0:T(8,128)(2,1)} %select_convert_fusion), channel_id=1, source_target_pairs={{0,1},{1,0},{2,3},{3,2},{4,5},{5,4},{6,7},{7,6},{8,9},{9,8},{10,11... | collective-permute-start | bytes 2359304 | tf_op jit(solution)/shard_map/ppermute | solution.py:759
  (163 other events, 1796.0 us)
Sparse Core Ops, SparseCore 0:
  10.2 30.6 all-gather.16
  43.0 27.4 all-gather.14
  72.6 45.2 all-gather.12
  119.9 44.8 all-gather.10
  166.2 44.4 all-gather.8
  212.8 44.6 all-gather.6
  546.7 27.4 reduce-scatter.6
  576.6 25.8 reduce-scatter.16
  615.0 27.5 reduce-scatter.14
  644.9 26.2 reduce-scatter.12
  674.1 28.0 reduce-scatter.10
  704.4 25.9 reduce-scatter.8

commit v5 on v4

--- a/solution.py
+++ b/solution.py
@@ -462,6 +462,7 @@
     blocks = length // rows
     masks = mask_ref.shape[0]
     mixed = [None] * wins
+    value_cols = [v_ref[win * length : (win + 1) * length, :].T for win in range(wins)]
     for head in range(2):
         strip = strip_ref[head]
         for block in range(blocks):
@@ -478,9 +479,9 @@
             probs = raised * (1.0 / jnp.sum(raised, axis=0, keepdims=True))
             probs = probs.astype(jnp.bfloat16)
             probs_ref[head, win] = probs
-            turned = (v_ref[here, :] * low).T
-            part = jnp.dot(turned, probs, preferred_element_type=jnp.float32)
-            mixed[win] = part if head == 0 else mixed[win] + part
+            own = value_cols[win][head * 64 : (head + 1) * 64, :]
+            part = jnp.dot(own, probs, preferred_element_type=jnp.float32)
+            mixed[win] = part if head == 0 else jnp.concatenate([mixed[win], part], axis=0)
     for win in range(wins):
         out_ref[win * length : (win + 1) * length, :] = mixed[win].T.astype(jnp.bfloat16)
 
@@ -521,6 +522,7 @@
     width = out_ref.shape[1] // 3
     step = pl.program_id(0)
     query_grads = [None] * wins
+    key_cols = [k_ref[win * length : (win + 1) * length, :].T for win in range(wins)]
     total[...] = jnp.zeros_like(total)
     for head in range(2):
         chosen = head_lanes(head)
@@ -528,7 +530,6 @@
         for win in range(wins):
             here = slice(win * length, (win + 1) * length)
             queries = q_ref[here, :] * jnp.bfloat16(0.125)
-            key_rows = k_ref[here, :]
             outer = g_ref[here, :]
             probs = probs_ref[head, win]
             grad_probs = lax.dot_general(v_ref[here, :] * low, outer, NT, preferred_element_type=jnp.float32)
@@ -539,12 +540,13 @@
                 total[:, :length] = grad_scores.astype(jnp.float32)
             else:
                 total[:, :length] = total[:, :length] + grad_scores.astype(jnp.float32)
-            part = jnp.dot((key_rows * low).T, grad_scores, preferred_element_type=jnp.float32)
+            own = key_cols[win][head * 64 : (head + 1) * 64, :]
+            part = jnp.dot(own, grad_scores, preferred_element_type=jnp.float32)
             if head == 0:
                 query_grads[win] = part
             else:
                 column = pl.multiple_of(step * 128, 128)
-                both = (query_grads[win] + part) * 0.125
+                both = jnp.concatenate([query_grads[win], part], axis=0) * 0.125
                 out_ref[here, pl.ds(column, 128)] = both.T.astype(jnp.bfloat16)
             new = (
                 None,

time: 748 us -> 757 us (1.012)
  Pallas kernels: 359 us -> 372 us
    pallas_call x2, Pallas kernels: 26.9 us -> 36.2 us  [attend(): pl.pallas_call(partial(attend_kernel, wins=wins, length=length), grid=(HE...]
  transfers between devices with their start and end apart: 98 -> 98, of which waited for: 30 -> 26; matrix products, arithmetic and copies ran while one was open for 18% -> 18% of each run, Pallas kernels for 42% -> 43%
where the time goes in v5:
time: 757 us; the launch traced here: 750 us
  Pallas kernels  372 us (49%)
  waiting for transfers between devices  118 us (16%)
  local copies, waits for them, and re-layouts  98.1 us (13%)
  starting transfers between devices  70.6 us (9%)
  other arithmetic  61.6 us (8%)
  between operations  17.4 us (2%)
  matrix products  12.7 us (2%)
    pallas_call x6, Pallas kernels, weight_grad(): pl.pallas_call(partial(grad_kernel, rows=rows, widths=widths, sources=sou...  81.8 us
    pallas_call x10, Pallas kernels, tiled(): pl.pallas_call(kernel, grid=(total // columns,), out_shape=jax.ShapeDtype...  81.6 us
    ppermute x82, waiting for transfers between devices, hop(): lax.ppermute(value, axis, [(i, i ^ mask) for i in range(lax.axis_size(axi...  79.6 us
    pallas_call x6, Pallas kernels, gathered(): pl.pallas_call(partial(gathered_kernel, rows=rows, widths=widths, kind=ki...  77 us
    ppermute x82, starting transfers between devices, hop(): lax.ppermute(value, axis, [(i, i ^ mask) for i in range(lax.axis_size(axi...  64 us
    pallas_call x2, Pallas kernels, attend_back(): pl.pallas_call(partial(attend_back_kernel, wins=wins, length=length, rows...  46.3 us
    pallas_call x2, Pallas kernels, attend(): pl.pallas_call(partial(attend_kernel, wins=wins, length=length), grid=(HE...  36.2 us
    unnamed x178, local copies, waits for them, and re-layouts  34.2 us
  transfers between devices with their start and end apart: 98, of which 26 were waited for; matrix products, arithmetic and copies ran while one was open for 18% of the time, Pallas kernels for 43%

profile of v5, /device:TPU:0, one launch (start us, length us, event | category | flops | bytes accessed | tf_op | source)
XLA Modules:
  0.0 750.1 jit_solution(10226249388457298474)
XLA Ops:
  17.6 14.4 %collective-permute-done = bf16[3,128,1024]{2,1,0:T(8,128)(2,1)S(1)} collective-permute-done((bf16[3,128,1024]{2,1,0:T(8,128)(2,1)S(1)}, bf16[3,128,1024]{2,1,0:T(8,128)(2,1)S(1)}, u32[]{:S(2)}, u32[]{:S(2)}) %collective-permute-start) | collective-permute-done | bytes 786464 | tf_op jit(solution)/shard_map/ppermute | solution.py:761
  102.6 11.6 %gathered.6 = (bf16[768,3072]{1,0:T(8,128)(2,1)}, bf16[1024,3072]{1,0:T(8,128)(2,1)}, bf16[1024,1024]{1,0:T(8,128)(2,1)}) custom-call(s32[4]{0:T(128)} %pad_add_fusion.row_of, s32[2]{0:T(128)} %pad_add_fusion.1.y_of, bf16[768,1024]{1,0:T(8,128)(2,1)} %add_convert_fusion.x_ref.refs_0_, bf16[2,4,128,512]{3,2,1,0:T(8,128)(2,1)} %pad_maximum_fusion.3.refs_0_, ...), custom_call_target="tpu_custom_call" | custom-call | flops 1 | bytes 1 | tf_op jit(solution)/shard_map/gathered/pallas_call | solution.py:156
  118.7 20.2 %attend.2 = (bf16[768,1024]{1,0:T(8,128)(2,1)}, bf16[16,3,256,256]{3,2,1,0:T(8,128)(2,1)}) custom-call(bf16[768,3072]{1,0:T(8,128)(2,1)} %get-tuple-element.444.q_ref.k_ref.v_ref, bf16[768,3072]{1,0:T(8,128)(2,1)} %get-tuple-element.444.q_ref.k_ref.v_ref, bf16[768,3072]{1,0:T(8,128)(2,1)} %get-tuple-element.444.q_ref.k_ref.v_ref, ...), custom_call_target="tpu_custom_call" | custom-call | flops 1 | bytes 1 | tf_op jit(solution)/shard_map/attend/pallas_call | solution.py:493
  186.5 14.8 %gathered.7 = (bf16[640,4096]{1,0:T(8,128)(2,1)}, bf16[640,4096]{1,0:T(8,128)(2,1)}, bf16[1024,4096]{1,0:T(8,128)(2,1)}) custom-call(s32[4]{0:T(128)} %pad_add_fusion.row_of, s32[2]{0:T(128)} %pad_add_fusion.1.y_of, bf16[640,1024]{1,0:T(8,128)(2,1)} %add_convert_fusion.1.x_ref.refs_0_, bf16[2,4,128,512]{3,2,1,0:T(8,128)(2,1)} %pad_maximum_fusion.5.refs_0_, ...), custom_call_target="tpu_custom_call" | custom-call | flops 1 | bytes 1 | tf_op jit(solution)/shard_map/gathered/pallas_call | solution.py:156
  209.6 12.0 %gathered.8 = (f32[640,1024]{1,0:T(8,128)}, bf16[4096,1024]{1,0:T(8,128)(2,1)}) custom-call(s32[4]{0:T(128)} %pad_add_fusion.row_of, s32[2]{0:T(128)} %pad_add_fusion.1.y_of, bf16[640,4096]{1,0:T(8,128)(2,1)} %get-tuple-element.471.x_ref.refs_0_, bf16[2,4,512,128]{3,2,1,0:T(8,128)(2,1)} %get-tuple-element.829.refs_0_, ...), custom_call_target="tpu_custom_call" | custom-call | flops 1 | bytes 1 | tf_op jit(solution)/shard_map/gathered/pallas_call | solution.py:156
  236.3 11.1 %gathered.9 = (bf16[640,3072]{1,0:T(8,128)(2,1)}, bf16[1024,3072]{1,0:T(8,128)(2,1)}, bf16[1024,1024]{1,0:T(8,128)(2,1)}) custom-call(s32[4]{0:T(128)} %pad_add_fusion.row_of, s32[2]{0:T(128)} %pad_add_fusion.1.y_of, bf16[640,1024]{1,0:T(8,128)(2,1)} %get-tuple-element.483.x_ref.refs_0_, bf16[2,4,128,512]{3,2,1,0:T(8,128)(2,1)} %get-tuple-element.484.refs_0_, ...), custom_call_target="tpu_custom_call" | custom-call | flops 1 | bytes 1 | tf_op jit(solution)/shard_map/gathered/pallas_call | solution.py:156
  248.0 16.1 %attend.3 = (bf16[640,1024]{1,0:T(8,128)(2,1)}, bf16[16,2,320,320]{3,2,1,0:T(8,128)(2,1)}) custom-call(bf16[640,3072]{1,0:T(8,128)(2,1)} %get-tuple-element.491.q_ref.k_ref.v_ref, bf16[640,3072]{1,0:T(8,128)(2,1)} %get-tuple-element.491.q_ref.k_ref.v_ref, bf16[640,3072]{1,0:T(8,128)(2,1)} %get-tuple-element.491.q_ref.k_ref.v_ref, ...), custom_call_target="tpu_custom_call" | custom-call | flops 1 | bytes 1 | tf_op jit(solution)/shard_map/attend/pallas_call | solution.py:493
  282.2 14.7 %gathered.10 = (bf16[640,4096]{1,0:T(8,128)(2,1)}, bf16[640,4096]{1,0:T(8,128)(2,1)}, bf16[1024,4096]{1,0:T(8,128)(2,1)}) custom-call(s32[4]{0:T(128)} %pad_add_fusion.row_of, s32[2]{0:T(128)} %pad_add_fusion.1.y_of, bf16[640,1024]{1,0:T(8,128)(2,1)} %get-tuple-element.504.x_ref.refs_0_, bf16[2,4,128,512]{3,2,1,0:T(8,128)(2,1)} %copy-done.47, ...), custom_call_target="tpu_custom_call" | custom-call | flops 1 | bytes 1 | tf_op jit(solution)/shard_map/gathered/pallas_call | solution.py:156
  297.0 13.2 %weight_grad.6 = (bf16[2,2,2,4,512,128]{5,4,3,2,1,0:T(8,128)(2,1)}, bf16[2,2,2,4,512,128]{5,4,3,2,1,0:T(8,128)(2,1)}) custom-call(s32[4]{0:T(128)} %pad_add_fusion.row_of, s32[2]{0:T(128)} %pad_add_fusion.1.y_of, bf16[640,4096]{1,0:T(8,128)(2,1)} %get-tuple-element.516.refs_0_.x_ref, bf16[640,1024]{1,0:T(8,128)(2,1)} %multiply_convert_fusion.1.refs_1_.left), custom_call_target="tpu_custom_call" | custom-call | flops 1 | bytes 1 | tf_op jit(solution)/shard_map/weight_grad/pallas_call | solution.py:326
  323.9 12.7 %gathered.11 = (f32[640,1024]{1,0:T(8,128)}, bf16[4096,1024]{1,0:T(8,128)(2,1)}) custom-call(s32[4]{0:T(128)} %pad_add_fusion.row_of, s32[2]{0:T(128)} %pad_add_fusion.1.y_of, bf16[640,4096]{1,0:T(8,128)(2,1)} %get-tuple-element.516.refs_0_.x_ref, bf16[2,4,512,128]{3,2,1,0:T(8,128)(2,1)} %copy-done.51, bf16[2,4,512,128]{3,2,1,0:T(8,128)(2,1)} %copy-done.61, ...), custom_call_target="tpu_custom_call" | custom-call | flops 1 | bytes 1 | tf_op jit(solution)/shard_map/gathered/pallas_call | solution.py:156
  336.6 11.4 %product.12.refs_1_.left = bf16[640,4096]{1,0:T(8,128)(2,1)} custom-call(bf16[640,1024]{1,0:T(8,128)(2,1)} %multiply_convert_fusion.1.refs_1_.left, bf16[4096,1024]{1,0:T(8,128)(2,1)} %get-tuple-element.521.right, bf16[640,4096]{1,0:T(8,128)(2,1)} %get-tuple-element.522.factor), custom_call_target="tpu_custom_call" | custom-call | flops 1 | bytes 1 | tf_op jit(solution)/shard_map/product/pallas_call | solution.py:195
  350.0 13.8 %weight_grad.7 = (bf16[2,2,2,4,128,512]{5,4,3,2,1,0:T(8,128)(2,1)}, bf16[2,2,2,4,128,512]{5,4,3,2,1,0:T(8,128)(2,1)}, bf16[2,4,512,128]{3,2,1,0:T(8,128)(2,1)}, ...) custom-call(s32[4]{0:T(128)} %pad_add_fusion.row_of, ...), custom_call_target="tpu_custom_call" | custom-call | flops 1 | bytes 1 | tf_op jit(solution)/shard_map/weight_grad/pallas_call | solution.py:326
  366.1 10.6 %product.13.grad_in = f32[640,1024]{1,0:T(8,128)} custom-call(bf16[640,4096]{1,0:T(8,128)(2,1)} %product.12.refs_1_.left, bf16[1024,4096]{1,0:T(8,128)(2,1)} %get-tuple-element.534.right), custom_call_target="tpu_custom_call" | custom-call | flops 1 | bytes 1 | tf_op jit(solution)/shard_map/product/pallas_call | solution.py:195
  407.6 22.4 %attend_back.2 = (bf16[640,3072]{1,0:T(8,128)(2,1)}, f32[16,2,1152]{2,1,0:T(2,128)}) custom-call(bf16[640,3072]{1,0:T(8,128)(2,1)} %get-tuple-element.491.q_ref.k_ref.v_ref, bf16[640,3072]{1,0:T(8,128)(2,1)} %get-tuple-element.491.q_ref.k_ref.v_ref, bf16[640,3072]{1,0:T(8,128)(2,1)} %get-tuple-element.491.q_ref.k_ref.v_ref, ...), custom_call_target="tpu_custom_call" | custom-call | flops 1 | bytes 1 | tf_op jit(solution)/shard_map/attend_back/pallas_call | solution.py:605
  434.5 12.7 %weight_grad.8 = (bf16[2,2,2,4,128,512]{5,4,3,2,1,0:T(8,128)(2,1)}, bf16[2,2,2,4,128,512]{5,4,3,2,1,0:T(8,128)(2,1)}, bf16[4,2,512,128]{3,2,1,0:T(8,128)(2,1)}) custom-call(s32[4]{0:T(128)} %pad_add_fusion.row_of, s32[2]{0:T(128)} %pad_add_fusion.1.y_of, bf16[640,1024]{1,0:T(8,128)(2,1)} %get-tuple-element.483.x_ref.refs_0_, ...), custom_call_target="tpu_custom_call" | custom-call | flops 1 | bytes 1 | tf_op jit(solution)/shard_map/weight_grad/pallas_call | solution.py:326
  466.4 15.7 %weight_grad.9 = (bf16[2,2,2,4,512,128]{5,4,3,2,1,0:T(8,128)(2,1)}, bf16[2,2,2,4,512,128]{5,4,3,2,1,0:T(8,128)(2,1)}, bf16[2,4,128,512]{3,2,1,0:T(8,128)(2,1)}, ...) custom-call(s32[4]{0:T(128)} %pad_add_fusion.row_of, ...), custom_call_target="tpu_custom_call" | custom-call | flops 1 | bytes 1 | tf_op jit(solution)/shard_map/weight_grad/pallas_call | solution.py:326
  484.3 11.5 %product.16.refs_1_.left = bf16[640,4096]{1,0:T(8,128)(2,1)} custom-call(bf16[640,1024]{1,0:T(8,128)(2,1)} %get-tuple-element.625.refs_1_.left, bf16[4096,1024]{1,0:T(8,128)(2,1)} %get-tuple-element.626.right, bf16[640,4096]{1,0:T(8,128)(2,1)} %get-tuple-element.627.factor), custom_call_target="tpu_custom_call" | custom-call | flops 1 | bytes 1 | tf_op jit(solution)/shard_map/product/pallas_call | solution.py:195
  495.8 14.2 %weight_grad.10 = (bf16[2,2,2,4,128,512]{5,4,3,2,1,0:T(8,128)(2,1)}, bf16[2,2,2,4,128,512]{5,4,3,2,1,0:T(8,128)(2,1)}, bf16[2,4,512,128]{3,2,1,0:T(8,128)(2,1)},...) custom-call(s32[4]{0:T(128)} %pad_add_fusion.row_of, ...), custom_call_target="tpu_custom_call" | custom-call | flops 1 | bytes 1 | tf_op jit(solution)/shard_map/weight_grad/pallas_call | solution.py:326
  512.4 10.5 %product.17.grad_in = f32[640,1024]{1,0:T(8,128)} custom-call(bf16[640,4096]{1,0:T(8,128)(2,1)} %product.16.refs_1_.left, bf16[1024,4096]{1,0:T(8,128)(2,1)} %get-tuple-element.659.right), custom_call_target="tpu_custom_call" | custom-call | flops 1 | bytes 1 | tf_op jit(solution)/shard_map/product/pallas_call | solution.py:195
  535.9 17.4 %collective-permute-done.63 = bf16[3,128,1024]{2,1,0:T(8,128)(2,1)S(1)} collective-permute-done((bf16[3,128,1024]{2,1,0:T(8,128)(2,1)S(1)}, bf16[3,128,1024]{2,1,0:T(8,128)(2,1)S(1)}, u32[]{:S(2)}, u32[]{:S(2)}) %collective-permute-start.63) | collective-permute-done | bytes 786464 | tf_op jit(solution)/shard_map/ppermute | solution.py:761
  573.9 23.9 %attend_back.3 = (bf16[768,3072]{1,0:T(8,128)(2,1)}, f32[16,2,512]{2,1,0:T(2,128)}) custom-call(bf16[768,3072]{1,0:T(8,128)(2,1)} %get-tuple-element.444.q_ref.k_ref.v_ref, bf16[768,3072]{1,0:T(8,128)(2,1)} %get-tuple-element.444.q_ref.k_ref.v_ref, bf16[768,3072]{1,0:T(8,128)(2,1)} %get-tuple-element.444.q_ref.k_ref.v_ref, bf16[768,1024]{1,0:T(8,128)(2,1)} %product.18.g_ref, ...), custom_call_target="tpu_custom_call" | custom-call | flops 1 | bytes 1 | tf_op jit(solution)/shard_map/attend_back/pallas_call | solution.py:605
  605.7 12.3 %weight_grad.11 = (bf16[2,2,2,4,128,512]{5,4,3,2,1,0:T(8,128)(2,1)}, bf16[2,2,2,4,128,512]{5,4,3,2,1,0:T(8,128)(2,1)}) custom-call(s32[4]{0:T(128)} %pad_add_fusion.row_of, s32[2]{0:T(128)} %pad_add_fusion.1.y_of, bf16[768,1024]{1,0:T(8,128)(2,1)} %add_convert_fusion.x_ref.refs_0_, bf16[768,1024]{1,0:T(8,128)(2,1)} %get-tuple-element.450.left.refs_1_, ...), custom_call_target="tpu_custom_call" | custom-call | flops 1 | bytes 1 | tf_op jit(solution)/shard_map/weight_grad/pallas_call | solution.py:326
  654.4 10.1 %product.19.grad_in = f32[768,1024]{1,0:T(8,128)} custom-call(bf16[768,3072]{1,0:T(8,128)(2,1)} %get-tuple-element.764.refs_2_.left, bf16[1024,3072]{1,0:T(8,128)(2,1)} %get-tuple-element.765.right), custom_call_target="tpu_custom_call" | custom-call | flops 1 | bytes 1 | tf_op jit(solution)/shard_map/product/pallas_call | solution.py:195
  700.7 11.5 %collective-permute-done.81 = f32[416,128]{1,0:T(8,128)S(1)} collective-permute-done((f32[416,128]{1,0:T(8,128)S(1)}, f32[416,128]{1,0:T(8,128)S(1)}, u32[]{:S(2)}, u32[]{:S(2)}) %collective-permute-start.81) | collective-permute-done | bytes 213024 | tf_op jit(solution)/shard_map/ppermute | solution.py:35
  (538 shorter events, 393.8 us)
Async XLA Ops:
  7.2 46.8 %all-gather.17.cloned.1.call-start = ((), (), s32[]{:S(2)}) async-start(), calls=%async_computation.11 | async-start | bytes 1310720 | tf_op jit(solution)/shard_map/all_gather | solution.py:48
  10.1 83.5 %all-gather.15.cloned.1.call-start = ((), (), s32[]{:S(2)}) async-start(), calls=%async_computation.10 | async-start | bytes 1310720 | tf_op jit(solution)/shard_map/all_gather | solution.py:48
  15.2 135.1 %all-gather.13.cloned.1.call-start = ((), (), s32[]{:S(2)}) async-start(), calls=%async_computation.9 | async-start | bytes 2621440 | tf_op jit(solution)/shard_map/all_gather | solution.py:48
  42.4 159.5 %all-gather.11.cloned.1.call-start = ((), (), s32[]{:S(2)}) async-start(), calls=%async_computation.8 | async-start | bytes 2621440 | tf_op jit(solution)/shard_map/all_gather | solution.py:48
  50.5 181.7 %all-gather.9.cloned.1.call-start = ((), (), s32[]{:S(2)}) async-start(), calls=%async_computation.7 | async-start | bytes 2621440 | tf_op jit(solution)/shard_map/all_gather | solution.py:48
  77.0 189.0 %all-gather.7.cloned.1.call-start = ((), (), s32[]{:S(2)}) async-start(), calls=%async_computation.6 | async-start | bytes 2621440 | tf_op jit(solution)/shard_map/all_gather | solution.py:48
  149.7 451.8 %reduce-scatter.7.cloned.1.call-start = ((), (), s32[]{:S(2)}) async-start(), calls=%async_computation.12 | async-start | bytes 1310720 | tf_op jit(solution)/shard_map/reduce_scatter | solution.py:377
  153.4 47.9 %collective-permute-start.18 = (bf16[2,4,512,128]{3,2,1,0:T(8,128)(2,1)}, bf16[2,4,512,128]{3,2,1,0:T(8,128)(2,1)}, u32[]{:S(2)}, u32[]{:S(2)}) collective-permute-start(bf16[2,4,512,128]{3,2,1,0:T(8,128)(2,1)} %get-tuple-element.828.refs_4_), channel_id=1, source_target_pairs={{0,1},{1,0},{2,3},{3,2},{4,5},{5,4},{6,7},{7,6},{8,9},{9,8},{10,11... | collective-permute-start | bytes 3145736 | tf_op jit(solution)/shard_map/ppermute | solution.py:35
  154.7 46.7 %collective-permute-start.17 = (bf16[2,4,512,128]{3,2,1,0:T(8,128)(2,1)}, bf16[2,4,512,128]{3,2,1,0:T(8,128)(2,1)}, u32[]{:S(2)}, u32[]{:S(2)}) collective-permute-start(bf16[2,4,512,128]{3,2,1,0:T(8,128)(2,1)} %get-tuple-element.829.refs_0_), channel_id=1, source_target_pairs={{0,16},{8,24},{16,0},{24,8},{1,17},{9,25},{17,1},{25,9},{2,18},{10... | collective-permute-start | bytes 3145736 | tf_op jit(solution)/shard_map/ppermute | solution.py:35
  247.5 34.7 %collective-permute-start.40 = (bf16[2,4,128,512]{3,2,1,0:T(8,128)(2,1)S(1)}, bf16[2,4,128,512]{3,2,1,0:T(8,128)(2,1)}, u32[]{:S(2)}, u32[]{:S(2)}) collective-permute-start(bf16[2,4,128,512]{3,2,1,0:T(8,128)(2,1)S(1)} %get-tuple-element.507.refs_4_), channel_id=1, source_target_pairs={{0,8},{8,0},{16,24},{24,16},{1,9},{9,1},{17,25},{25,17},{2,10},{10... | collective-permute-start | bytes 3145736 | tf_op jit(solution)/shard_map/ppermute | solution.py:35
  310.1 37.9 %collective-permute-start.46 = (bf16[2,2,2,4,512,128]{5,4,3,2,1,0:T(8,128)(2,1)}, bf16[2,2,2,4,512,128]{5,4,3,2,1,0:T(8,128)(2,1)S(1)}, u32[]{:S(2)}, u32[]{:S(2)}) collective-permute-start(bf16[2,2,2,4,512,128]{5,4,3,2,1,0:T(8,128)(2,1)} %get-tuple-element.524), channel_id=1, source_target_pairs={{0,8},{8,0},{16,24},{24,16},{1,9},{9,1},{17,25},{25,17},{2,10},{10... | collective-permute-start | bytes 12582920 | tf_op jit(solution)/shard_map/ppermute | solution.py:35
  396.9 50.2 %collective-permute-start.52 = (bf16[2,4,128,512]{3,2,1,0:T(8,128)(2,1)}, bf16[2,4,128,512]{3,2,1,0:T(8,128)(2,1)S(1)}, u32[]{:S(2)}, u32[]{:S(2)}) collective-permute-start(bf16[2,4,128,512]{3,2,1,0:T(8,128)(2,1)} %get-tuple-element.583), channel_id=1, source_target_pairs={{0,16},{8,24},{16,0},{24,8},{1,17},{9,25},{17,1},{25,9},{2,18},{10... | collective-permute-start | bytes 3145736 | tf_op jit(solution)/shard_map/ppermute | solution.py:35
  398.3 48.9 %collective-permute-start.53 = (bf16[2,4,128,512]{3,2,1,0:T(8,128)(2,1)}, bf16[2,4,128,512]{3,2,1,0:T(8,128)(2,1)S(1)}, u32[]{:S(2)}, u32[]{:S(2)}) collective-permute-start(bf16[2,4,128,512]{3,2,1,0:T(8,128)(2,1)} %get-tuple-element.585), channel_id=1, source_target_pairs={{0,1},{1,0},{2,3},{3,2},{4,5},{5,4},{6,7},{7,6},{8,9},{9,8},{10,11... | collective-permute-start | bytes 3145736 | tf_op jit(solution)/shard_map/ppermute | solution.py:35
  399.1 34.4 %collective-permute-start.50 = (bf16[4,512,128]{2,1,0:T(8,128)(2,1)S(1)}, bf16[4,512,128]{2,1,0:T(8,128)(2,1)S(1)}, u32[]{:S(2)}, u32[]{:S(2)}) collective-permute-start(bf16[4,512,128]{2,1,0:T(8,128)(2,1)S(1)} %get-tuple-element.565), channel_id=1, source_target_pairs={{0,1},{1,0},{2,3},{3,2},{4,5},{5,4},{6,7},{7,6},{8,9},{9,8},{10,11... | collective-permute-start | bytes 1572872 | tf_op jit(solution)/shard_map/ppermute | solution.py:35
  553.3 163.1 %reduce-scatter.17.cloned.1.call-start = ((), (), s32[]{:S(2)}) async-start(), calls=%async_computation.17 | async-start | bytes 1310720 | tf_op jit(solution)/shard_map/reduce_scatter | solution.py:377
  554.1 164.2 %reduce-scatter.15.cloned.1.call-start = ((), (), s32[]{:S(2)}) async-start(), calls=%async_computation.16 | async-start | bytes 1310720 | tf_op jit(solution)/shard_map/reduce_scatter | solution.py:377
  554.1 43.7 %collective-permute-start.64 = (bf16[2,4,512,128]{3,2,1,0:T(8,128)(2,1)}, bf16[2,4,512,128]{3,2,1,0:T(8,128)(2,1)S(1)}, u32[]{:S(2)}, u32[]{:S(2)}) collective-permute-start(bf16[2,4,512,128]{3,2,1,0:T(8,128)(2,1)} %get-tuple-element.693), channel_id=1, source_target_pairs={{0,16},{8,24},{16,0},{24,8},{1,17},{9,25},{17,1},{25,9},{2,18},{10... | collective-permute-start | bytes 3145736 | tf_op jit(solution)/shard_map/ppermute | solution.py:35
  555.1 42.7 %collective-permute-start.65 = (bf16[2,4,512,128]{3,2,1,0:T(8,128)(2,1)}, bf16[2,4,512,128]{3,2,1,0:T(8,128)(2,1)S(1)}, u32[]{:S(2)}, u32[]{:S(2)}) collective-permute-start(bf16[2,4,512,128]{3,2,1,0:T(8,128)(2,1)} %get-tuple-element.695), channel_id=1, source_target_pairs={{0,1},{1,0},{2,3},{3,2},{4,5},{5,4},{6,7},{7,6},{8,9},{9,8},{10,11... | collective-permute-start | bytes 3145736 | tf_op jit(solution)/shard_map/ppermute | solution.py:35
  567.3 50.7 %collective-permute-start.66 = (bf16[2,4,128,512]{3,2,1,0:T(8,128)(2,1)}, bf16[2,4,128,512]{3,2,1,0:T(8,128)(2,1)S(1)}, u32[]{:S(2)}, u32[]{:S(2)}) collective-permute-start(bf16[2,4,128,512]{3,2,1,0:T(8,128)(2,1)} %get-tuple-element.718), channel_id=1, source_target_pairs={{0,16},{8,24},{16,0},{24,8},{1,17},{9,25},{17,1},{25,9},{2,18},{10... | collective-permute-start | bytes 3145736 | tf_op jit(solution)/shard_map/ppermute | solution.py:35
  567.7 50.3 %collective-permute-start.67 = (bf16[2,4,128,512]{3,2,1,0:T(8,128)(2,1)}, bf16[2,4,128,512]{3,2,1,0:T(8,128)(2,1)}, u32[]{:S(2)}, u32[]{:S(2)}) collective-permute-start(bf16[2,4,128,512]{3,2,1,0:T(8,128)(2,1)} %get-tuple-element.720), channel_id=1, source_target_pairs={{0,1},{1,0},{2,3},{3,2},{4,5},{5,4},{6,7},{7,6},{8,9},{9,8},{10,11... | collective-permute-start | bytes 3145736 | tf_op jit(solution)/shard_map/ppermute | solution.py:35
  624.3 99.6 %reduce-scatter.13.cloned.1.call-start = ((), (), s32[]{:S(2)}) async-start(), calls=%async_computation.15 | async-start | bytes 1310720 | tf_op jit(solution)/shard_map/reduce_scatter | solution.py:377
  624.9 105.9 %reduce-scatter.11.cloned.1.call-start = ((), (), s32[]{:S(2)}) async-start(), calls=%async_computation.14 | async-start | bytes 1310720 | tf_op jit(solution)/shard_map/reduce_scatter | solution.py:377
  646.1 93.5 %reduce-scatter.9.cloned.1.call-start = ((), (), s32[]{:S(2)}) async-start(), calls=%async_computation.13 | async-start | bytes 1310720 | tf_op jit(solution)/shard_map/reduce_scatter | solution.py:377
  690.7 41.9 %collective-permute-start.80 = (bf16[3,128,1024]{2,1,0:T(8,128)(2,1)}, bf16[3,128,1024]{2,1,0:T(8,128)(2,1)S(1)}, u32[]{:S(2)}, u32[]{:S(2)}) collective-permute-start(bf16[3,128,1024]{2,1,0:T(8,128)(2,1)} %select_convert_fusion), channel_id=1, source_target_pairs={{0,1},{1,0},{2,3},{3,2},{4,5},{5,4},{6,7},{7,6},{8,9},{9,8},{10,11... | collective-permute-start | bytes 2359304 | tf_op jit(solution)/shard_map/ppermute | solution.py:761
  (163 other events, 1820.6 us)
Sparse Core Ops, SparseCore 0:
  10.2 30.6 all-gather.16
  43.0 27.4 all-gather.14
  72.6 45.2 all-gather.12
  119.9 44.8 all-gather.10
  166.2 44.6 all-gather.8
  212.9 44.6 all-gather.6
  553.4 27.4 reduce-scatter.6
  583.3 25.8 reduce-scatter.16
  624.4 27.1 reduce-scatter.14
  653.8 26.6 reduce-scatter.12
  683.4 27.7 reduce-scatter.10
  713.4 26.0 reduce-scatter.8
